TPU v7x, 512 devices: a whole 4x8x8 slice. The times are simulated.
512 devices in a mesh: dom: 64 (over z, x, core), feat: 8 (over y).
Axes of the slice: x: 4, y: 8, z: 8, core: 2. Of those that a mesh axis runs over, the one named last changes fastest.
Arguments:
- node_in: bfloat16 [40960, 512], P('dom'), may hold values from -6 to 6
- local_edges: bfloat16 [65536, 512], P(('dom', 'feat')), may hold values from -6 to 6
- cut_edges: bfloat16 [524288, 512], P(('dom', 'feat')), may hold values from -6 to 6
- node_cot: bfloat16 [40960, 512], P(('dom', 'feat')), may hold values from -6 to 6
- edge_w1: bfloat16 [1536, 512], P('feat'), may hold values from -0.15625 to 0.15625
- edge_w2: bfloat16 [512, 512], P('feat'), may hold values from -0.25 to 0.25
- node_w1: bfloat16 [1024, 512], P('feat'), may hold values from -0.1875 to 0.1875
- node_w2: bfloat16 [512, 512], P('feat'), may hold values from -0.25 to 0.25
- edge_b1: float32 [512], replicated, may hold values from -3 to 3
- edge_b2: float32 [512], replicated, may hold values from -3 to 3
- edge_gain: float32 [512], replicated, may hold values from 0.5 to 1.5
- edge_shift: float32 [512], replicated, may hold values from -3 to 3
- node_b1: float32 [512], replicated, may hold values from -3 to 3
- node_b2: float32 [512], replicated, may hold values from -3 to 3
- node_gain: float32 [512], replicated, may hold values from 0.5 to 1.5
- node_shift: float32 [512], replicated, may hold values from -3 to 3
- local_send: int32 [65536], P(('dom', 'feat')), may hold values from 0 to 639
- local_recv: int32 [65536], P(('dom', 'feat')), may hold values from 0 to 79
- cut_send: int32 [64, 8, 1024], P('dom', 'feat'), may hold values from 0 to 15
- cut_recv: int32 [64, 8, 1024], P('dom', 'feat'), may hold values from 0 to 79
- cut_count: int32 [64, 8, 64], P('dom', 'feat'), may hold values from 0 to 16, as said below
Outputs:
- node_out: bfloat16 [40960, 512], P(('dom', 'feat'))
- node_grad: float32 [40960, 512], P(('dom', 'feat'))
- local_grad: bfloat16 [65536, 512], P(('dom', 'feat'))
- cut_grad: bfloat16 [524288, 512], P(('dom', 'feat'))
Inputs may be any that keep to these rules, and one draw needn't show every extreme that they name: `cut_count`: every device has one source partition whose 16 slots are all live, and at least one device has all its slots live.
All inputs are finite; a program needn't handle non-finite values.
Results may differ from a plain program's by a relative error of at most 0.02.
Values may be sent and summed in bfloat16 or wider, within the bound.
No kernel may reach another device: no remote copies, remote signals or barrier semaphores. Data moves between devices by JAX's collectives and lax.ppermute only.
A program may use at most 64 MiB of HBM per device.

v0:
```python
import jax
import jax.numpy as jnp
from jax import lax
from jax.sharding import PartitionSpec as P

BORDER = 16


NORM_EPS = 1e-05


def normalize(values):
    centered = values - jnp.mean(values, axis=-1, keepdims=True)
    inv_std = lax.rsqrt(jnp.mean(centered * centered, axis=-1, keepdims=True) + NORM_EPS)
    return (centered * inv_std, inv_std)


def norm_back(grad_out, normed, inv_std, norm_gain):
    scaled = grad_out * norm_gain
    first_mean = jnp.mean(scaled, axis=-1, keepdims=True)
    second_mean = jnp.mean(scaled * normed, axis=-1, keepdims=True)
    return inv_std * (scaled - first_mean - normed * second_mean)


def silu_slope(pre_act):
    sigmoid_val = jax.nn.sigmoid(pre_act)
    return sigmoid_val * (1.0 + pre_act * (1.0 - sigmoid_val))


def times_transpose(operand, weight):
    return lax.dot_general(
        operand, weight, (((1,), (1,)), ((), ())), preferred_element_type=jnp.float32
    )


def select_sum(form, selector, values):
    upper_part = values.astype(jnp.bfloat16)
    lower_part = (values - upper_part.astype(jnp.float32)).astype(jnp.bfloat16)
    first = jnp.einsum(form, selector, upper_part, preferred_element_type=jnp.float32)
    return first + jnp.einsum(form, selector, lower_part, preferred_element_type=jnp.float32)


def edge_forward(edge_rows, senders, receivers, live_mask, params):
    w_first, w_second, b_first, b_second, norm_gain, norm_shift = params
    joined = jnp.concatenate([edge_rows, senders, receivers], axis=1)
    pre_act = jnp.dot(joined, w_first, preferred_element_type=jnp.float32) + b_first
    activation = jax.nn.silu(pre_act).astype(jnp.bfloat16)
    pre_norm = jnp.dot(activation, w_second, preferred_element_type=jnp.float32) + b_second
    normed, inv_std = normalize(pre_norm)
    message = live_mask[:, None] * (edge_rows.astype(jnp.float32) + normed * norm_gain + norm_shift)
    return (message, (pre_act, normed, inv_std))


def edge_backward(grad_message, stored, params):
    w_first, w_second, b_first, b_second, norm_gain, norm_shift = params
    pre_act, normed, inv_std = stored
    grad_norm = norm_back(grad_message, normed, inv_std, norm_gain).astype(jnp.bfloat16)
    grad_pre = (times_transpose(grad_norm, w_second) * silu_slope(pre_act)).astype(jnp.bfloat16)
    grad_in = times_transpose(grad_pre, w_first)
    feat_width = grad_message.shape[1]
    return (
        grad_message + grad_in[:, :feat_width],
        grad_in[:, feat_width : 2 * feat_width],
        grad_in[:, 2 * feat_width :],
    )


def shards(
    node_in,
    local_edges,
    cut_edges,
    node_cot,
    edge_w1,
    edge_w2,
    node_w1,
    node_w2,
    edge_b1,
    edge_b2,
    edge_gain,
    edge_shift,
    node_b1,
    node_b2,
    node_gain,
    node_shift,
    local_send,
    local_recv,
    cut_send,
    cut_recv,
    cut_count,
):
    feat_width = node_in.shape[1]
    part_rows = node_in.shape[0]
    own_count = node_cot.shape[0]
    local_count = local_edges.shape[0]
    domains = lax.axis_size("dom")
    border_rows = BORDER
    slot_rows = cut_recv.shape[2] // domains
    offset = lax.axis_index("feat") * own_count
    own_nodes = lax.dynamic_slice_in_dim(node_in, offset, own_count, 0)
    edge_first, edge_second, node_first, node_second = (
        lax.all_gather(edge_w1, "feat", axis=0, tiled=True),
        lax.all_gather(edge_w2, "feat", axis=0, tiled=True),
        lax.all_gather(node_w1, "feat", axis=0, tiled=True),
        lax.all_gather(node_w2, "feat", axis=0, tiled=True),
    )
    edge_params = (edge_first, edge_second, edge_b1, edge_b2, edge_gain, edge_shift)
    send_list = cut_send[0, 0]
    recv_list = cut_recv[0, 0]
    border = node_in[:border_rows]
    positions = jnp.arange(border_rows, dtype=jnp.int32)
    picker = (send_list.reshape(domains, slot_rows)[:, :, None] == positions).astype(jnp.bfloat16)
    picked = jnp.einsum("sjb,bd->sjd", picker, border, preferred_element_type=jnp.float32)
    cut_senders = lax.all_to_all(
        picked.astype(jnp.bfloat16).reshape(domains * slot_rows, feat_width),
        "dom",
        split_axis=0,
        concat_axis=0,
        tiled=True,
    )
    slot_pos = jnp.arange(slot_rows, dtype=jnp.int32)
    cut_live = (slot_pos[None, :] < cut_count[0, 0][:, None]).astype(jnp.float32).reshape(-1)
    local_live = jnp.ones((local_count,), jnp.float32)
    local_senders = jnp.take(node_in, local_send, axis=0)
    local_receivers = jnp.take(own_nodes, local_recv, axis=0)
    cut_receivers = jnp.take(own_nodes, recv_list, axis=0)
    own_pos = jnp.arange(own_count, dtype=jnp.int32)[:, None]
    local_spread = (local_recv[None, :] == own_pos).astype(jnp.bfloat16)
    cut_spread = (recv_list[None, :] == own_pos).astype(jnp.bfloat16)
    all_live = jnp.concatenate([local_live, cut_live])
    all_recv = jnp.concatenate([local_recv, recv_list])
    message, stored = edge_forward(
        jnp.concatenate([local_edges, cut_edges], axis=0),
        jnp.concatenate([local_senders, cut_senders], axis=0),
        jnp.concatenate([local_receivers, cut_receivers], axis=0),
        all_live,
        edge_params,
    )
    spread = jnp.concatenate([local_spread, cut_spread], axis=1)
    summed = select_sum("ne,ed->nd", spread, message)
    aggregate = summed.astype(jnp.bfloat16)
    node_joined = jnp.concatenate([own_nodes, aggregate], axis=1)
    node_pre = jnp.dot(node_joined, node_first, preferred_element_type=jnp.float32) + node_b1
    node_act = jax.nn.silu(node_pre).astype(jnp.bfloat16)
    node_norm_in = jnp.dot(node_act, node_second, preferred_element_type=jnp.float32) + node_b2
    node_normed, node_inv = normalize(node_norm_in)
    node_out = (own_nodes.astype(jnp.float32) + node_normed * node_gain + node_shift).astype(
        jnp.bfloat16
    )
    cotangent = node_cot.astype(jnp.float32)
    grad_node_norm = norm_back(cotangent, node_normed, node_inv, node_gain).astype(jnp.bfloat16)
    grad_node_pre = (times_transpose(grad_node_norm, node_second) * silu_slope(node_pre)).astype(
        jnp.bfloat16
    )
    grad_node_in = times_transpose(grad_node_pre, node_first)
    grad_agg = grad_node_in[:, feat_width:]
    own_grad = cotangent + grad_node_in[:, :feat_width]
    grad_message = all_live[:, None] * jnp.take(grad_agg, all_recv, axis=0)
    grad_edge, grad_send, grad_recv = edge_backward(grad_message, stored, edge_params)
    own_grad = own_grad + select_sum("ne,ed->nd", spread, grad_recv)
    local_grad = grad_edge[:local_count]
    cut_grad = grad_edge[local_count:]
    local_send_grad = grad_send[:local_count]
    cut_send_grad = grad_send[local_count:]
    send_spread = (local_send[None, :] == jnp.arange(part_rows, dtype=jnp.int32)[:, None]).astype(
        jnp.bfloat16
    )
    partial_value = select_sum("ne,ed->nd", send_spread, local_send_grad)
    own_rows = lax.dynamic_slice_in_dim(partial_value, offset, own_count, 0) + own_grad
    partial_value = lax.dynamic_update_slice_in_dim(partial_value, own_rows, offset, 0)
    returned = (
        lax.all_to_all(
            cut_send_grad.astype(jnp.bfloat16), "dom", split_axis=0, concat_axis=0, tiled=True
        )
        .astype(cut_send_grad.dtype)
        .reshape(domains, slot_rows, feat_width)
    )
    border_grad = select_sum("sjb,sjd->bd", picker, returned)
    partial_value = jnp.concatenate(
        [partial_value[:border_rows] + border_grad, partial_value[border_rows:]], axis=0
    )
    node_grad = lax.psum_scatter(
        partial_value.astype(jnp.bfloat16), "feat", scatter_dimension=0, tiled=True
    ).astype(jnp.float32)
    return (node_out, node_grad, local_grad.astype(jnp.bfloat16), cut_grad.astype(jnp.bfloat16))


def solution(mesh):
    placed = (
        P("dom", None),
        P(("dom", "feat"), None),
        P(("dom", "feat"), None),
        P(("dom", "feat"), None),
        P("feat", None),
        P("feat", None),
        P("feat", None),
        P("feat", None),
        P(),
        P(),
        P(),
        P(),
        P(),
        P(),
        P(),
        P(),
        P(("dom", "feat")),
        P(("dom", "feat")),
        P("dom", "feat", None),
        P("dom", "feat", None),
        P("dom", "feat", None),
    )
    return jax.shard_map(
        shards,
        mesh=mesh,
        in_specs=placed,
        out_specs=(
            P(("dom", "feat"), None),
            P(("dom", "feat"), None),
            P(("dom", "feat"), None),
            P(("dom", "feat"), None),
        ),
        check_vma=False,
    )
```

profile of v0, /device:TPU:6, one launch (start us, length us, event | category | flops | bytes accessed | tf_op | source)
XLA Modules:
  0.0 226.7 jit_solution(10734635277108146672)
XLA Ops:
  7.3 0.7 all-gather.3.cloned.1.call-update
  8.0 0.5 broadcast.169
  8.5 1.3 reduce.5
  10.0 0.3 copy.56
  10.3 2.1 convolution_convert_fusion
  12.5 13.9 %all-to-all-start = ((bf16[64,16,512]{2,1,0:T(8,128)(2,1)}), bf16[64,16,512]{2,1,0:T(8,128)(2,1)S(1)}, u32[]{:S(2)}, u32[]{:S(2)}) async-start(bf16[64,16,512]{2,1,0:T(8,128)(2,1)} %convolution_convert_fusion), calls=%async_computation | async-start | bytes 2097152 | tf_op jit(solution)/shard_map/all_to_all | solution.py:113
  26.5 0.7 all-gather.5.cloned.1.call-update
  27.4 0.1 convert_element_type.89
  27.5 0.8 gather_fusion.1
  28.4 0.1 copy.58
  28.5 0.9 gather_fusion
  29.4 0.8 copy.54
  30.1 0.1 copy.52
  30.3 4.0 %gather_fusion.2 = bf16[1024,512]{1,0:T(8,128)(2,1)S(1)} fusion(bf16[80,512]{1,0:T(8,128)(2,1)S(1)} %constant_dynamic-slice_fusion, s32[1024]{0:T(1024)S(1)} %broadcast_clamp_fusion), kind=kCustom, calls=%fused_computation.2 | custom fusion | bytes 2101248 | tf_op jit(solution)/shard_map/jit(_take)/gather | solution.py:125
  34.2 1.3 copy.59
  35.5 1.6 copy.53
  37.2 0.7 iota_compare_fusion.3
  37.9 29.6 %all_gather.13 = bf16[512,512]{1,0:T(8,128)(2,1)} all-gather(bf16[64,512]{1,0:T(8,128)(2,1)} %param.26), channel_id=1, replica_groups=mesh['dom'=64,'feat'=8] {'feat'}, dimensions={0}, use_global_device_ids=true | all-gather | bytes 589824 | tf_op jit(solution)/shard_map/all_gather | solution.py:102
  67.5 28.7 %all_gather.15 = bf16[512,512]{1,0:T(8,128)(2,1)} all-gather(bf16[64,512]{1,0:T(8,128)(2,1)} %param.28), channel_id=1, replica_groups=mesh['dom'=64,'feat'=8] {'feat'}, dimensions={0}, use_global_device_ids=true | all-gather | bytes 589824 | tf_op jit(solution)/shard_map/all_gather | solution.py:104
  96.2 0.7 broadcast_select_fusion.1
  96.8 1.6 broadcast_select_fusion.2
  98.4 1.1 broadcast_select_fusion
  99.5 0.5 copy.57
  100.1 3.9 %fusion.12 = f32[1152,512]{1,0:T(8,128)S(1)} fusion(bf16[1536,512]{1,0:T(8,128)(2,1)} %all-gather.3.cloned.1.call-done, bf16[1024,512]{0,1:T(8,128)(2,1)} %broadcast_select_fusion, bf16[128,512]{0,1:T(8,128)(2,1)S(1)} %copy-done.15, bf16[1024,512]{0,1:T(8,128)(2,1)S(1)} %copy.57, bf16[128,512]{0,1:T(8,128)(2,1)} %broadcast_select_fusion.2, ...), kind=kOutput, calls=%fused_computation.18 | convolution fusion | flops 1833762816 | bytes 7473152 | tf_op jit(solution)/shard_map/dot_general | solution.py:46
  104.0 1.4 copy-done.24
  105.4 1.0 fusion.100
  106.4 0.3 multiply_reduce_fusion.1
  106.7 0.6 copy-done.8
  107.3 0.6 add_multiply_fusion
  107.9 0.3 copy-done.3
  108.2 0.5 fusion.53
  108.7 1.1 fusion.45
  109.8 1.6 convolution_add_fusion.3
  111.4 1.4 fusion.101
  112.9 0.2 multiply_reduce_fusion.2
  113.1 0.5 copy-done.6
  113.6 1.8 fusion.59
  115.4 2.6 %fusion.46 = f32[80,1024]{1,0:T(8,128)} fusion(bf16[1024,512]{1,0:T(8,128)(2,1)S(1)} %copy-done.5, bf16[512,512]{1,0:T(8,128)(2,1)} %all_gather.15, f32[80,512]{1,0:T(8,128)} %copy-done.13, bf16[80,512]{1,0:T(8,128)(2,1)} %param.24, f32[80,512]{1,0:T(8,128)} %copy-done.6, f32[80]{0:T(128)S(1)} %broadcast_multiply_fusion.3, ...), kind=kOutput, calls=%fused_computation.62 | convolution fusion | flops 126566400 | bytes 2313472 | tf_op jit(solution)/shard_map/dot_general | solution.py:31
  118.0 0.9 slice.59
  119.0 4.3 %gather_fusion.3 = f32[1152,512]{1,0:T(8,128)} fusion(f32[80,512]{1,0:T(8,128)S(1)} %slice.59, s32[2048]{0:T(1024)S(1)} %pad_clamp_fusion), kind=kCustom, calls=%fused_computation.3 | custom fusion | bytes 4723200 | tf_op jit(solution)/shard_map/jit(_take)/gather | solution.py:157
  123.3 3.1 %copy.60 = f32[1152,512]{0,1:T(8,128)} copy(f32[1152,512]{1,0:T(8,128)} %gather_fusion.3) | data formatting | bytes 4718592 | tf_op jit(solution)/shard_map/jit(_take)/gather | solution.py:157
  126.4 2.5 %fusion.18 = (f32[1152]{0:T(1024)S(1)}, f32[1152]{0:T(1024)S(1)}) fusion(f32[1152,512]{0,1:T(8,128)} %copy.60, f32[512]{0:T(512)S(1)} %copy-done.18, f32[1152]{0:T(1024)S(1)} %get-tuple-element.30, pred[1152]{0:T(1024)(128)(4,1)S(1)} %get-tuple-element.29, f32[1152]{0:T(1024)S(1)} %add_rsqrt_fusion, f32[1152,512]{0,1:T(8,128)S(1)} %get-tuple-element.22, ...), kind=kLoop, calls=%fused_computation.36 | loop fusion | flops 4716288 | bytes 4744832 | tf_op jit(solution)/shard_map/reduce_sum | solution.py:20
  128.9 9.1 %fusion.17 = f32[1152,1536]{1,0:T(8,128)} fusion(bf16[1536,512]{1,0:T(8,128)(2,1)} %all-gather.3.cloned.1.call-done, bf16[512,512]{1,0:T(8,128)(2,1)S(1)} %copy-done.10, f32[1152,512]{1,0:T(8,128)} %copy-done.24, f32[1152,512]{0,1:T(8,128)S(1)} %get-tuple-element.22, f32[1152,512]{0,1:T(8,128)} %copy.60, f32[1152]{0:T(1024)S(1)} %broadcast_multiply_fusion, ...), kind=kOutput, calls=%fused_computation.35 | convolution fusion | flops 2427125760 | bytes 16279168 | tf_op jit(solution)/shard_map/dot_general | solution.py:31
  138.0 2.7 %slice.99 = bf16[1024,512]{1,0:T(8,128)(2,1)} slice(f32[1152,1536]{1,0:T(8,128)} %fusion.17), slice={[128:1152], [512:1024]} | slice | bytes 2097152 | tf_op jit(solution)/shard_map/slice | solution.py:163
  140.7 10.2 %all-to-all-start.1 = ((bf16[64,16,512]{2,1,0:T(8,128)(2,1)}), bf16[64,16,512]{2,1,0:T(8,128)(2,1)S(1)}, u32[]{:S(2)}, u32[]{:S(2)}) async-start(bf16[64,16,512]{2,1,0:T(8,128)(2,1)} %bitcast.7), calls=%async_computation.1 | async-start | bytes 2097152 | tf_op jit(solution)/shard_map/all_to_all | solution.py:171
  150.9 0.3 reduce-scatter.2.cloned.1.call-start
  151.2 1.3 fusion.56
  152.5 2.0 fusion.55
  154.5 1.3 convolution_add_fusion.1
  155.8 2.0 fusion.42
  157.8 0.1 slice.100
  157.9 21.8 %all-to-all-done.1 = bf16[64,16,512]{2,1,0:T(8,128)(2,1)S(1)} async-done(((bf16[64,16,512]{2,1,0:T(8,128)(2,1)}), bf16[64,16,512]{2,1,0:T(8,128)(2,1)S(1)}, u32[]{:S(2)}, u32[]{:S(2)}) %all-to-all-start.1) | async-done | bytes 1048608 | tf_op jit(solution)/shard_map/all_to_all | solution.py:171
  179.7 1.2 convolution_bitcast_fusion.1
  181.0 0.2 subtract_convert_fusion.2
  181.2 1.2 fusion.49
  182.4 0.9 pad_maximum_fusion
  183.3 3.3 %slice.66 = f32[1152,512]{1,0:T(8,128)} slice(f32[1152,1536]{1,0:T(8,128)} %fusion.17), slice={[0:1152], [0:512]} | slice | bytes 4718592 | tf_op jit(solution)/shard_map/slice | solution.py:62
  186.6 3.2 %copy.66 = f32[1152,512]{0,1:T(8,128)} copy(f32[1152,512]{1,0:T(8,128)} %slice.66) | data formatting | bytes 4718592
  189.8 1.9 add_convert_fusion
  191.8 0.1 slice.68
  191.9 1.3 copy.65
  193.3 0.8 copy.64
  194.0 24.6 %reduce-scatter.2.cloned.1.call-done = bf16[80,512]{1,0:T(8,128)(2,1)} async-done(((bf16[640,512]{1,0:T(8,128)(2,1)}), bf16[80,512]{1,0:T(8,128)(2,1)}) %reduce-scatter.2.cloned.1.call-update) | async-done | bytes 81936 | tf_op jit(solution)/shard_map/reduce_scatter | solution.py:181
  218.6 1.6 convert_element_type.112
  (77 shorter events, 0.6 us)
Async XLA Ops:
  7.2 20.3 %copy-start.2 = (bf16[640,512]{1,0:T(8,128)(2,1)S(1)}, bf16[640,512]{1,0:T(8,128)(2,1)}, u32[]{:S(2)}) copy-start(bf16[640,512]{1,0:T(8,128)(2,1)} %param.21) | copy-start | bytes 1966084
  7.2 20.0 %copy-start.17 = (s32[128]{0:T(128)S(1)}, s32[128]{0:T(128)}, u32[]{:S(2)}) copy-start(s32[128]{0:T(128)} %param.38) | copy-start | bytes 1540
  7.2 20.0 %copy-start.19 = (s32[128]{0:T(128)S(1)}, s32[128]{0:T(128)}, u32[]{:S(2)}) copy-start(s32[128]{0:T(128)} %param.37) | copy-start | bytes 1540
  7.2 20.0 %copy-start.16 = (s32[1,1,1024]{2,1,0:T(1,128)S(1)}, s32[1,1,1024]{2,1,0:T(1,128)}, u32[]{:S(2)}) copy-start(s32[1,1,1024]{2,1,0:T(1,128)} %param.40) | copy-start | bytes 12292
  7.2 20.1 %copy-start.21 = (s32[1,1,64]{2,1,0:T(1,128)S(1)}, s32[1,1,64]{2,1,0:T(1,128)}, u32[]{:S(2)}) copy-start(s32[1,1,64]{2,1,0:T(1,128)} %param.41) | copy-start | bytes 772
  7.2 92.9 %all-gather.3.cloned.1.call-start = ((), (), s32[]{:S(2)}) async-start(), calls=%async_computation.3 | async-start | bytes 1769472 | tf_op jit(solution)/shard_map/all_gather | solution.py:101
  12.5 17.7 %copy-start.14 = (bf16[128,512]{1,0:T(8,128)(2,1)S(1)}, bf16[128,512]{1,0:T(8,128)(2,1)}, u32[]{:S(2)}) copy-start(bf16[128,512]{1,0:T(8,128)(2,1)} %param.22) | copy-start | bytes 393220
  12.5 87.1 %all-to-all-start = ((bf16[64,16,512]{2,1,0:T(8,128)(2,1)}), bf16[64,16,512]{2,1,0:T(8,128)(2,1)S(1)}, u32[]{:S(2)}, u32[]{:S(2)}) async-start(bf16[64,16,512]{2,1,0:T(8,128)(2,1)} %convolution_convert_fusion), calls=%async_computation | async-start | bytes 2097152 | tf_op jit(solution)/shard_map/all_to_all | solution.py:113
  26.4 83.4 %all-gather.5.cloned.1.call-start = ((), (), s32[]{:S(2)}) async-start(), calls=%async_computation.4 | async-start | bytes 1179648 | tf_op jit(solution)/shard_map/all_gather | solution.py:103
  30.2 69.9 %copy-start.7 = (bf16[128,512]{0,1:T(8,128)(2,1)}, bf16[128,512]{0,1:T(8,128)(2,1)S(1)}, u32[]{:S(2)}) copy-start(bf16[128,512]{0,1:T(8,128)(2,1)S(1)} %copy.52) | copy-start | bytes 393220
  35.5 62.9 %copy-start.1 = (bf16[1024,512]{0,1:T(8,128)(2,1)S(1)}, bf16[1024,512]{0,1:T(8,128)(2,1)}, u32[]{:S(2)}) copy-start(bf16[1024,512]{0,1:T(8,128)(2,1)} %copy.59) | copy-start | bytes 3145732
  96.2 4.0 %copy-start.22 = (f32[512]{0:T(512)S(1)}, f32[512]{0:T(512)}, u32[]{:S(2)}) copy-start(f32[512]{0:T(512)} %param.29) | copy-start | bytes 6148
  96.8 3.3 %copy-start.15 = (bf16[128,512]{0,1:T(8,128)(2,1)S(1)}, bf16[128,512]{0,1:T(8,128)(2,1)}, u32[]{:S(2)}) copy-start(bf16[128,512]{0,1:T(8,128)(2,1)} %broadcast_select_fusion.1) | copy-start | bytes 393220
  100.1 5.3 %copy-start.23 = (f32[512]{0:T(512)S(1)}, f32[512]{0:T(512)}, u32[]{:S(2)}) copy-start(f32[512]{0:T(512)} %param.30) | copy-start | bytes 6148
  100.1 5.3 %copy-start.9 = (bf16[512,512]{1,0:T(8,128)(2,1)S(1)}, bf16[512,512]{1,0:T(8,128)(2,1)}, u32[]{:S(2)}) copy-start(bf16[512,512]{1,0:T(8,128)(2,1)} %all_gather.13) | copy-start | bytes 1572868
  104.0 1.4 copy-start.24
  106.4 0.9 copy-start.8
  106.4 0.9 copy-start.18
  106.4 0.9 copy-start.20
  107.3 0.9 copy-start.3
  109.8 5.6 %copy-start.5 = (bf16[1024,512]{1,0:T(8,128)(2,1)S(1)}, bf16[1024,512]{1,0:T(8,128)(2,1)}, u32[]{:S(2)}) copy-start(bf16[1024,512]{1,0:T(8,128)(2,1)} %all-gather.5.cloned.1.call-done) | copy-start | bytes 3145732
  111.4 4.0 %copy-start.13 = (f32[80,512]{1,0:T(8,128)}, f32[80,512]{1,0:T(8,128)S(1)}, u32[]{:S(2)}) copy-start(f32[80,512]{1,0:T(8,128)S(1)} %convolution_add_fusion.3) | copy-start | bytes 491524
  112.9 0.7 copy-start.6
  126.4 2.5 %copy-start.10 = (bf16[512,512]{1,0:T(8,128)(2,1)S(1)}, bf16[512,512]{1,0:T(8,128)(2,1)}, u32[]{:S(2)}) copy-start(bf16[512,512]{1,0:T(8,128)(2,1)} %all_gather.13) | copy-start | bytes 1572868
  140.7 11.8 %copy-start.4 = (pred[80,1024]{1,0:T(8,128)(4,1)S(1)}, pred[80,1024]{1,0:T(8,128)(4,1)}, u32[]{:S(2)}) copy-start(pred[80,1024]{1,0:T(8,128)(4,1)} %iota_compare_fusion.3) | copy-start | bytes 245764
  140.7 39.1 %all-to-all-start.1 = ((bf16[64,16,512]{2,1,0:T(8,128)(2,1)}), bf16[64,16,512]{2,1,0:T(8,128)(2,1)S(1)}, u32[]{:S(2)}, u32[]{:S(2)}) async-start(bf16[64,16,512]{2,1,0:T(8,128)(2,1)} %bitcast.7), calls=%async_computation.1 | async-start | bytes 2097152 | tf_op jit(solution)/shard_map/all_to_all | solution.py:171
  150.9 67.7 %reduce-scatter.2.cloned.1.call-start = ((), (), s32[]{:S(2)}) async-start(), calls=%async_computation.5 | async-start | bytes 737280 | tf_op jit(solution)/shard_map/reduce_scatter | solution.py:181
  152.5 3.4 %copy-start.11 = (bf16[80,512]{1,0:T(8,128)(2,1)S(1)}, bf16[80,512]{1,0:T(8,128)(2,1)}, u32[]{:S(2)}) copy-start(bf16[80,512]{1,0:T(8,128)(2,1)} %param.24) | copy-start | bytes 245764
  152.5 3.4 %copy-start.12 = (f32[80,1024]{1,0:T(8,128)S(1)}, f32[80,1024]{1,0:T(8,128)}, u32[]{:S(2)}) copy-start(f32[80,1024]{1,0:T(8,128)} %fusion.46) | copy-start | bytes 983044
  186.6 3.2 %copy-start = (f32[1152,512]{0,1:T(8,128)S(1)}, f32[1152,512]{0,1:T(8,128)}, u32[]{:S(2)}) copy-start(f32[1152,512]{0,1:T(8,128)} %copy.60) | copy-start | bytes 7077892
Sparse Core Ops, SparseCore 0:
  10.1 47.7 all-gather.2
  60.0 40.4 all-gather.4
  183.5 35.0 reduce-scatter.1
where the time goes:
time: 228 us; the launch traced here: 227 us
  blocking collectives  58.3 us (26%)
  waiting for transfers between devices  47.8 us (21%)
  local copies, waits for them, and re-layouts  33.8 us (15%)
  matrix products  32.3 us (14%)
  starting transfers between devices  24.5 us (11%)
  other arithmetic  15.6 us (7%)
  between operations  14.4 us (6%)
    all_gather x1, blocking collectives, shards(): lax.all_gather(edge_w2, 'feat', axis=0, tiled=True)  29.6 us
    all_gather x1, blocking collectives, shards(): lax.all_gather(node_w2, 'feat', axis=0, tiled=True)  28.7 us
    reduce_scatter x1, waiting for transfers between devices, shards(): lax.psum_scatter(partial_value.astype(jnp.bfloat16), 'feat', scatter_dime...  24.6 us
    all_to_all x1, waiting for transfers between devices, shards(): lax.all_to_all(cut_send_grad.astype(jnp.bfloat16), 'dom', split_axis=0, c...  21.8 us
    all_to_all x1, starting transfers between devices, shards(): lax.all_to_all(picked.astype(jnp.bfloat16).reshape(domains * slot_rows, f...  13.9 us
    dot_general x2, matrix products, times_transpose(): lax.dot_general(operand, weight, (((1,), (1,)), ((), ())), preferred_elem...  11.7 us
    unnamed x56, local copies, waits for them, and re-layouts  10.3 us
    all_to_all x1, starting transfers between devices, shards(): lax.all_to_all(cut_send_grad.astype(jnp.bfloat16), 'dom', split_axis=0, c...  10.2 us
  transfers between devices with their start and end apart: 5, of which 2 were waited for; matrix products, arithmetic and copies ran while one was open for 19% of the time, Pallas kernels for 0%

commit v1 on v0

v1 whole, which is shorter than its diff:
```python
import jax
import jax.numpy as jnp
from jax import lax
from jax.experimental import pallas as pl
from jax.experimental.pallas import tpu as pltpu
from jax.sharding import Mesh
from jax.sharding import PartitionSpec as P

Z, X, C, F = 8, 4, 2, 8
DOM = ("z", "x", "core")
D = 512
BORDER = 16
SLOTS = 16
OWN = 80
LOC = 128
CUT = 1024
ALL = LOC + CUT
PART = 640
GROUP = 256
GROUPS = CUT // GROUP
PACK = BORDER + 2
EPS = 1e-05
F32 = jnp.float32
BF16 = jnp.bfloat16


def dot(left, right):
    return jnp.dot(left, right, preferred_element_type=F32)


def dot_t(left, right):
    return lax.dot_general(left, right, (((1,), (1,)), ((), ())), preferred_element_type=F32)


def onehot(match):
    return jnp.where(match, 1.0, 0.0).astype(BF16)


def iota(shape, axis):
    return lax.broadcasted_iota(jnp.int32, shape, axis)


def normalize(values):
    centered = values - jnp.mean(values, axis=-1, keepdims=True)
    inv_std = lax.rsqrt(jnp.mean(centered * centered, axis=-1, keepdims=True) + EPS)
    return centered * inv_std, inv_std


def norm_back(scaled, normed, inv_std):
    first_mean = jnp.mean(scaled, axis=-1, keepdims=True)
    second_mean = jnp.mean(scaled * normed, axis=-1, keepdims=True)
    return inv_std * (scaled - first_mean - normed * second_mean)


def silu_and_slope(values):
    sigmoid = 0.5 * jnp.tanh(0.5 * values) + 0.5
    act = values * sigmoid
    return act.astype(BF16), sigmoid + act * (1.0 - sigmoid)


def split(values):
    upper = values.astype(BF16)
    return upper, (values - upper.astype(F32)).astype(BF16)


def prepare_body(
    nodes, border, lsend_col, lsend_row, recv_col, recv_row, sel_col, sel_row,
    senders, expand, spread, pick_t, send_t,
):
    pick = onehot(lsend_col[...] == iota((LOC, PART), 1))
    senders[0:LOC, :] = dot(pick, nodes[...]).astype(BF16)
    send_t[...] = onehot(lsend_row[...] == iota((PART, LOC), 0))
    expand[...] = onehot(recv_col[...] == (iota((ALL, 256), 1) & 127))
    spread[...] = onehot(recv_row[...] == iota((OWN, ALL), 0))
    for k in range(GROUPS):
        rows = slice(k * GROUP, (k + 1) * GROUP)
        table = jnp.concatenate(
            [border[c, x, 2 * k + dz, 0:BORDER, :] for dz in range(2) for x in range(X) for c in range(C)],
            axis=0,
        )
        pick = onehot(sel_col[rows, :] == iota((GROUP, GROUP), 1))
        senders[LOC + k * GROUP : LOC + (k + 1) * GROUP, :] = dot(pick, table).astype(BF16)
        pick_t[k, :, :] = onehot(sel_row[:, rows] == iota((GROUP, GROUP), 0))


def layer_body(
    core, weights, senders, local_edges, cut_edges, expand, spread, pick_t, send_t, own, cot,
    eb1, eb2, eg, es, nb1, nb2, ng, ns,
    node_out, local_grad, cut_grad, own_grad, keep, send, local_send,
    w1, w2, n1, n2, slope, normed, inv, sems,
):
    copies = []
    for f in range(F):
        for i, (ref, start, size) in enumerate(((w1, 0, 192), (w2, 192, 64), (n1, 256, 128), (n2, 384, 64))):
            copy = pltpu.make_async_copy(
                weights.at[f, pl.ds(start, size), :], ref.at[pl.ds(f * size, size), :], sems.at[i, f]
            )
            copy.start()
            copies.append((i, copy))

    def arrive(which):
        for i, copy in copies:
            if i == which:
                copy.wait()

    chunks = [(0, LOC, local_edges, 0)]
    chunks += [(LOC + k * GROUP, GROUP, cut_edges, k * GROUP) for k in range(GROUPS)]
    zeros = jnp.zeros((128 - OWN, D), BF16)

    arrive(0)
    received = dot(own[...], w1[2 * D : 3 * D, :]) + eb1[...]
    upper, lower = split(received)
    table = jnp.concatenate([upper, zeros, lower, zeros], axis=0)
    arrive(1)
    aggregate = jnp.zeros((OWN, D), F32)
    for row, count, edges, base in chunks:
        at = slice(row, row + count)
        edge = edges[base : base + count, :]
        pre = dot(edge, w1[0:D, :]) + dot(senders[at, :], w1[D : 2 * D, :]) + dot(expand[at, :], table)
        act, slope[at, :] = silu_and_slope(pre)
        unit, inv_std = normalize(dot(act, w2[...]) + eb2[...])
        normed[at, :] = unit
        inv[at, :] = inv_std
        message = edge.astype(F32) + unit * eg[...] + es[...]
        aggregate += dot(spread[:, at], message.astype(BF16))

    arrive(2)
    arrive(3)
    pre = dot(own[...], n1[0:D, :]) + dot(aggregate.astype(BF16), n1[D : 2 * D, :]) + nb1[...]
    act, node_slope = silu_and_slope(pre)
    unit, inv_std = normalize(dot(act, n2[...]) + nb2[...])
    node_out[...] = (own[...].astype(F32) + unit * ng[...] + ns[...]).astype(BF16)
    cotangent = cot[...].astype(F32)
    back = norm_back(cotangent * ng[...], unit, inv_std).astype(BF16)
    back = (dot_t(back, n2[...]) * node_slope).astype(BF16)
    result = cotangent + dot_t(back, n1[0:D, :])
    upper, lower = split(dot_t(back, n1[D : 2 * D, :]))
    table = jnp.concatenate([upper, zeros, lower, zeros], axis=0)

    received = jnp.zeros((OWN, D), F32)
    mine = core[0] == 0
    for index, (row, count, _, base) in enumerate(chunks):
        at = slice(row, row + count)
        grad = dot(expand[at, :], table)
        back = norm_back(grad * eg[...], normed[at, :], inv[at, :]).astype(BF16)
        back = (dot_t(back, w2[...]) * slope[at, :]).astype(BF16)
        edge_grad = (grad + dot_t(back, w1[0:D, :])).astype(BF16)
        send_grad = dot_t(back, w1[D : 2 * D, :]).astype(BF16)
        received += dot(spread[:, at], back)
        if index == 0:
            local_grad[...] = edge_grad
            local_send[...] = dot(send_t[...], send_grad).astype(BF16)
        else:
            cut_grad[base : base + count, :] = edge_grad
            summed = dot(pick_t[index - 1], send_grad)
            for dz in range(2):
                for x in range(X):
                    start = (dz * X + x) * C * BORDER
                    first = summed[start : start + BORDER, :]
                    second = summed[start + BORDER : start + 2 * BORDER, :]
                    to = (x * Z + 2 * (index - 1) + dz) * BORDER
                    keep[to : to + BORDER, :] = jnp.where(mine, first, second)
                    send[to : to + BORDER, :] = jnp.where(mine, second, first).astype(BF16)
    upper, lower = split(received)
    both = dot_t(jnp.concatenate([upper, lower], axis=0), w1[2 * D : 3 * D, :])
    own_grad[...] = result + both[0:OWN, :] + both[OWN : 2 * OWN, :]


def shape(*dims, kind=BF16):
    return jax.ShapeDtypeStruct(dims, kind)


VMEM = pl.BlockSpec(memory_space=pltpu.VMEM)


def prepare(*args):
    return pl.pallas_call(
        prepare_body,
        in_specs=[VMEM] * 8,
        out_specs=[VMEM] * 5,
        out_shape=[
            shape(ALL, D), shape(ALL, 256), shape(OWN, ALL), shape(GROUPS, GROUP, GROUP), shape(PART, LOC),
        ],
        compiler_params=pltpu.CompilerParams(vmem_limit_bytes=24 * 1024 * 1024),
        cost_estimate=pl.CostEstimate(flops=800_000_000, bytes_accessed=6_000_000, transcendentals=0),
        name="prepare",
    )(*args)


def layer(*args):
    return pl.pallas_call(
        layer_body,
        in_specs=[pl.BlockSpec(memory_space=pltpu.SMEM), pl.BlockSpec(memory_space=pl.ANY)] + [VMEM] * 17,
        out_specs=[VMEM] * 7,
        out_shape=[
            shape(OWN, D), shape(LOC, D), shape(CUT, D), shape(OWN, D, kind=F32),
            shape(CUT // 2, D, kind=F32), shape(CUT // 2, D), shape(PART, D),
        ],
        scratch_shapes=[
            pltpu.VMEM((3 * D, D), BF16),
            pltpu.VMEM((D, D), BF16),
            pltpu.VMEM((2 * D, D), BF16),
            pltpu.VMEM((D, D), BF16),
            pltpu.VMEM((ALL, D), F32),
            pltpu.VMEM((ALL, D), F32),
            pltpu.VMEM((ALL, 1), F32),
            pltpu.SemaphoreType.DMA((4, F)),
        ],
        compiler_params=pltpu.CompilerParams(vmem_limit_bytes=40 * 1024 * 1024),
        cost_estimate=pl.CostEstimate(flops=4_000_000_000, bytes_accessed=12_000_000, transcendentals=600_000),
        name="layer",
    )(*args)


def exchange(values, axis):
    return lax.all_to_all(values, axis, split_axis=0, concat_axis=0, tiled=True)


def shards(
    node_in, local_edges, cut_edges, node_cot, edge_w1, edge_w2, node_w1, node_w2,
    edge_b1, edge_b2, edge_gain, edge_shift, node_b1, node_b2, node_gain, node_shift,
    local_send, local_recv, cut_send, cut_recv, cut_count,
):
    feat = lax.axis_index("feat")
    core = lax.axis_index("core")
    partition = (lax.axis_index("z") * X + lax.axis_index("x")) * C + core
    packed = jnp.concatenate([edge_w1, edge_w2, node_w1, node_w2], axis=0)
    weights = lax.all_gather(packed, "feat", axis=0, tiled=False)

    selectors = cut_send[0, 0].astype(BF16).reshape(2, D)
    payload = jnp.concatenate([node_in[:BORDER], selectors], axis=0)
    payload = exchange(jnp.broadcast_to(payload[None], (Z, PACK, D)), "z")
    payload = exchange(jnp.broadcast_to(payload[None], (X, Z, PACK, D)), "x")
    other = lax.ppermute(payload, "core", [(0, 1), (1, 0)])
    border = jnp.where(core == 0, jnp.stack([payload, other]), jnp.stack([other, payload]))
    selectors = lax.dynamic_slice(
        border,
        (0, 0, 0, BORDER + partition // 32, (partition % 32) * SLOTS),
        (C, X, Z, 1, SLOTS),
    )
    selectors = selectors.reshape(C, X, Z, SLOTS).transpose(2, 1, 0, 3).reshape(CUT).astype(jnp.int32)
    selectors = selectors + (jnp.arange(CUT, dtype=jnp.int32) % GROUP) // SLOTS * SLOTS

    live = jnp.arange(SLOTS, dtype=jnp.int32)[None, :] < cut_count[0, 0][:, None]
    receivers = jnp.concatenate([local_recv, jnp.where(live.reshape(-1), cut_recv[0, 0], -1)])
    senders, expand, spread, pick_t, send_t = prepare(
        node_in, border, local_send[:, None], local_send[None, :], receivers[:, None], receivers[None, :],
        selectors[:, None], selectors[None, :],
    )
    own = lax.dynamic_slice_in_dim(node_in, feat * OWN, OWN, 0)
    vectors = [
        v[None, :]
        for v in (edge_b1, edge_b2, edge_gain, edge_shift, node_b1, node_b2, node_gain, node_shift)
    ]
    node_out, local_grad, cut_grad, own_grad, keep, send, local_sums = layer(
        core.astype(jnp.int32).reshape(1), weights, senders, local_edges, cut_edges, expand, spread, pick_t,
        send_t, own, node_cot, *vectors,
    )
    scattered = lax.psum_scatter(local_sums, "feat", scatter_dimension=0, tiled=True)
    summed = keep + lax.ppermute(send, "core", [(0, 1), (1, 0)]).astype(F32)
    summed = exchange(summed.astype(BF16).reshape(X, Z * BORDER, D), "x")
    summed = jnp.sum(summed.astype(F32), axis=0)
    summed = exchange(summed.astype(BF16).reshape(Z, BORDER, D), "z")
    summed = jnp.sum(summed.astype(F32), axis=0).astype(BF16)
    summed = exchange(jnp.broadcast_to(summed[None], (F, BORDER, D)), "feat")
    summed = jnp.where(feat == 0, jnp.sum(summed.astype(F32), axis=0), 0.0)
    node_grad = own_grad + scattered.astype(F32) + jnp.pad(summed, ((0, OWN - BORDER), (0, 0)))
    return node_out, node_grad, local_grad, cut_grad


def solution(mesh):
    split_mesh = Mesh(mesh.devices.reshape(Z, X, C, F), (*DOM, "feat"))
    both = (*DOM, "feat")
    placed = (
        P(DOM, None),
        *[P(both, None)] * 3,
        *[P("feat", None)] * 4,
        *[P()] * 8,
        *[P(both)] * 2,
        *[P(DOM, "feat", None)] * 3,
    )
    return jax.shard_map(
        shards,
        mesh=split_mesh,
        in_specs=placed,
        out_specs=(P(both, None),) * 4,
        check_vma=False,
    )
```

time: 228 us -> 151 us (0.66)
  matrix products: 32.3 us -> 0 us
  Pallas kernels: 0 us -> 19 us
  local copies, waits for them, and re-layouts: 33.8 us -> 16.1 us
  waiting for transfers between devices: 47.8 us -> 32.8 us
  starting transfers between devices: 24.5 us -> 13.1 us
  other arithmetic: 15.6 us -> 5.11 us
  blocking collectives: 58.3 us -> 49.1 us
    all_gather x2 -> x0, blocking collectives: 58.3 us -> none  [the longest x1 29.6 us: shards(): lax.all_gather(edge_w2, 'feat', axis=0, tiled=True)]
    all_to_all x0 -> x3, blocking collectives: none -> 49.1 us  [exchange(): return lax.all_to_all(values, axis, split_axis=0, concat_axis=0, tiled=True)]
    dot_general x15 -> x0, matrix products: 32.3 us -> none  [the longest x2 11.7 us: times_transpose(): lax.dot_general(operand, weight, (((1,), (1,)), ((), ())), preferred_elem...]
    reduce_scatter x1, waiting for transfers between devices: 24.6 us -> 0.02 us  [shards(): lax.psum_scatter(local_sums, 'feat', scatter_dimension=0, tiled=True)]
    pallas_call x0 -> x2, Pallas kernels: none -> 19 us  [the longest x1 18.1 us: layer(): pl.pallas_call(layer_body, in_specs=[pl.BlockSpec(memory_space=pltpu.SMEM...]
    gather x8 -> x0, local copies, waits for them, and re-layouts: 15.3 us -> none  [the longest x2 7.43 us: shards(): grad_message = all_live[:, None] * jnp.take(grad_agg, all_recv, axis=0)]
    all_to_all x2, starting transfers between devices: 24.2 us -> 9.26 us  [exchange(): return lax.all_to_all(values, axis, split_axis=0, concat_axis=0, tiled=True)]
    all_gather x2 -> x1, waiting for transfers between devices: 0.02 us -> 14.3 us  [shards(): weights = lax.all_gather(packed, 'feat', axis=0, tiled=False)]
  transfers between devices with their start and end apart: 5 -> 6, of which waited for: 2 -> 5; matrix products, arithmetic and copies ran while one was open for 19% -> 4% of each run, Pallas kernels for 0% -> 1%
where the time goes in v1:
time: 151 us; the launch traced here: 150 us
  blocking collectives  49.1 us (33%)
  waiting for transfers between devices  32.8 us (22%)
  Pallas kernels  19 us (13%)
  local copies, waits for them, and re-layouts  16.1 us (11%)
  between operations  14.4 us (10%)
  starting transfers between devices  13.1 us (9%)
  other arithmetic  5.11 us (3%)
    all_to_all x3, blocking collectives, exchange(): return lax.all_to_all(values, axis, split_axis=0, concat_axis=0, tiled=True)  49.1 us
    pallas_call x1, Pallas kernels, layer(): pl.pallas_call(layer_body, in_specs=[pl.BlockSpec(memory_space=pltpu.SMEM...  18.1 us
    all_to_all x2, waiting for transfers between devices, exchange(): return lax.all_to_all(values, axis, split_axis=0, concat_axis=0, tiled=True)  15.4 us
    all_gather x1, waiting for transfers between devices, shards(): weights = lax.all_gather(packed, 'feat', axis=0, tiled=False)  14.3 us
    unnamed x50, local copies, waits for them, and re-layouts  12.5 us
    all_to_all x2, starting transfers between devices, exchange(): return lax.all_to_all(values, axis, split_axis=0, concat_axis=0, tiled=True)  9.26 us
  transfers between devices with their start and end apart: 6, of which 5 were waited for; matrix products, arithmetic and copies ran while one was open for 4% of the time, Pallas kernels for 1%

profile of v1, /device:TPU:6, one launch (start us, length us, event | category | flops | bytes accessed | tf_op | source)
XLA Modules:
  0.0 149.7 jit_solution(11709515401539151583)
XLA Ops:
  7.2 0.0 all-gather.3.cloned.1.call-start
  7.2 1.9 %pad_maximum_fusion = bf16[448,512]{1,0:T(8,128)(2,1)} fusion(bf16[64,512]{1,0:T(8,128)(2,1)} %param.28, bf16[128,512]{1,0:T(8,128)(2,1)} %param.27, bf16[64,512]{1,0:T(8,128)(2,1)} %param.26, bf16[192,512]{1,0:T(8,128)(2,1)} %param.25), kind=kLoop, calls=%fused_computation.19 | loop fusion | flops 1835008 | bytes 917504 | tf_op jit(solution)/shard_map/concatenate | solution.py:227
  9.1 0.0 all-gather.3.cloned.1.call-update
  9.1 0.0 copy-start.23
  9.1 0.0 copy-start.22
  9.1 0.0 copy-start.24
  9.1 0.7 convert_reduce_fusion.1
  9.9 0.7 slice.3
  10.6 20.6 %all_to_all.25 = bf16[8,18,512]{2,1,0:T(8,128)(2,1)S(1)} all-to-all(bf16[8,18,512]{2,1,0:T(8,128)(2,1)S(1)} %broadcast_in_dim.65), channel_id=1, replica_groups=mesh['z'=8,'x'=4,'core'=2,'feat'=8] {'z'}, dimensions={0} | all-to-all | bytes 294912 | tf_op jit(solution)/shard_map/all_to_all | solution.py:216
  31.3 0.9 broadcast_in_dim.66
  32.1 4.8 %all-to-all-start.1 = ((bf16[4,8,18,512]{3,1,2,0:T(8,128)(2,1)}), bf16[4,8,18,512]{3,1,2,0:T(8,128)(2,1)S(1)}, u32[]{:S(2)}, u32[]{:S(2)}) async-start(bf16[4,8,18,512]{3,1,2,0:T(8,128)(2,1)} %broadcast_in_dim.66), calls=%async_computation.1 | async-start | bytes 1179648 | tf_op jit(solution)/shard_map/all_to_all | solution.py:216
  36.9 0.0 reduce-scatter.2.cloned.1.call-start
  36.9 6.4 %all-to-all-done.1 = bf16[4,8,18,512]{3,1,2,0:T(8,128)(2,1)S(1)} async-done(((bf16[4,8,18,512]{3,1,2,0:T(8,128)(2,1)}), bf16[4,8,18,512]{3,1,2,0:T(8,128)(2,1)S(1)}, u32[]{:S(2)}, u32[]{:S(2)}) %all-to-all-start.1) | async-done | bytes 589856 | tf_op jit(solution)/shard_map/all_to_all | solution.py:216
  43.3 1.9 %collective-permute-start = (bf16[4,8,18,512]{3,1,2,0:T(8,128)(2,1)S(1)}, bf16[4,8,18,512]{3,1,2,0:T(8,128)(2,1)S(1)}, u32[]{:S(2)}, u32[]{:S(2)}) collective-permute-start(bf16[4,8,18,512]{3,1,2,0:T(8,128)(2,1)S(1)} %all-to-all-done.1), channel_id=1, source_target_pairs={{0,8},{8,0},{1,9},{9,1},{2,10},{10,2},{3,11},{11,3},{4,12},{12,4},... | collective-permute-start | bytes 1769480 | tf_op jit(solution)/shard_map/ppermute | solution.py:234
  45.2 0.0 copy-done.23
  45.2 0.1 iota_compare_fusion
  45.3 0.1 lt.46
  45.4 0.2 broadcast_in_dim.82.recv_col
  45.7 0.1 copy.63.lsend_col
  45.8 0.0 copy-done
  45.8 0.2 copy.70
  46.0 1.1 collective-permute-done
  47.2 0.2 copy.69
  47.4 0.3 maximum_select_fusion.border
  47.7 0.1 dynamic-slice_convert_fusion
  47.8 0.1 reshape.208
  47.9 0.3 reshape.212
  48.3 0.1 fusion.2.sel_col
  48.4 0.0 copy-start.14
  48.4 0.0 copy-start.15
  48.4 0.0 copy-start.16
  48.4 0.0 copy-start.17
  48.4 0.0 copy-start.18
  48.4 0.0 copy-start.19
  48.5 0.0 copy-start.20
  48.5 0.0 copy-start.21
  48.5 0.9 prepare.1
  49.4 0.0 copy-start.3
  49.4 1.0 copy-done.3
  50.4 0.8 copy-done.6
  51.2 0.7 copy-done.8
  51.9 0.7 copy-done.10
  52.6 14.3 %all-gather.3.cloned.1.call-done = bf16[3584,512]{1,0:T(8,128)(2,1)} async-done(((bf16[448,512]{1,0:T(8,128)(2,1)}), bf16[3584,512]{1,0:T(8,128)(2,1)}) %all-gather.3.cloned.1.call-update) | async-done | bytes 3670032 | tf_op jit(solution)/shard_map/all_gather | solution.py:228
  67.0 2.0 %copy-done.2 = bf16[3584,512]{1,0:T(8,128)(2,1)S(1)} copy-done((bf16[3584,512]{1,0:T(8,128)(2,1)S(1)}, bf16[3584,512]{1,0:T(8,128)(2,1)}, u32[]{:S(2)}) %copy-start.2) | copy-done | bytes 3670040
  69.0 1.3 copy-done.4
  70.3 1.2 copy-done.5
  71.5 1.1 copy-done.7
  72.6 0.9 copy-done.9
  73.5 0.9 copy-done.11
  74.4 0.9 copy-done.12
  75.3 0.9 copy-done.13
  76.2 18.1 %layer.1 = (bf16[80,512]{1,0:T(8,128)(2,1)}, bf16[128,512]{1,0:T(8,128)(2,1)}, bf16[1024,512]{1,0:T(8,128)(2,1)}, f32[80,512]{1,0:T(8,128)S(1)}, f32[512,512]{1,...) custom-call(s32[1]{0:T(128)} %bitcast.core, bf16[8,448,512]{2,1,0:T(8,128)(2,1)S(1)} %bitcast.27, ...), custom_call_target="tpu_custom_call" | custom-call | flops 4000000000 | bytes 12000000 | tf_op jit(solution)/shard_map/layer/pallas_call | solution.py:191
  94.3 1.9 %collective-permute-start.1 = (bf16[512,512]{1,0:T(8,128)(2,1)S(1)}, bf16[512,512]{1,0:T(8,128)(2,1)S(1)}, u32[]{:S(2)}, u32[]{:S(2)}) collective-permute-start(bf16[512,512]{1,0:T(8,128)(2,1)S(1)} %get-tuple-element.25), channel_id=1, source_target_pairs={{0,8},{8,0},{1,9},{9,1},{2,10},{10,2},{3,11},{11,3},{4,12},{12,4},... | collective-permute-start | bytes 1572872 | tf_op jit(solution)/shard_map/ppermute | solution.py:260
  96.2 0.0 reduce-scatter.2.cloned.1.call-update
  96.3 1.9 %collective-permute-done.1 = bf16[512,512]{1,0:T(8,128)(2,1)S(1)} collective-permute-done((bf16[512,512]{1,0:T(8,128)(2,1)S(1)}, bf16[512,512]{1,0:T(8,128)(2,1)S(1)}, u32[]{:S(2)}, u32[]{:S(2)}) %collective-permute-start.1) | collective-permute-done | bytes 524320 | tf_op jit(solution)/shard_map/ppermute | solution.py:260
  98.1 0.2 add_convert_fusion
  98.3 12.3 %all_to_all.26 = bf16[4,128,512]{2,1,0:T(8,128)(2,1)S(1)} all-to-all(bf16[4,128,512]{2,1,0:T(8,128)(2,1)S(1)} %bitcast.38), channel_id=1, replica_groups=mesh['z'=8,'x'=4,'core'=2,'feat'=8] {'x'}, dimensions={0} | all-to-all | bytes 1048576 | tf_op jit(solution)/shard_map/all_to_all | solution.py:216
  110.6 0.1 reduce_sum.33
  110.7 16.3 %all_to_all.27 = bf16[8,16,512]{2,1,0:T(8,128)(2,1)S(1)} all-to-all(bf16[8,16,512]{2,1,0:T(8,128)(2,1)S(1)} %bitcast.39), channel_id=1, replica_groups=mesh['z'=8,'x'=4,'core'=2,'feat'=8] {'z'}, dimensions={0} | all-to-all | bytes 262144 | tf_op jit(solution)/shard_map/all_to_all | solution.py:216
  126.9 0.7 broadcast_in_dim.80
  127.6 4.5 %all-to-all-start.4 = ((bf16[8,16,512]{2,1,0:T(8,128)(2,1)}), bf16[8,16,512]{2,1,0:T(8,128)(2,1)S(1)}, u32[]{:S(2)}, u32[]{:S(2)}) async-start(bf16[8,16,512]{2,1,0:T(8,128)(2,1)} %broadcast_in_dim.80), calls=%async_computation.5 | async-start | bytes 262144 | tf_op jit(solution)/shard_map/all_to_all | solution.py:216
  132.1 9.1 %all-to-all-done.4 = bf16[8,16,512]{2,1,0:T(8,128)(2,1)S(1)} async-done(((bf16[8,16,512]{2,1,0:T(8,128)(2,1)}), bf16[8,16,512]{2,1,0:T(8,128)(2,1)S(1)}, u32[]{:S(2)}, u32[]{:S(2)}) %all-to-all-start.4) | async-done | bytes 131104 | tf_op jit(solution)/shard_map/all_to_all | solution.py:216
  141.2 0.0 reduce-scatter.2.cloned.1.call-done
  141.2 1.6 %pad_add_fusion = f32[80,512]{1,0:T(8,128)} fusion(f32[16,512]{1,0:T(8,128)S(1)} %broadcast_select_fusion, f32[80,512]{1,0:T(8,128)S(1)} %get-tuple-element.22, bf16[80,512]{1,0:T(8,128)(2,1)} %reduce-scatter.2.cloned.1.call-done), kind=kLoop, calls=%fused_computation.21 | loop fusion | flops 122880 | bytes 442368 | tf_op jit(solution)/shard_map/add | solution.py:267
  (37 shorter events, 0.3 us)
Async XLA Ops:
  7.2 59.8 %all-gather.3.cloned.1.call-start = ((), (), s32[]{:S(2)}) async-start(), calls=%async_computation.7 | async-start | bytes 4128768 | tf_op jit(solution)/shard_map/all_gather | solution.py:228
  9.1 36.1 %copy-start.23 = (s32[1,1,64]{2,1,0:T(1,128)S(1)}, s32[1,1,64]{2,1,0:T(1,128)}, u32[]{:S(2)}) copy-start(s32[1,1,64]{2,1,0:T(1,128)} %param.41) | copy-start | bytes 772
  9.1 36.2 %copy-start.22 = (s32[1,1,1024]{2,1,0:T(1,128)S(1)}, s32[1,1,1024]{2,1,0:T(1,128)}, u32[]{:S(2)}) copy-start(s32[1,1,1024]{2,1,0:T(1,128)} %param.40) | copy-start | bytes 12292
  9.1 36.2 %copy-start.24 = (s32[128]{0:T(128)S(1)}, s32[128]{0:T(128)}, u32[]{:S(2)}) copy-start(s32[128]{0:T(128)} %param.38) | copy-start | bytes 1540
  31.2 14.5 %copy-start.1 = (s32[128]{0:T(128)S(1)}, s32[128]{0:T(128)}, u32[]{:S(2)}) copy-start(s32[128]{0:T(128)} %param.37) | copy-start | bytes 1540
  31.2 14.6 %copy-start = (bf16[640,512]{1,0:T(8,128)(2,1)S(1)}, bf16[640,512]{1,0:T(8,128)(2,1)}, u32[]{:S(2)}) copy-start(bf16[640,512]{1,0:T(8,128)(2,1)} %nodes.1) | copy-start | bytes 1966084
  32.1 11.1 %all-to-all-start.1 = ((bf16[4,8,18,512]{3,1,2,0:T(8,128)(2,1)}), bf16[4,8,18,512]{3,1,2,0:T(8,128)(2,1)S(1)}, u32[]{:S(2)}, u32[]{:S(2)}) async-start(bf16[4,8,18,512]{3,1,2,0:T(8,128)(2,1)} %broadcast_in_dim.66), calls=%async_computation.1 | async-start | bytes 1179648 | tf_op jit(solution)/shard_map/all_to_all | solution.py:216
  36.9 104.3 %reduce-scatter.2.cloned.1.call-start = ((), (), s32[]{:S(2)}) async-start(), calls=%async_computation.6 | async-start | bytes 737280 | tf_op jit(solution)/shard_map/reduce_scatter | solution.py:259
  43.3 3.9 %collective-permute-start = (bf16[4,8,18,512]{3,1,2,0:T(8,128)(2,1)S(1)}, bf16[4,8,18,512]{3,1,2,0:T(8,128)(2,1)S(1)}, u32[]{:S(2)}, u32[]{:S(2)}) collective-permute-start(bf16[4,8,18,512]{3,1,2,0:T(8,128)(2,1)S(1)} %all-to-all-done.1), channel_id=1, source_target_pairs={{0,8},{8,0},{1,9},{9,1},{2,10},{10,2},{3,11},{11,3},{4,12},{12,4},... | collective-permute-start | bytes 1769480 | tf_op jit(solution)/shard_map/ppermute | solution.py:234
  48.4 18.5 %copy-start.14 = (f32[512]{0:T(512)S(1)}, f32[512]{0:T(512)}, u32[]{:S(2)}) copy-start(f32[512]{0:T(512)} %param.29) | copy-start | bytes 6148
  48.4 18.5 %copy-start.15 = (f32[512]{0:T(512)S(1)}, f32[512]{0:T(512)}, u32[]{:S(2)}) copy-start(f32[512]{0:T(512)} %param.30) | copy-start | bytes 6148
  48.4 18.5 %copy-start.16 = (f32[512]{0:T(512)S(1)}, f32[512]{0:T(512)}, u32[]{:S(2)}) copy-start(f32[512]{0:T(512)} %param.31) | copy-start | bytes 6148
  48.4 18.5 %copy-start.17 = (f32[512]{0:T(512)S(1)}, f32[512]{0:T(512)}, u32[]{:S(2)}) copy-start(f32[512]{0:T(512)} %param.32) | copy-start | bytes 6148
  48.4 18.5 %copy-start.18 = (f32[512]{0:T(512)S(1)}, f32[512]{0:T(512)}, u32[]{:S(2)}) copy-start(f32[512]{0:T(512)} %param.33) | copy-start | bytes 6148
  48.4 18.5 %copy-start.19 = (f32[512]{0:T(512)S(1)}, f32[512]{0:T(512)}, u32[]{:S(2)}) copy-start(f32[512]{0:T(512)} %param.34) | copy-start | bytes 6148
  48.5 18.5 %copy-start.20 = (f32[512]{0:T(512)S(1)}, f32[512]{0:T(512)}, u32[]{:S(2)}) copy-start(f32[512]{0:T(512)} %param.35) | copy-start | bytes 6148
  48.5 18.5 %copy-start.21 = (f32[512]{0:T(512)S(1)}, f32[512]{0:T(512)}, u32[]{:S(2)}) copy-start(f32[512]{0:T(512)} %param.36) | copy-start | bytes 6148
  49.4 1.0 copy-start.3
  50.4 0.8 copy-start.6
  51.2 0.7 copy-start.8
  51.9 0.7 copy-start.10
  67.0 2.0 %copy-start.2 = (bf16[3584,512]{1,0:T(8,128)(2,1)S(1)}, bf16[3584,512]{1,0:T(8,128)(2,1)}, u32[]{:S(2)}) copy-start(bf16[3584,512]{1,0:T(8,128)(2,1)} %all-gather.3.cloned.1.call-done) | copy-start | bytes 11010052
  69.0 1.3 copy-start.4
  70.3 1.2 copy-start.5
  71.5 1.1 copy-start.7
  72.6 0.9 copy-start.9
  73.5 0.9 copy-start.11
  74.4 0.9 copy-start.12
  75.3 0.9 copy-start.13
  94.3 3.8 %collective-permute-start.1 = (bf16[512,512]{1,0:T(8,128)(2,1)S(1)}, bf16[512,512]{1,0:T(8,128)(2,1)S(1)}, u32[]{:S(2)}, u32[]{:S(2)}) collective-permute-start(bf16[512,512]{1,0:T(8,128)(2,1)S(1)} %get-tuple-element.25), channel_id=1, source_target_pairs={{0,8},{8,0},{1,9},{9,1},{2,10},{10,2},{3,11},{11,3},{4,12},{12,4},... | collective-permute-start | bytes 1572872 | tf_op jit(solution)/shard_map/ppermute | solution.py:260
  127.6 13.6 %all-to-all-start.4 = ((bf16[8,16,512]{2,1,0:T(8,128)(2,1)}), bf16[8,16,512]{2,1,0:T(8,128)(2,1)S(1)}, u32[]{:S(2)}, u32[]{:S(2)}) async-start(bf16[8,16,512]{2,1,0:T(8,128)(2,1)} %broadcast_in_dim.80), calls=%async_computation.5 | async-start | bytes 262144 | tf_op jit(solution)/shard_map/all_to_all | solution.py:216
Sparse Core Ops, SparseCore 0:
  10.1 56.7 all-gather.2
  96.4 39.2 reduce-scatter.1

commit v2 on v1

v2 whole, which is shorter than its diff:
```python
import jax
import jax.numpy as jnp
from jax import lax
from jax.experimental import pallas as pl
from jax.experimental.pallas import tpu as pltpu
from jax.sharding import Mesh
from jax.sharding import PartitionSpec as P

Z, X, C, F = 8, 4, 2, 8
DOM = ("z", "x", "core")
D = 512
BORDER = 16
SLOTS = 16
OWN = 80
LOC = 128
CUT = 1024
ALL = LOC + CUT
PART = 640
GROUP = 256
GROUPS = CUT // GROUP
PACK = BORDER + 8
EPS = 1e-05
LIMIT = 60 * 1024 * 1024
F32 = jnp.float32
BF16 = jnp.bfloat16


def dot(left, right):
    return jnp.dot(left, right, preferred_element_type=F32)


def dot_t(left, right):
    return lax.dot_general(left, right, (((1,), (1,)), ((), ())), preferred_element_type=F32)


def onehot(match):
    return jnp.where(match, 1.0, 0.0).astype(BF16)


def iota(shape, axis):
    return lax.broadcasted_iota(jnp.int32, shape, axis)


def normalize(values):
    centered = values - jnp.mean(values, axis=-1, keepdims=True)
    inv_std = lax.rsqrt(jnp.mean(centered * centered, axis=-1, keepdims=True) + EPS)
    return centered * inv_std, inv_std


def norm_back(scaled, normed, inv_std):
    first_mean = jnp.mean(scaled, axis=-1, keepdims=True)
    second_mean = jnp.mean(scaled * normed, axis=-1, keepdims=True)
    return inv_std * (scaled - first_mean - normed * second_mean)


def silu_and_slope(values):
    sigmoid = 0.5 * jnp.tanh(0.5 * values) + 0.5
    act = values * sigmoid
    return act.astype(BF16), sigmoid + act * (1.0 - sigmoid)


def split(values):
    upper = values.astype(BF16)
    return upper, (values - upper.astype(F32)).astype(BF16)


def index_body(
    feat, nodes, sent, moved, local_to, cut_to, counts, eb1, eb2, eg, es, nb1, nb2, ng, ns,
    senders, expand, spread, send_t, own, vectors,
):
    for i, vector in enumerate((eb1, eb2, eg, es, nb1, nb2, ng, ns)):
        vectors[i : i + 1, :] = vector[...]
    own[...] = nodes[pl.ds(pl.multiple_of(feat[0] * OWN, 16), OWN), :]
    pick = jnp.where(sent[...] == iota((PART, LOC), 0), 1.0, 0.0)
    senders[...] = dot(pick.T.astype(BF16), nodes[...]).astype(BF16)
    send_t[...] = onehot(moved[...] == iota((PART, LOC), 0))
    sources = CUT // SLOTS
    repeat = onehot(iota((sources, CUT), 1) // SLOTS == iota((sources, CUT), 0))
    count = dot(counts[...].astype(F32).astype(BF16), repeat)
    live = (iota((1, CUT), 1) & (SLOTS - 1)).astype(F32) < count
    cut = jnp.where(live, cut_to[...], -1)
    for start, count, to in ((0, LOC, local_to[...]), (LOC, CUT, cut)):
        match = jnp.where(to == iota((128, count), 0), 1.0, 0.0)
        spread[:, start : start + count] = match[0:OWN, :].astype(BF16)
        turned = match.T.astype(BF16)
        expand[start : start + count, 0:128] = turned
        expand[start : start + count, 128:256] = turned


def pick_body(where, near, far, senders, pick_t, selected):
    z, x, c = [where[i] for i in range(3)]
    partition = (z * X + x) * C + c
    tables = []
    for zz in range(Z):
        blocks = []
        for xx in range(X):
            step, turn = (x - xx + X) % X, (z + 1 - zz + Z) % Z
            pair = near[step, turn], far[step, turn]
            for cc in range(C):
                block = jnp.where(c == cc, pair[0], pair[1])
                blocks.append(block[0:BORDER, :])
                row = jnp.where(partition < 32, block[BORDER : BORDER + 1, :], block[BORDER + 1 : BORDER + 2, :])
                place = (zz * X + xx) * C + cc
                selected[place : place + 1, :] = row.astype(F32)
        tables.append(jnp.concatenate(blocks, axis=0))
    offset = (partition & 31) * SLOTS
    take = onehot(iota((D, GROUP), 0) == (iota((D, GROUP), 1) & (SLOTS - 1)) + offset)
    values = dot(selected[...].astype(BF16), take)
    lanes, rows = iota((SLOTS, GROUP), 1), iota((SLOTS, GROUP), 0)
    for k in range(GROUPS):
        group = values[k * SLOTS : (k + 1) * SLOTS, :]
        picked = jnp.sum(jnp.where(lanes // SLOTS == rows, group, 0.0), axis=0, keepdims=True)
        picked = picked.astype(jnp.int32) + iota((1, GROUP), 1) // SLOTS * SLOTS
        match = jnp.where(picked == iota((GROUP, GROUP), 0), 1.0, 0.0)
        pick_t[k, :, :] = match.astype(BF16)
        table = jnp.concatenate(tables[2 * k : 2 * k + 2], axis=0)
        senders[k * GROUP : (k + 1) * GROUP, :] = dot(match.T.astype(BF16), table).astype(BF16)


def layer_body(
    core, mine, other, local_edges, cut_edges, cot, local_senders, expand, spread, send_t, own, vectors,
    cut_senders, pick_t,
    node_out, local_grad, cut_grad, own_grad, keep, send, local_keep, local_send,
    w1, w2, n1, n2, edges, slope, normed, inv, sems, edge_sems,
):
    copies = []
    edge_copies = [
        pltpu.make_async_copy(local_edges, edges.at[pl.ds(0, LOC), :], edge_sems.at[0]),
        pltpu.make_async_copy(cut_edges, edges.at[pl.ds(LOC, CUT), :], edge_sems.at[1]),
    ]
    first = core[0]
    for i, (ref, start, size) in enumerate(((w1, 0, 96), (w2, 96, 32), (n1, 128, 64), (n2, 192, 32))):
        for f in range(F):
            for j, (half, place) in enumerate(((mine, first), (other, 1 - first))):
                to = pl.multiple_of((2 * f + place) * size, 32)
                copy = pltpu.make_async_copy(
                    half.at[f, pl.ds(start, size), :], ref.at[pl.ds(to, size), :], sems.at[i, f, j]
                )
                copy.start()
                copies.append((i, copy))
        if i == 0:
            for copy in edge_copies:
                copy.start()
    eb1, eb2, eg, es, nb1, nb2, ng, ns = [vectors.at[pl.ds(i, 1), :] for i in range(8)]

    def arrive(which):
        for i, copy in copies:
            if i == which:
                copy.wait()

    chunks = [(0, LOC)] + [(LOC + k * GROUP, GROUP) for k in range(GROUPS)]
    zeros = jnp.zeros((128 - OWN, D), BF16)

    arrive(0)
    received = dot(own[...], w1[2 * D : 3 * D, :]) + eb1[...]
    upper, lower = split(received)
    table = jnp.concatenate([upper, zeros, lower, zeros], axis=0)
    arrive(1)
    for copy in edge_copies:
        copy.wait()
    aggregate = jnp.zeros((OWN, D), F32)
    for row, count in chunks:
        at = slice(row, row + count)
        edge = edges[at, :]
        sender = local_senders[...] if row == 0 else cut_senders[row - LOC : row - LOC + count, :]
        pre = dot(edge, w1[0:D, :]) + dot(sender, w1[D : 2 * D, :]) + dot(expand[at, :], table)
        act, slope[at, :] = silu_and_slope(pre)
        unit, inv_std = normalize(dot(act, w2[...]) + eb2[...])
        normed[at, :] = unit
        inv[at, :] = inv_std
        message = edge.astype(F32) + unit * eg[...] + es[...]
        aggregate += dot(spread[:, at], message.astype(BF16))

    arrive(2)
    arrive(3)
    pre = dot(own[...], n1[0:D, :]) + dot(aggregate.astype(BF16), n1[D : 2 * D, :]) + nb1[...]
    act, node_slope = silu_and_slope(pre)
    unit, inv_std = normalize(dot(act, n2[...]) + nb2[...])
    node_out[...] = (own[...].astype(F32) + unit * ng[...] + ns[...]).astype(BF16)
    cotangent = cot[...].astype(F32)
    back = norm_back(cotangent * ng[...], unit, inv_std).astype(BF16)
    back = (dot_t(back, n2[...]) * node_slope).astype(BF16)
    result = cotangent + dot_t(back, n1[0:D, :])
    upper, lower = split(dot_t(back, n1[D : 2 * D, :]))
    table = jnp.concatenate([upper, zeros, lower, zeros], axis=0)

    received = jnp.zeros((OWN, D), F32)
    is_first = first == 0
    for index, (row, count) in enumerate(chunks):
        at = slice(row, row + count)
        grad = dot(expand[at, :], table)
        back = norm_back(grad * eg[...], normed[at, :], inv[at, :]).astype(BF16)
        back = (dot_t(back, w2[...]) * slope[at, :]).astype(BF16)
        edge_grad = (grad + dot_t(back, w1[0:D, :])).astype(BF16)
        send_grad = dot_t(back, w1[D : 2 * D, :]).astype(BF16)
        received += dot(spread[:, at], back)
        if index == 0:
            local_grad[...] = edge_grad
            by_owner = dot(send_t[...], send_grad)
            local_keep[...] = by_owner[0 : PART // 2, :]
            local_send[...] = by_owner[PART // 2 : PART, :].astype(BF16)
        else:
            cut_grad[row - LOC : row - LOC + count, :] = edge_grad
            summed = dot(pick_t[index - 1], send_grad)
            for dz in range(2):
                for x in range(X):
                    start = (dz * X + x) * C * BORDER
                    near = summed[start : start + BORDER, :]
                    far = summed[start + BORDER : start + 2 * BORDER, :]
                    to = ((2 * (index - 1) + dz) * X + x) * BORDER
                    keep[to : to + BORDER, :] = jnp.where(is_first, near, far)
                    send[to : to + BORDER, :] = jnp.where(is_first, far, near).astype(BF16)
    upper, lower = split(received)
    both = dot_t(jnp.concatenate([upper, lower], axis=0), w1[2 * D : 3 * D, :])
    own_grad[...] = result + both[0:OWN, :] + both[OWN : 2 * OWN, :]


def shape(*dims, kind=BF16):
    return jax.ShapeDtypeStruct(dims, kind)


VMEM = pl.BlockSpec(memory_space=pltpu.VMEM)
SMEM = pl.BlockSpec(memory_space=pltpu.SMEM)
HBM = pl.BlockSpec(memory_space=pltpu.HBM)
ANY = pl.BlockSpec(memory_space=pl.ANY)


def index(*args):
    return pl.pallas_call(
        index_body,
        in_specs=[SMEM] + [VMEM] * 14,
        out_specs=[VMEM] * 6,
        out_shape=[
            shape(LOC, D), shape(ALL, 256), shape(OWN, ALL), shape(PART, LOC), shape(OWN, D), shape(8, D, kind=F32),
        ],
        compiler_params=pltpu.CompilerParams(vmem_limit_bytes=LIMIT),
        cost_estimate=pl.CostEstimate(flops=200_000_000, bytes_accessed=3_000_000, transcendentals=0),
        name="index",
    )(*args)


def pick(*args):
    return pl.pallas_call(
        pick_body,
        in_specs=[SMEM, VMEM, VMEM],
        out_specs=[VMEM] * 2,
        out_shape=[shape(CUT, D), shape(GROUPS, GROUP, GROUP)],
        scratch_shapes=[pltpu.VMEM((Z * X * C, D), F32)],
        compiler_params=pltpu.CompilerParams(vmem_limit_bytes=LIMIT),
        cost_estimate=pl.CostEstimate(flops=300_000_000, bytes_accessed=4_000_000, transcendentals=0),
        name="pick",
    )(*args)


def layer(*args):
    return pl.pallas_call(
        layer_body,
        in_specs=[SMEM] + [ANY] * 4 + [VMEM] * 9,
        out_specs=[VMEM] * 8,
        out_shape=[
            shape(OWN, D), shape(LOC, D), shape(CUT, D), shape(OWN, D, kind=F32),
            shape(CUT // 2, D, kind=F32), shape(CUT // 2, D),
            shape(PART // 2, D, kind=F32), shape(PART // 2, D),
        ],
        scratch_shapes=[
            pltpu.VMEM((3 * D, D), BF16),
            pltpu.VMEM((D, D), BF16),
            pltpu.VMEM((2 * D, D), BF16),
            pltpu.VMEM((D, D), BF16),
            pltpu.VMEM((ALL, D), BF16),
            pltpu.VMEM((ALL, D), F32),
            pltpu.VMEM((ALL, D), F32),
            pltpu.VMEM((ALL, 1), F32),
            pltpu.SemaphoreType.DMA((4, F, 2)),
            pltpu.SemaphoreType.DMA((2,)),
        ],
        compiler_params=pltpu.CompilerParams(vmem_limit_bytes=LIMIT),
        cost_estimate=pl.CostEstimate(flops=4_000_000_000, bytes_accessed=12_000_000, transcendentals=600_000),
        name="layer",
    )(*args)


def after_body(values, other, out):
    del values, other, out


def after(values, other):
    return pl.pallas_call(
        after_body,
        in_specs=[HBM, ANY],
        out_specs=HBM,
        out_shape=jax.ShapeDtypeStruct(values.shape, values.dtype),
        input_output_aliases={0: 0},
        cost_estimate=pl.CostEstimate(flops=0, bytes_accessed=0, transcendentals=0),
        name="after",
    )(values, other)


def pack_body(core, first, second, third, fourth, out, half, sems):
    start = 0
    for ref in (first, second, third, fourth):
        size = ref.shape[0] // C
        half[start : start + size, :] = ref[pl.ds(pl.multiple_of(core[0] * size, 32), size), :]
        start += size
    copies = [pltpu.make_async_copy(half, out.at[f], sems.at[f]) for f in range(F)]
    for copy in copies:
        copy.start()
    for copy in copies:
        copy.wait()


def pack(core, *parts):
    rows = sum(part.shape[0] for part in parts) // C
    return pl.pallas_call(
        pack_body,
        in_specs=[SMEM] + [VMEM] * 4,
        out_specs=HBM,
        out_shape=shape(F, rows, D),
        scratch_shapes=[pltpu.VMEM((rows, D), BF16), pltpu.SemaphoreType.DMA((F,))],
        compiler_params=pltpu.CompilerParams(vmem_limit_bytes=LIMIT),
        cost_estimate=pl.CostEstimate(flops=0, bytes_accessed=2_000_000, transcendentals=0),
        name="pack",
    )(core, *parts)


def shift(values, axis, size, step):
    return lax.ppermute(values, axis, [(i, (i + step) % size) for i in range(size)])


def exchange(values, axis):
    return lax.all_to_all(values, axis, split_axis=0, concat_axis=0, tiled=True)


def shards(
    node_in, local_edges, cut_edges, node_cot, edge_w1, edge_w2, node_w1, node_w2,
    edge_b1, edge_b2, edge_gain, edge_shift, node_b1, node_b2, node_gain, node_shift,
    local_send, local_recv, cut_send, cut_recv, cut_count,
):
    feat = lax.axis_index("feat")
    core = lax.axis_index("core")
    weights = exchange(pack(core.astype(jnp.int32).reshape(1), edge_w1, edge_w2, node_w1, node_w2), "feat")
    selectors = cut_send[0, 0].astype(BF16).reshape(2, D)
    selectors = jnp.pad(selectors, ((0, PACK - BORDER - 2), (0, 0)))
    payload = jnp.concatenate([node_in[:BORDER], selectors], axis=0)
    payload = jnp.stack([shift(payload, "z", Z, Z - 1), payload, shift(payload, "z", Z, 1)])
    payload = jnp.concatenate([payload, shift(payload, "z", Z, 3), shift(payload[1:], "z", Z, Z - 3)], axis=0)
    near = jnp.stack([payload] + [shift(payload, "x", X, step) for step in range(1, X)])
    far = shift(near, "core", C, 1)
    owner = jnp.bitwise_xor(local_send // OWN, feat.astype(jnp.int32))
    owner = (owner & 1) * 4 + (owner & 2) + (owner >> 2)
    relative = owner * OWN + local_send % OWN
    vectors = (edge_b1, edge_b2, edge_gain, edge_shift, node_b1, node_b2, node_gain, node_shift)
    indices = index(
        feat.astype(jnp.int32).reshape(1), node_in, local_send[None, :], relative[None, :], local_recv[None, :],
        cut_recv[0], cut_count[0], *[v[None, :] for v in vectors],
    )
    place = jnp.stack([lax.axis_index(axis) for axis in DOM]).astype(jnp.int32)
    cut_senders, pick_t = pick(place, near, far)
    weights = after(weights, cut_senders)
    other_weights = shift(weights, "core", C, 1)
    node_out, local_grad, cut_grad, own_grad, keep, send, local_keep, local_sums = layer(
        core.astype(jnp.int32).reshape(1), weights, other_weights, local_edges, cut_edges, node_cot,
        *indices, cut_senders, pick_t,
    )
    summed = keep + lax.ppermute(send, "core", [(0, 1), (1, 0)]).astype(F32)
    for distance in (1, 2, 4):
        if distance > 1:
            half = local_keep.shape[0] // 2
            local_keep, local_sums = local_keep[:half], local_keep[half:].astype(BF16)
        arrived = lax.ppermute(local_sums, "feat", [(f, f ^ distance) for f in range(F)])
        local_keep = local_keep + arrived.astype(F32)
    summed = summed.astype(BF16)
    summed = exchange(summed.reshape(Z * X, BORDER, D), ("z", "x"))
    summed = jnp.sum(summed.astype(F32), axis=0).astype(BF16)
    summed = exchange(jnp.broadcast_to(summed[None], (F, BORDER, D)), "feat")
    summed = jnp.where(feat == 0, jnp.sum(summed.astype(F32), axis=0), 0.0)
    node_grad = own_grad + local_keep + jnp.pad(summed, ((0, OWN - BORDER), (0, 0)))
    return node_out, node_grad, local_grad, cut_grad


def solution(mesh):
    split_mesh = Mesh(mesh.devices.reshape(Z, X, C, F), (*DOM, "feat"))
    both = (*DOM, "feat")
    placed = (
        P(DOM, None),
        *[P(both, None)] * 3,
        *[P("feat", None)] * 4,
        *[P()] * 8,
        *[P(both)] * 2,
        *[P(DOM, "feat", None)] * 3,
    )
    return jax.shard_map(
        shards,
        mesh=split_mesh,
        in_specs=placed,
        out_specs=(P(both, None),) * 4,
        check_vma=False,
    )
```

time: 151 us -> 139 us (0.921)
  starting transfers between devices: 13.1 us -> 73.5 us
  blocking collectives: 49.1 us -> 0 us
  between operations: 14.4 us -> 0.97 us
  local copies, waits for them, and re-layouts: 16.1 us -> 4.84 us
  Pallas kernels: 19 us -> 25.3 us
  waiting for transfers between devices: 32.8 us -> 28.4 us
    all_to_all x3 -> x0, blocking collectives: 49.1 us -> none  [exchange(): return lax.all_to_all(values, axis, split_axis=0, concat_axis=0, tiled=True)]
    ppermute x1 -> x12, starting transfers between devices: 1.91 us -> 49.3 us  [the longest x9 34.8 us: shift(): lax.ppermute(values, axis, [(i, (i + step) % size) for i in range(size)])]
    ppermute x1 -> x12, waiting for transfers between devices: 1.12 us -> 23.3 us  [the longest x9 12.9 us: shift(): lax.ppermute(values, axis, [(i, (i + step) % size) for i in range(size)])]
    all_gather x1 -> x0, waiting for transfers between devices: 14.3 us -> none  [shards(): weights = lax.all_gather(packed, 'feat', axis=0, tiled=False)]
    all_to_all x2 -> x3, starting transfers between devices: 9.26 us -> 21.9 us  [exchange(): return lax.all_to_all(values, axis, split_axis=0, concat_axis=0, tiled=True)]
    all_to_all x2 -> x3, waiting for transfers between devices: 15.4 us -> 3.19 us  [exchange(): return lax.all_to_all(values, axis, split_axis=0, concat_axis=0, tiled=True)]
    unnamed x50 -> x21, local copies, waits for them, and re-layouts: 12.5 us -> 3.4 us
    pallas_call x2 -> x5, Pallas kernels: 19 us -> 25.3 us  [the longest x1 17.2 us: layer(): pl.pallas_call(layer_body, in_specs=[SMEM] + [ANY] * 4 + [VMEM] * 9, out_...]
  transfers between devices with their start and end apart: 6 -> 16, of which waited for: 5 -> 10; matrix products, arithmetic and copies ran while one was open for 4% -> 2% of each run, Pallas kernels for 1% -> 4%
where the time goes in v2:
time: 139 us; the launch traced here: 137 us
  starting transfers between devices  73.5 us (53%)
  waiting for transfers between devices  28.4 us (20%)
  Pallas kernels  25.3 us (18%)
  local copies, waits for them, and re-layouts  4.84 us (3%)
  other arithmetic  4.39 us (3%)
    ppermute x9, starting transfers between devices, shift(): lax.ppermute(values, axis, [(i, (i + step) % size) for i in range(size)])  34.8 us
    all_to_all x3, starting transfers between devices, exchange(): return lax.all_to_all(values, axis, split_axis=0, concat_axis=0, tiled=True)  21.9 us
    pallas_call x1, Pallas kernels, layer(): pl.pallas_call(layer_body, in_specs=[SMEM] + [ANY] * 4 + [VMEM] * 9, out_...  17.2 us
    ppermute x3, starting transfers between devices, shards(): lax.ppermute(local_sums, 'feat', [(f, f ^ distance) for f in range(F)])  14.5 us
    ppermute x9, waiting for transfers between devices, shift(): lax.ppermute(values, axis, [(i, (i + step) % size) for i in range(size)])  12.9 us
    ppermute x3, waiting for transfers between devices, shards(): lax.ppermute(local_sums, 'feat', [(f, f ^ distance) for f in range(F)])  10.4 us
    unnamed x21, local copies, waits for them, and re-layouts  3.4 us
    all_to_all x3, waiting for transfers between devices, exchange(): return lax.all_to_all(values, axis, split_axis=0, concat_axis=0, tiled=True)  3.19 us
  transfers between devices with their start and end apart: 16, of which 10 were waited for; matrix products, arithmetic and copies ran while one was open for 2% of the time, Pallas kernels for 4%

profile of v2, /device:TPU:6, one launch (start us, length us, event | category | flops | bytes accessed | tf_op | source)
XLA Modules:
  0.0 137.4 jit_solution(15103023269828952874)
XLA Ops:
  0.6 2.4 %pack.1 = bf16[8,224,512]{2,1,0:T(8,128)(2,1)} custom-call(s32[1]{0:T(128)} %bitcast.core, bf16[192,512]{1,0:T(8,128)(2,1)} %first.1, bf16[64,512]{1,0:T(8,128)(2,1)} %second.1, bf16[128,512]{1,0:T(8,128)(2,1)} %third.1, bf16[64,512]{1,0:T(8,128)(2,1)} %fourth.1), custom_call_target="tpu_custom_call" | custom-call | bytes 2000000 | tf_op jit(solution)/shard_map/pack/pallas_call | solution.py:314
  3.0 0.0 copy-start.5
  3.1 7.1 %all-to-all-start = ((bf16[8,224,512]{2,1,0:T(8,128)(2,1)}), bf16[8,224,512]{2,1,0:T(8,128)(2,1)S(1)}, u32[]{:S(2)}, u32[]{:S(2)}) async-start(bf16[8,224,512]{2,1,0:T(8,128)(2,1)} %pack.1), calls=%async_computation | async-start | bytes 3670016 | tf_op jit(solution)/shard_map/all_to_all | solution.py:331
  10.2 0.0 copy-done.5
  10.2 0.7 slice.19
  10.9 4.3 %collective-permute-start.1 = (bf16[24,512]{1,0:T(8,128)(2,1)S(1)}, bf16[24,512]{1,0:T(8,128)(2,1)S(1)}, u32[]{:S(2)}, u32[]{:S(2)}) collective-permute-start(bf16[24,512]{1,0:T(8,128)(2,1)S(1)} %get-tuple-element.37), channel_id=1, source_target_pairs={{0,64},{64,128},{128,192},{192,256},{256,320},{320,384},{384,448},... | collective-permute-start | bytes 73736 | tf_op jit(solution)/shard_map/ppermute | solution.py:327
  15.2 8.6 %collective-permute-start = (bf16[24,512]{1,0:T(8,128)(2,1)S(1)}, bf16[24,512]{1,0:T(8,128)(2,1)S(1)}, u32[]{:S(2)}, u32[]{:S(2)}) collective-permute-start(bf16[24,512]{1,0:T(8,128)(2,1)S(1)} %get-tuple-element.37), channel_id=1, source_target_pairs={{0,448},{64,0},{128,64},{192,128},{256,192},{320,256},{384,320},{4... | collective-permute-start | bytes 73736 | tf_op jit(solution)/shard_map/ppermute | solution.py:327
  23.8 0.0 collective-permute-done.1
  23.8 3.9 %collective-permute-start.3 = (bf16[2,24,512]{2,1,0:T(8,128)(2,1)S(1)}, bf16[2,24,512]{2,1,0:T(8,128)(2,1)S(1)}, u32[]{:S(2)}, u32[]{:S(2)}) collective-permute-start(bf16[2,24,512]{2,1,0:T(8,128)(2,1)S(1)} %pad_maximum_fusion.2), channel_id=1, source_target_pairs={{0,320},{64,384},{128,448},{192,0},{256,64},{320,128},{384,192},{4... | collective-permute-start | bytes 147464 | tf_op jit(solution)/shard_map/ppermute | solution.py:327
  27.8 0.0 collective-permute-done
  27.8 4.2 %collective-permute-start.2 = (bf16[3,24,512]{2,1,0:T(8,128)(2,1)S(1)}, bf16[3,24,512]{2,1,0:T(8,128)(2,1)S(1)}, u32[]{:S(2)}, u32[]{:S(2)}) collective-permute-start(bf16[3,24,512]{2,1,0:T(8,128)(2,1)S(1)} %pad_maximum_fusion.1), channel_id=1, source_target_pairs={{0,192},{64,256},{128,320},{192,384},{256,448},{320,0},{384,64},{4... | collective-permute-start | bytes 221192 | tf_op jit(solution)/shard_map/ppermute | solution.py:327
  32.1 6.7 %collective-permute-done.2 = bf16[3,24,512]{2,1,0:T(8,128)(2,1)S(1)} collective-permute-done((bf16[3,24,512]{2,1,0:T(8,128)(2,1)S(1)}, bf16[3,24,512]{2,1,0:T(8,128)(2,1)S(1)}, u32[]{:S(2)}, u32[]{:S(2)}) %collective-permute-start.2) | collective-permute-done | bytes 73760 | tf_op jit(solution)/shard_map/ppermute | solution.py:327
  38.8 0.0 collective-permute-done.3
  38.8 2.7 %collective-permute-start.6 = (bf16[8,24,512]{2,1,0:T(8,128)(2,1)S(1)}, bf16[8,24,512]{2,1,0:T(8,128)(2,1)S(1)}, u32[]{:S(2)}, u32[]{:S(2)}) collective-permute-start(bf16[8,24,512]{2,1,0:T(8,128)(2,1)S(1)} %constant_dynamic-update-slice_fusion), channel_id=1, source_target_pairs={{0,48},{16,0},{32,16},{48,32},{1,49},{17,1},{33,17},{49,33},{2,50}... | collective-permute-start | bytes 589832 | tf_op jit(solution)/shard_map/ppermute | solution.py:327
  41.5 3.0 %collective-permute-start.5 = (bf16[8,24,512]{2,1,0:T(8,128)(2,1)S(1)}, bf16[8,24,512]{2,1,0:T(8,128)(2,1)S(1)}, u32[]{:S(2)}, u32[]{:S(2)}) collective-permute-start(bf16[8,24,512]{2,1,0:T(8,128)(2,1)S(1)} %constant_dynamic-update-slice_fusion), channel_id=1, source_target_pairs={{0,32},{16,48},{32,0},{48,16},{1,33},{17,49},{33,1},{49,17},{2,34}... | collective-permute-start | bytes 589832 | tf_op jit(solution)/shard_map/ppermute | solution.py:327
  44.5 4.0 %collective-permute-start.4 = (bf16[8,24,512]{2,1,0:T(8,128)(2,1)S(1)}, bf16[8,24,512]{2,1,0:T(8,128)(2,1)S(1)}, u32[]{:S(2)}, u32[]{:S(2)}) collective-permute-start(bf16[8,24,512]{2,1,0:T(8,128)(2,1)S(1)} %constant_dynamic-update-slice_fusion), channel_id=1, source_target_pairs={{0,16},{16,32},{32,48},{48,0},{1,17},{17,33},{33,49},{49,1},{2,18}... | collective-permute-start | bytes 589832 | tf_op jit(solution)/shard_map/ppermute | solution.py:327
  48.6 2.4 %collective-permute-done.6 = bf16[8,24,512]{2,1,0:T(8,128)(2,1)S(1)} collective-permute-done((bf16[8,24,512]{2,1,0:T(8,128)(2,1)S(1)}, bf16[8,24,512]{2,1,0:T(8,128)(2,1)S(1)}, u32[]{:S(2)}, u32[]{:S(2)}) %collective-permute-start.6) | collective-permute-done | bytes 196640 | tf_op jit(solution)/shard_map/ppermute | solution.py:327
  50.9 0.0 collective-permute-done.5
  50.9 1.5 %collective-permute-done.4 = bf16[8,24,512]{2,1,0:T(8,128)(2,1)S(1)} collective-permute-done((bf16[8,24,512]{2,1,0:T(8,128)(2,1)S(1)}, bf16[8,24,512]{2,1,0:T(8,128)(2,1)S(1)}, u32[]{:S(2)}, u32[]{:S(2)}) %collective-permute-start.4) | collective-permute-done | bytes 196640 | tf_op jit(solution)/shard_map/ppermute | solution.py:327
  52.4 0.1 pad_maximum_fusion.near
  52.5 0.0 copy-start.1
  52.5 1.9 %collective-permute-start.7 = (bf16[4,8,24,512]{3,2,1,0:T(8,128)(2,1)S(1)}, bf16[4,8,24,512]{3,2,1,0:T(8,128)(2,1)S(1)}, u32[]{:S(2)}, u32[]{:S(2)}) collective-permute-start(bf16[4,8,24,512]{3,2,1,0:T(8,128)(2,1)S(1)} %pad_maximum_fusion.near), channel_id=1, source_target_pairs={{0,8},{8,0},{1,9},{9,1},{2,10},{10,2},{3,11},{11,3},{4,12},{12,4},... | collective-permute-start | bytes 2359304 | tf_op jit(solution)/shard_map/ppermute | solution.py:327
  54.5 0.6 pad_add_fusion.where
  55.1 1.7 %collective-permute-done.7.far = bf16[4,8,24,512]{3,2,1,0:T(8,128)(2,1)S(1)} collective-permute-done((bf16[4,8,24,512]{3,2,1,0:T(8,128)(2,1)S(1)}, bf16[4,8,24,512]{3,2,1,0:T(8,128)(2,1)S(1)}, u32[]{:S(2)}, u32[]{:S(2)}) %collective-permute-start.7) | collective-permute-done | bytes 786464 | tf_op jit(solution)/shard_map/ppermute | solution.py:327
  56.7 0.0 copy-done.1
  56.7 0.0 copy-start.2
  56.7 0.9 copy-done.2
  57.6 3.1 %pick.1 = (bf16[1024,512]{1,0:T(8,128)(2,1)}, bf16[4,256,256]{2,1,0:T(8,128)(2,1)}) custom-call(s32[3]{0:T(128)} %pad_add_fusion.where, bf16[4,8,24,512]{3,2,1,0:T(8,128)(2,1)} %copy-done.1, bf16[4,8,24,512]{3,2,1,0:T(8,128)(2,1)} %copy-done.2), custom_call_target="tpu_custom_call" | custom-call | flops 300000000 | bytes 4000000 | tf_op jit(solution)/shard_map/pick/pallas_call | solution.py:243
  60.7 0.0 all-to-all-done.values
  60.7 0.0 copy-start
  60.7 1.2 copy-done
  61.9 0.0 copy-start.8
  61.9 2.2 %collective-permute-start.8 = (bf16[8,224,512]{2,1,0:T(8,128)(2,1)}, bf16[8,224,512]{2,1,0:T(8,128)(2,1)S(1)}, u32[]{:S(2)}, u32[]{:S(2)}) collective-permute-start(bf16[8,224,512]{2,1,0:T(8,128)(2,1)} %after.1.mine), channel_id=1, source_target_pairs={{0,8},{8,0},{1,9},{9,1},{2,10},{10,2},{3,11},{11,3},{4,12},{12,4},... | collective-permute-start | bytes 5505032 | tf_op jit(solution)/shard_map/ppermute | solution.py:327
  64.1 0.0 copy-done.8
  64.1 0.5 fusion.5.moved
  64.7 2.6 %index.1 = (bf16[128,512]{1,0:T(8,128)(2,1)}, bf16[1152,256]{1,0:T(8,128)(2,1)}, bf16[80,1152]{1,0:T(8,128)(2,1)}, bf16[640,128]{1,0:T(8,128)(2,1)}, bf16[80,512]{1,0:T(8,128)(2,1)}, /*index=5*/f32[8,512]{1,0:T(8,128)}) custom-call(s32[1]{0:T(128)} %bitcast.10.feat, bf16[640,512]{1,0:T(8,128)(2,1)} %nodes.1, s32[1,128]{1,0:T(1,128)} %bitcast.46, ...), custom_call_target="tpu_custom_call" | custom-call | flops 200000000 | bytes 3000000 | tf_op jit(solution)/shard_map/index/pallas_call | solution.py:229
  67.3 0.7 collective-permute-done.8.other
  67.9 0.0 copy-start.6
  67.9 1.3 copy-done.6
  69.2 17.2 %layer.1 = (bf16[80,512]{1,0:T(8,128)(2,1)}, bf16[128,512]{1,0:T(8,128)(2,1)}, bf16[1024,512]{1,0:T(8,128)(2,1)}, f32[80,512]{1,0:T(8,128)}, f32[512,512]{1,0:T(...) custom-call(s32[1]{0:T(128)} %bitcast.core, bf16[8,224,512]{2,1,0:T(8,128)(2,1)} %after.1.mine, ...), custom_call_target="tpu_custom_call" | custom-call | flops 4000000000 | bytes 12000000 | tf_op jit(solution)/shard_map/layer/pallas_call | solution.py:256
  86.4 0.0 copy-start.7
  86.4 0.0 copy-start.3
  86.4 2.2 %collective-permute-start.12 = (bf16[512,512]{1,0:T(8,128)(2,1)}, bf16[512,512]{1,0:T(8,128)(2,1)S(1)}, u32[]{:S(2)}, u32[]{:S(2)}) collective-permute-start(bf16[512,512]{1,0:T(8,128)(2,1)} %get-tuple-element.33), channel_id=1, source_target_pairs={{0,8},{8,0},{1,9},{9,1},{2,10},{10,2},{3,11},{11,3},{4,12},{12,4},... | collective-permute-start | bytes 1572872 | tf_op jit(solution)/shard_map/ppermute | solution.py:365
  88.7 1.9 %collective-permute-done.12 = bf16[512,512]{1,0:T(8,128)(2,1)S(1)} collective-permute-done((bf16[512,512]{1,0:T(8,128)(2,1)}, bf16[512,512]{1,0:T(8,128)(2,1)S(1)}, u32[]{:S(2)}, u32[]{:S(2)}) %collective-permute-start.12) | collective-permute-done | bytes 524320 | tf_op jit(solution)/shard_map/ppermute | solution.py:365
  90.6 2.2 %add_convert_fusion = bf16[512,512]{1,0:T(8,128)(2,1)} fusion(f32[512,512]{1,0:T(8,128)} %get-tuple-element.32, bf16[512,512]{1,0:T(8,128)(2,1)S(1)} %collective-permute-done.12), kind=kLoop, calls=%fused_computation | loop fusion | flops 786432 | bytes 2097152 | tf_op jit(solution)/shard_map/convert_element_type | solution.py:372
  92.8 8.8 %all-to-all-start.1 = ((bf16[32,16,512]{2,1,0:T(8,128)(2,1)}), bf16[32,16,512]{2,1,0:T(8,128)(2,1)S(1)}, u32[]{:S(2)}, u32[]{:S(2)}) async-start(bf16[32,16,512]{2,1,0:T(8,128)(2,1)} %bitcast.24), calls=%async_computation.1 | async-start | bytes 1048576 | tf_op jit(solution)/shard_map/all_to_all | solution.py:331
  101.6 0.0 copy-done.7
  101.6 2.7 %collective-permute-start.9 = (bf16[320,512]{1,0:T(8,128)(2,1)S(1)}, bf16[320,512]{1,0:T(8,128)(2,1)S(1)}, u32[]{:S(2)}, u32[]{:S(2)}) collective-permute-start(bf16[320,512]{1,0:T(8,128)(2,1)S(1)} %copy-done.7), channel_id=1, source_target_pairs={{0,1},{1,0},{2,3},{3,2},{4,5},{5,4},{6,7},{7,6},{8,9},{9,8},{10,11... | collective-permute-start | bytes 983048 | tf_op jit(solution)/shard_map/ppermute | solution.py:370
  104.3 8.4 %collective-permute-done.9 = bf16[320,512]{1,0:T(8,128)(2,1)S(1)} collective-permute-done((bf16[320,512]{1,0:T(8,128)(2,1)S(1)}, bf16[320,512]{1,0:T(8,128)(2,1)S(1)}, u32[]{:S(2)}, u32[]{:S(2)}) %collective-permute-start.9) | collective-permute-done | bytes 327712 | tf_op jit(solution)/shard_map/ppermute | solution.py:370
  112.7 0.0 copy-done.3
  112.7 0.0 copy-start.4
  112.7 0.1 convert_add_fusion
  112.8 3.9 %collective-permute-start.10 = (bf16[160,512]{1,0:T(8,128)(2,1)S(1)}, bf16[160,512]{1,0:T(8,128)(2,1)S(1)}, u32[]{:S(2)}, u32[]{:S(2)}) collective-permute-start(bf16[160,512]{1,0:T(8,128)(2,1)S(1)} %slice.36), channel_id=1, source_target_pairs={{0,2},{1,3},{2,0},{3,1},{4,6},{5,7},{6,4},{7,5},{8,10},{9,11},{10,... | collective-permute-start | bytes 491528 | tf_op jit(solution)/shard_map/ppermute | solution.py:370
  116.8 2.0 %all-to-all-done.1 = bf16[32,16,512]{2,1,0:T(8,128)(2,1)S(1)} async-done(((bf16[32,16,512]{2,1,0:T(8,128)(2,1)}), bf16[32,16,512]{2,1,0:T(8,128)(2,1)S(1)}, u32[]{:S(2)}, u32[]{:S(2)}) %all-to-all-start.1) | async-done | bytes 524320 | tf_op jit(solution)/shard_map/all_to_all | solution.py:331
  118.7 0.1 reduce_sum.21
  118.8 0.7 broadcast_in_dim.54
  119.5 6.0 %all-to-all-start.2 = ((bf16[8,16,512]{2,1,0:T(8,128)(2,1)}), bf16[8,16,512]{2,1,0:T(8,128)(2,1)S(1)}, u32[]{:S(2)}, u32[]{:S(2)}) async-start(bf16[8,16,512]{2,1,0:T(8,128)(2,1)} %broadcast_in_dim.54), calls=%async_computation.2 | async-start | bytes 262144 | tf_op jit(solution)/shard_map/all_to_all | solution.py:331
  125.5 0.0 collective-permute-done.10
  125.6 7.8 %collective-permute-start.11 = (bf16[80,512]{1,0:T(8,128)(2,1)S(1)}, bf16[80,512]{1,0:T(8,128)(2,1)S(1)}, u32[]{:S(2)}, u32[]{:S(2)}) collective-permute-start(bf16[80,512]{1,0:T(8,128)(2,1)S(1)} %slice.37), channel_id=1, source_target_pairs={{0,4},{1,5},{2,6},{3,7},{4,0},{5,1},{6,2},{7,3},{8,12},{9,13},{10,... | collective-permute-start | bytes 245768 | tf_op jit(solution)/shard_map/ppermute | solution.py:370
  133.4 1.2 all-to-all-done.2
  134.7 2.0 %collective-permute-done.11 = bf16[80,512]{1,0:T(8,128)(2,1)S(1)} collective-permute-done((bf16[80,512]{1,0:T(8,128)(2,1)S(1)}, bf16[80,512]{1,0:T(8,128)(2,1)S(1)}, u32[]{:S(2)}, u32[]{:S(2)}) %collective-permute-start.11) | collective-permute-done | bytes 81952 | tf_op jit(solution)/shard_map/ppermute | solution.py:370
  136.7 0.0 copy-done.4
  136.7 0.7 fusion.1
  (16 shorter events, 0.2 us)
Async XLA Ops:
  3.0 7.1 %copy-start.5 = (s32[1,1,1024]{2,1,0:T(1,128)S(1)}, s32[1,1,1024]{2,1,0:T(1,128)}, u32[]{:S(2)}) copy-start(s32[1,1,1024]{2,1,0:T(1,128)} %param.39) | copy-start | bytes 12292
  3.1 57.6 %all-to-all-start = ((bf16[8,224,512]{2,1,0:T(8,128)(2,1)}), bf16[8,224,512]{2,1,0:T(8,128)(2,1)S(1)}, u32[]{:S(2)}, u32[]{:S(2)}) async-start(bf16[8,224,512]{2,1,0:T(8,128)(2,1)} %pack.1), calls=%async_computation | async-start | bytes 3670016 | tf_op jit(solution)/shard_map/all_to_all | solution.py:331
  10.9 12.9 %collective-permute-start.1 = (bf16[24,512]{1,0:T(8,128)(2,1)S(1)}, bf16[24,512]{1,0:T(8,128)(2,1)S(1)}, u32[]{:S(2)}, u32[]{:S(2)}) collective-permute-start(bf16[24,512]{1,0:T(8,128)(2,1)S(1)} %get-tuple-element.37), channel_id=1, source_target_pairs={{0,64},{64,128},{128,192},{192,256},{256,320},{320,384},{384,448},... | collective-permute-start | bytes 73736 | tf_op jit(solution)/shard_map/ppermute | solution.py:327
  15.2 12.5 %collective-permute-start = (bf16[24,512]{1,0:T(8,128)(2,1)S(1)}, bf16[24,512]{1,0:T(8,128)(2,1)S(1)}, u32[]{:S(2)}, u32[]{:S(2)}) collective-permute-start(bf16[24,512]{1,0:T(8,128)(2,1)S(1)} %get-tuple-element.37), channel_id=1, source_target_pairs={{0,448},{64,0},{128,64},{192,128},{256,192},{320,256},{384,320},{4... | collective-permute-start | bytes 73736 | tf_op jit(solution)/shard_map/ppermute | solution.py:327
  23.8 14.9 %collective-permute-start.3 = (bf16[2,24,512]{2,1,0:T(8,128)(2,1)S(1)}, bf16[2,24,512]{2,1,0:T(8,128)(2,1)S(1)}, u32[]{:S(2)}, u32[]{:S(2)}) collective-permute-start(bf16[2,24,512]{2,1,0:T(8,128)(2,1)S(1)} %pad_maximum_fusion.2), channel_id=1, source_target_pairs={{0,320},{64,384},{128,448},{192,0},{256,64},{320,128},{384,192},{4... | collective-permute-start | bytes 147464 | tf_op jit(solution)/shard_map/ppermute | solution.py:327
  27.8 11.0 %collective-permute-start.2 = (bf16[3,24,512]{2,1,0:T(8,128)(2,1)S(1)}, bf16[3,24,512]{2,1,0:T(8,128)(2,1)S(1)}, u32[]{:S(2)}, u32[]{:S(2)}) collective-permute-start(bf16[3,24,512]{2,1,0:T(8,128)(2,1)S(1)} %pad_maximum_fusion.1), channel_id=1, source_target_pairs={{0,192},{64,256},{128,320},{192,384},{256,448},{320,0},{384,64},{4... | collective-permute-start | bytes 221192 | tf_op jit(solution)/shard_map/ppermute | solution.py:327
  38.8 12.2 %collective-permute-start.6 = (bf16[8,24,512]{2,1,0:T(8,128)(2,1)S(1)}, bf16[8,24,512]{2,1,0:T(8,128)(2,1)S(1)}, u32[]{:S(2)}, u32[]{:S(2)}) collective-permute-start(bf16[8,24,512]{2,1,0:T(8,128)(2,1)S(1)} %constant_dynamic-update-slice_fusion), channel_id=1, source_target_pairs={{0,48},{16,0},{32,16},{48,32},{1,49},{17,1},{33,17},{49,33},{2,50}... | collective-permute-start | bytes 589832 | tf_op jit(solution)/shard_map/ppermute | solution.py:327
  41.5 9.4 %collective-permute-start.5 = (bf16[8,24,512]{2,1,0:T(8,128)(2,1)S(1)}, bf16[8,24,512]{2,1,0:T(8,128)(2,1)S(1)}, u32[]{:S(2)}, u32[]{:S(2)}) collective-permute-start(bf16[8,24,512]{2,1,0:T(8,128)(2,1)S(1)} %constant_dynamic-update-slice_fusion), channel_id=1, source_target_pairs={{0,32},{16,48},{32,0},{48,16},{1,33},{17,49},{33,1},{49,17},{2,34}... | collective-permute-start | bytes 589832 | tf_op jit(solution)/shard_map/ppermute | solution.py:327
  44.5 7.9 %collective-permute-start.4 = (bf16[8,24,512]{2,1,0:T(8,128)(2,1)S(1)}, bf16[8,24,512]{2,1,0:T(8,128)(2,1)S(1)}, u32[]{:S(2)}, u32[]{:S(2)}) collective-permute-start(bf16[8,24,512]{2,1,0:T(8,128)(2,1)S(1)} %constant_dynamic-update-slice_fusion), channel_id=1, source_target_pairs={{0,16},{16,32},{32,48},{48,0},{1,17},{17,33},{33,49},{49,1},{2,18}... | collective-permute-start | bytes 589832 | tf_op jit(solution)/shard_map/ppermute | solution.py:327
  52.5 4.2 %copy-start.1 = (bf16[4,8,24,512]{3,2,1,0:T(8,128)(2,1)}, bf16[4,8,24,512]{3,2,1,0:T(8,128)(2,1)S(1)}, u32[]{:S(2)}) copy-start(bf16[4,8,24,512]{3,2,1,0:T(8,128)(2,1)S(1)} %pad_maximum_fusion.near) | copy-start | bytes 2359300
  52.5 4.2 %collective-permute-start.7 = (bf16[4,8,24,512]{3,2,1,0:T(8,128)(2,1)S(1)}, bf16[4,8,24,512]{3,2,1,0:T(8,128)(2,1)S(1)}, u32[]{:S(2)}, u32[]{:S(2)}) collective-permute-start(bf16[4,8,24,512]{3,2,1,0:T(8,128)(2,1)S(1)} %pad_maximum_fusion.near), channel_id=1, source_target_pairs={{0,8},{8,0},{1,9},{9,1},{2,10},{10,2},{3,11},{11,3},{4,12},{12,4},... | collective-permute-start | bytes 2359304 | tf_op jit(solution)/shard_map/ppermute | solution.py:327
  56.7 0.9 copy-start.2
  60.7 1.2 copy-start
  61.9 2.2 %copy-start.8 = (s32[128]{0:T(128)S(1)}, s32[128]{0:T(128)}, u32[]{:S(2)}) copy-start(s32[128]{0:T(128)} %param.37) | copy-start | bytes 1540
  61.9 6.0 %collective-permute-start.8 = (bf16[8,224,512]{2,1,0:T(8,128)(2,1)}, bf16[8,224,512]{2,1,0:T(8,128)(2,1)S(1)}, u32[]{:S(2)}, u32[]{:S(2)}) collective-permute-start(bf16[8,224,512]{2,1,0:T(8,128)(2,1)} %after.1.mine), channel_id=1, source_target_pairs={{0,8},{8,0},{1,9},{9,1},{2,10},{10,2},{3,11},{11,3},{4,12},{12,4},... | collective-permute-start | bytes 5505032 | tf_op jit(solution)/shard_map/ppermute | solution.py:327
  67.9 1.3 copy-start.6
  86.4 15.2 %copy-start.7 = (bf16[320,512]{1,0:T(8,128)(2,1)S(1)}, bf16[320,512]{1,0:T(8,128)(2,1)}, u32[]{:S(2)}) copy-start(bf16[320,512]{1,0:T(8,128)(2,1)} %get-tuple-element.31) | copy-start | bytes 983044
  86.4 26.3 %copy-start.3 = (f32[320,512]{1,0:T(8,128)S(1)}, f32[320,512]{1,0:T(8,128)}, u32[]{:S(2)}) copy-start(f32[320,512]{1,0:T(8,128)} %get-tuple-element.30) | copy-start | bytes 1966084
  86.4 4.1 %collective-permute-start.12 = (bf16[512,512]{1,0:T(8,128)(2,1)}, bf16[512,512]{1,0:T(8,128)(2,1)S(1)}, u32[]{:S(2)}, u32[]{:S(2)}) collective-permute-start(bf16[512,512]{1,0:T(8,128)(2,1)} %get-tuple-element.33), channel_id=1, source_target_pairs={{0,8},{8,0},{1,9},{9,1},{2,10},{10,2},{3,11},{11,3},{4,12},{12,4},... | collective-permute-start | bytes 1572872 | tf_op jit(solution)/shard_map/ppermute | solution.py:365
  92.8 25.9 %all-to-all-start.1 = ((bf16[32,16,512]{2,1,0:T(8,128)(2,1)}), bf16[32,16,512]{2,1,0:T(8,128)(2,1)S(1)}, u32[]{:S(2)}, u32[]{:S(2)}) async-start(bf16[32,16,512]{2,1,0:T(8,128)(2,1)} %bitcast.24), calls=%async_computation.1 | async-start | bytes 1048576 | tf_op jit(solution)/shard_map/all_to_all | solution.py:331
  101.6 11.1 %collective-permute-start.9 = (bf16[320,512]{1,0:T(8,128)(2,1)S(1)}, bf16[320,512]{1,0:T(8,128)(2,1)S(1)}, u32[]{:S(2)}, u32[]{:S(2)}) collective-permute-start(bf16[320,512]{1,0:T(8,128)(2,1)S(1)} %copy-done.7), channel_id=1, source_target_pairs={{0,1},{1,0},{2,3},{3,2},{4,5},{5,4},{6,7},{7,6},{8,9},{9,8},{10,11... | collective-permute-start | bytes 983048 | tf_op jit(solution)/shard_map/ppermute | solution.py:370
  112.7 24.0 %copy-start.4 = (f32[80,512]{1,0:T(8,128)S(1)}, f32[80,512]{1,0:T(8,128)}, u32[]{:S(2)}) copy-start(f32[80,512]{1,0:T(8,128)} %get-tuple-element.29) | copy-start | bytes 491524
  112.8 12.7 %collective-permute-start.10 = (bf16[160,512]{1,0:T(8,128)(2,1)S(1)}, bf16[160,512]{1,0:T(8,128)(2,1)S(1)}, u32[]{:S(2)}, u32[]{:S(2)}) collective-permute-start(bf16[160,512]{1,0:T(8,128)(2,1)S(1)} %slice.36), channel_id=1, source_target_pairs={{0,2},{1,3},{2,0},{3,1},{4,6},{5,7},{6,4},{7,5},{8,10},{9,11},{10,... | collective-permute-start | bytes 491528 | tf_op jit(solution)/shard_map/ppermute | solution.py:370
  119.5 15.2 %all-to-all-start.2 = ((bf16[8,16,512]{2,1,0:T(8,128)(2,1)}), bf16[8,16,512]{2,1,0:T(8,128)(2,1)S(1)}, u32[]{:S(2)}, u32[]{:S(2)}) async-start(bf16[8,16,512]{2,1,0:T(8,128)(2,1)} %broadcast_in_dim.54), calls=%async_computation.2 | async-start | bytes 262144 | tf_op jit(solution)/shard_map/all_to_all | solution.py:331
  125.6 11.1 %collective-permute-start.11 = (bf16[80,512]{1,0:T(8,128)(2,1)S(1)}, bf16[80,512]{1,0:T(8,128)(2,1)S(1)}, u32[]{:S(2)}, u32[]{:S(2)}) collective-permute-start(bf16[80,512]{1,0:T(8,128)(2,1)S(1)} %slice.37), channel_id=1, source_target_pairs={{0,4},{1,5},{2,6},{3,7},{4,0},{5,1},{6,2},{7,3},{8,12},{9,13},{10,... | collective-permute-start | bytes 245768 | tf_op jit(solution)/shard_map/ppermute | solution.py:370

commit v3 on v2

--- a/solution.py
+++ b/solution.py
@@ -18,9 +18,10 @@
 PART = 640
 GROUP = 256
 GROUPS = CUT // GROUP
+CHUNK = 512
 PACK = BORDER + 8
 EPS = 1e-05
-LIMIT = 60 * 1024 * 1024
+LIMIT = 65_500_000
 F32 = jnp.float32
 BF16 = jnp.bfloat16
 
@@ -87,7 +88,7 @@
         expand[start : start + count, 128:256] = turned
 
 
-def pick_body(where, near, far, senders, pick_t, selected):
+def pick_senders(where, near, far, senders, pick_t, selected):
     z, x, c = [where[i] for i in range(3)]
     partition = (z * X + x) * C + c
     tables = []
@@ -114,105 +115,138 @@
         match = jnp.where(picked == iota((GROUP, GROUP), 0), 1.0, 0.0)
         pick_t[k, :, :] = match.astype(BF16)
         table = jnp.concatenate(tables[2 * k : 2 * k + 2], axis=0)
-        senders[k * GROUP : (k + 1) * GROUP, :] = dot(match.T.astype(BF16), table).astype(BF16)
-
-
-def layer_body(
-    core, mine, other, local_edges, cut_edges, cot, local_senders, expand, spread, send_t, own, vectors,
-    cut_senders, pick_t,
-    node_out, local_grad, cut_grad, own_grad, keep, send, local_keep, local_send,
-    w1, w2, n1, n2, edges, slope, normed, inv, sems, edge_sems,
-):
-    copies = []
-    edge_copies = [
-        pltpu.make_async_copy(local_edges, edges.at[pl.ds(0, LOC), :], edge_sems.at[0]),
-        pltpu.make_async_copy(cut_edges, edges.at[pl.ds(LOC, CUT), :], edge_sems.at[1]),
+        senders[LOC + k * GROUP : LOC + (k + 1) * GROUP, :] = dot(match.T.astype(BF16), table).astype(BF16)
+
+
+INPUTS = 13
+OUTPUTS = 8
+WEIGHTS = ((0, 96), (96, 32), (128, 64), (192, 32))
+
+
+def layer_body(where, *refs):
+    inputs, refs = refs[:INPUTS], refs[INPUTS:]
+    outputs, scratch = refs[:OUTPUTS], refs[OUTPUTS:]
+    mine, other, near_in, far_in, local_edges, cut_edges, local_senders, *small = inputs
+    node_out, local_grad, cut_grad, own_grad, keep, send, local_keep, local_send = outputs
+    near, far, edges, senders, expand, spread, send_t, own, cot, vectors, *scratch = scratch
+    w1, w2, n1, n2, pick_t, selected, slope, normed, inv, *scratch = scratch
+    node_out_v, own_grad_v, keep_v, send_v, local_keep_v, local_send_v, in_sems, w_sems, out_sems = scratch
+    c = where[2]
+
+    copies = [
+        pltpu.make_async_copy(source, to, in_sems.at[i])
+        for i, (source, to) in enumerate(
+            (
+                (near_in, near),
+                (far_in, far),
+                (local_edges, edges.at[pl.ds(0, LOC), :]),
+                (cut_edges, edges.at[pl.ds(LOC, CUT), :]),
+                (local_senders, senders.at[pl.ds(0, LOC), :]),
+                *zip(small, (expand, spread, send_t, own, vectors, cot)),
+            )
+        )
     ]
-    first = core[0]
-    for i, (ref, start, size) in enumerate(((w1, 0, 96), (w2, 96, 32), (n1, 128, 64), (n2, 192, 32))):
-        for f in range(F):
-            for j, (half, place) in enumerate(((mine, first), (other, 1 - first))):
-                to = pl.multiple_of((2 * f + place) * size, 32)
-                copy = pltpu.make_async_copy(
-                    half.at[f, pl.ds(start, size), :], ref.at[pl.ds(to, size), :], sems.at[i, f, j]
-                )
-                copy.start()
-                copies.append((i, copy))
-        if i == 0:
-            for copy in edge_copies:
-                copy.start()
+    weight_copies = [
+        [
+            pltpu.make_async_copy(half.at[:, pl.ds(start, size), :], ref.at[:, place], w_sems.at[i, j])
+            for j, (half, place) in enumerate(((mine, c), (other, 1 - c)))
+        ]
+        for i, (ref, (start, size)) in enumerate(zip((w1, w2, n1, n2), WEIGHTS))
+    ]
+    for copy in (*copies[:2], *weight_copies[0], *copies[2:], *weight_copies[1], *weight_copies[2], *weight_copies[3]):
+        copy.start()
+    leaving = []
+
+    def leave(source, to):
+        copy = pltpu.make_async_copy(source, to, out_sems.at[len(leaving)])
+        copy.start()
+        leaving.append(copy)
+
+    def whole(ref):
+        return ref[...].reshape(-1, D)
+
+    for copy in copies[:2]:
+        copy.wait()
+    pick_senders(where, near, far, senders, pick_t, selected)
     eb1, eb2, eg, es, nb1, nb2, ng, ns = [vectors.at[pl.ds(i, 1), :] for i in range(8)]
-
-    def arrive(which):
-        for i, copy in copies:
-            if i == which:
-                copy.wait()
-
-    chunks = [(0, LOC)] + [(LOC + k * GROUP, GROUP) for k in range(GROUPS)]
+    forward = ((0, LOC + CUT // 2), (LOC + CUT // 2, CUT // 2))
+    chunks = ((0, LOC), (LOC, CUT))
     zeros = jnp.zeros((128 - OWN, D), BF16)
 
-    arrive(0)
-    received = dot(own[...], w1[2 * D : 3 * D, :]) + eb1[...]
+    for copy in (*copies[2:], *weight_copies[0]):
+        copy.wait()
+    first = whole(w1)
+    first_edge, first_send, first_recv = first[0:D], first[D : 2 * D], first[2 * D : 3 * D]
+    received = dot(own[...], first_recv) + eb1[...]
     upper, lower = split(received)
     table = jnp.concatenate([upper, zeros, lower, zeros], axis=0)
-    arrive(1)
-    for copy in edge_copies:
-        copy.wait()
+    for copy in weight_copies[1]:
+        copy.wait()
+    second = whole(w2)
     aggregate = jnp.zeros((OWN, D), F32)
-    for row, count in chunks:
+    for row, count in forward:
         at = slice(row, row + count)
         edge = edges[at, :]
-        sender = local_senders[...] if row == 0 else cut_senders[row - LOC : row - LOC + count, :]
-        pre = dot(edge, w1[0:D, :]) + dot(sender, w1[D : 2 * D, :]) + dot(expand[at, :], table)
+        pre = dot(edge, first_edge) + dot(senders[at, :], first_send) + dot(expand[at, :], table)
         act, slope[at, :] = silu_and_slope(pre)
-        unit, inv_std = normalize(dot(act, w2[...]) + eb2[...])
+        unit, inv_std = normalize(dot(act, second) + eb2[...])
         normed[at, :] = unit
         inv[at, :] = inv_std
         message = edge.astype(F32) + unit * eg[...] + es[...]
         aggregate += dot(spread[:, at], message.astype(BF16))
 
-    arrive(2)
-    arrive(3)
-    pre = dot(own[...], n1[0:D, :]) + dot(aggregate.astype(BF16), n1[D : 2 * D, :]) + nb1[...]
+    for copy in (*weight_copies[2], *weight_copies[3]):
+        copy.wait()
+    node_first, node_second = whole(n1), whole(n2)
+    pre = dot(own[...], node_first[0:D]) + dot(aggregate.astype(BF16), node_first[D : 2 * D]) + nb1[...]
     act, node_slope = silu_and_slope(pre)
-    unit, inv_std = normalize(dot(act, n2[...]) + nb2[...])
-    node_out[...] = (own[...].astype(F32) + unit * ng[...] + ns[...]).astype(BF16)
+    unit, inv_std = normalize(dot(act, node_second) + nb2[...])
+    node_out_v[...] = (own[...].astype(F32) + unit * ng[...] + ns[...]).astype(BF16)
+    leave(node_out_v, node_out)
     cotangent = cot[...].astype(F32)
     back = norm_back(cotangent * ng[...], unit, inv_std).astype(BF16)
-    back = (dot_t(back, n2[...]) * node_slope).astype(BF16)
-    result = cotangent + dot_t(back, n1[0:D, :])
-    upper, lower = split(dot_t(back, n1[D : 2 * D, :]))
+    back = (dot_t(back, node_second) * node_slope).astype(BF16)
+    upper, lower = split(dot_t(back, node_first[D : 2 * D]))
     table = jnp.concatenate([upper, zeros, lower, zeros], axis=0)
+    result = cotangent + dot_t(back, node_first[0:D])
 
     received = jnp.zeros((OWN, D), F32)
-    is_first = first == 0
+    is_first = c == 0
     for index, (row, count) in enumerate(chunks):
         at = slice(row, row + count)
         grad = dot(expand[at, :], table)
         back = norm_back(grad * eg[...], normed[at, :], inv[at, :]).astype(BF16)
-        back = (dot_t(back, w2[...]) * slope[at, :]).astype(BF16)
-        edge_grad = (grad + dot_t(back, w1[0:D, :])).astype(BF16)
-        send_grad = dot_t(back, w1[D : 2 * D, :]).astype(BF16)
+        back = (dot_t(back, second) * slope[at, :]).astype(BF16)
+        edges[at, :] = (grad + dot_t(back, first_edge)).astype(BF16)
+        send_grad = dot_t(back, first_send).astype(BF16)
         received += dot(spread[:, at], back)
         if index == 0:
-            local_grad[...] = edge_grad
+            leave(edges.at[pl.ds(0, LOC), :], local_grad)
             by_owner = dot(send_t[...], send_grad)
-            local_keep[...] = by_owner[0 : PART // 2, :]
-            local_send[...] = by_owner[PART // 2 : PART, :].astype(BF16)
+            local_keep_v[...] = by_owner[0 : PART // 2, :]
+            local_send_v[...] = by_owner[PART // 2 : PART, :].astype(BF16)
+            leave(local_keep_v, local_keep)
+            leave(local_send_v, local_send)
         else:
-            cut_grad[row - LOC : row - LOC + count, :] = edge_grad
-            summed = dot(pick_t[index - 1], send_grad)
-            for dz in range(2):
-                for x in range(X):
-                    start = (dz * X + x) * C * BORDER
-                    near = summed[start : start + BORDER, :]
-                    far = summed[start + BORDER : start + 2 * BORDER, :]
-                    to = ((2 * (index - 1) + dz) * X + x) * BORDER
-                    keep[to : to + BORDER, :] = jnp.where(is_first, near, far)
-                    send[to : to + BORDER, :] = jnp.where(is_first, far, near).astype(BF16)
+            leave(edges.at[pl.ds(row, count), :], cut_grad.at[pl.ds(row - LOC, count), :])
+            base = (row - LOC) // C
+            for k in range(count // GROUP):
+                summed = dot(pick_t[(row - LOC) // GROUP + k], send_grad[k * GROUP : (k + 1) * GROUP])
+                for place in range(2 * X):
+                    near_sum = summed[place * C * BORDER : (place * C + 1) * BORDER, :]
+                    far_sum = summed[(place * C + 1) * BORDER : (place + 1) * C * BORDER, :]
+                    to = base + (k * 2 * X + place) * BORDER
+                    keep_v[to : to + BORDER, :] = jnp.where(is_first, near_sum, far_sum).astype(BF16)
+                    send_v[to : to + BORDER, :] = jnp.where(is_first, far_sum, near_sum).astype(BF16)
+            part = pl.ds(base, count // C)
+            leave(send_v.at[part, :], send.at[part, :])
+            leave(keep_v.at[part, :], keep.at[part, :])
     upper, lower = split(received)
-    both = dot_t(jnp.concatenate([upper, lower], axis=0), w1[2 * D : 3 * D, :])
-    own_grad[...] = result + both[0:OWN, :] + both[OWN : 2 * OWN, :]
+    both = dot_t(jnp.concatenate([upper, lower], axis=0), first_recv)
+    own_grad_v[...] = result + both[0:OWN, :] + both[OWN : 2 * OWN, :]
+    leave(own_grad_v, own_grad)
+    for copy in leaving:
+        copy.wait()
 
 
 def shape(*dims, kind=BF16):
@@ -239,40 +273,42 @@
     )(*args)
 
 
-def pick(*args):
-    return pl.pallas_call(
-        pick_body,
-        in_specs=[SMEM, VMEM, VMEM],
-        out_specs=[VMEM] * 2,
-        out_shape=[shape(CUT, D), shape(GROUPS, GROUP, GROUP)],
-        scratch_shapes=[pltpu.VMEM((Z * X * C, D), F32)],
-        compiler_params=pltpu.CompilerParams(vmem_limit_bytes=LIMIT),
-        cost_estimate=pl.CostEstimate(flops=300_000_000, bytes_accessed=4_000_000, transcendentals=0),
-        name="pick",
-    )(*args)
-
-
 def layer(*args):
     return pl.pallas_call(
         layer_body,
-        in_specs=[SMEM] + [ANY] * 4 + [VMEM] * 9,
-        out_specs=[VMEM] * 8,
+        in_specs=[SMEM] + [ANY] * INPUTS,
+        out_specs=[ANY] * OUTPUTS,
         out_shape=[
             shape(OWN, D), shape(LOC, D), shape(CUT, D), shape(OWN, D, kind=F32),
-            shape(CUT // 2, D, kind=F32), shape(CUT // 2, D),
+            shape(CUT // 2, D), shape(CUT // 2, D),
             shape(PART // 2, D, kind=F32), shape(PART // 2, D),
         ],
         scratch_shapes=[
-            pltpu.VMEM((3 * D, D), BF16),
-            pltpu.VMEM((D, D), BF16),
-            pltpu.VMEM((2 * D, D), BF16),
-            pltpu.VMEM((D, D), BF16),
+            pltpu.VMEM((X, Z, PACK, D), BF16),
+            pltpu.VMEM((X, Z, PACK, D), BF16),
             pltpu.VMEM((ALL, D), BF16),
+            pltpu.VMEM((ALL, D), BF16),
+            pltpu.VMEM((ALL, 256), BF16),
+            pltpu.VMEM((OWN, ALL), BF16),
+            pltpu.VMEM((PART, LOC), BF16),
+            pltpu.VMEM((OWN, D), BF16),
+            pltpu.VMEM((OWN, D), BF16),
+            pltpu.VMEM((8, D), F32),
+            *[pltpu.VMEM((F, C, size, D), BF16) for _, size in WEIGHTS],
+            pltpu.VMEM((GROUPS, GROUP, GROUP), BF16),
+            pltpu.VMEM((Z * X * C, D), F32),
             pltpu.VMEM((ALL, D), F32),
             pltpu.VMEM((ALL, D), F32),
             pltpu.VMEM((ALL, 1), F32),
-            pltpu.SemaphoreType.DMA((4, F, 2)),
-            pltpu.SemaphoreType.DMA((2,)),
+            pltpu.VMEM((OWN, D), BF16),
+            pltpu.VMEM((OWN, D), F32),
+            pltpu.VMEM((CUT // 2, D), BF16),
+            pltpu.VMEM((CUT // 2, D), BF16),
+            pltpu.VMEM((PART // 2, D), F32),
+            pltpu.VMEM((PART // 2, D), BF16),
+            pltpu.SemaphoreType.DMA((11,)),
+            pltpu.SemaphoreType.DMA((4, C)),
+            pltpu.SemaphoreType.DMA((17,)),
         ],
         compiler_params=pltpu.CompilerParams(vmem_limit_bytes=LIMIT),
         cost_estimate=pl.CostEstimate(flops=4_000_000_000, bytes_accessed=12_000_000, transcendentals=600_000),
@@ -291,6 +327,7 @@
         out_specs=HBM,
         out_shape=jax.ShapeDtypeStruct(values.shape, values.dtype),
         input_output_aliases={0: 0},
+        compiler_params=pltpu.CompilerParams(vmem_limit_bytes=LIMIT),
         cost_estimate=pl.CostEstimate(flops=0, bytes_accessed=0, transcendentals=0),
         name="after",
     )(values, other)
@@ -355,14 +392,12 @@
         cut_recv[0], cut_count[0], *[v[None, :] for v in vectors],
     )
     place = jnp.stack([lax.axis_index(axis) for axis in DOM]).astype(jnp.int32)
-    cut_senders, pick_t = pick(place, near, far)
-    weights = after(weights, cut_senders)
+    weights = after(weights, far)
     other_weights = shift(weights, "core", C, 1)
     node_out, local_grad, cut_grad, own_grad, keep, send, local_keep, local_sums = layer(
-        core.astype(jnp.int32).reshape(1), weights, other_weights, local_edges, cut_edges, node_cot,
-        *indices, cut_senders, pick_t,
+        place, weights, other_weights, near, far, local_edges, cut_edges, *indices, node_cot
     )
-    summed = keep + lax.ppermute(send, "core", [(0, 1), (1, 0)]).astype(F32)
+    summed = keep.astype(F32) + lax.ppermute(send, "core", [(0, 1), (1, 0)]).astype(F32)
     for distance in (1, 2, 4):
         if distance > 1:
             half = local_keep.shape[0] // 2

time: 139 us -> 130 us (0.935)
  Pallas kernels: 25.3 us -> 18.9 us
  waiting for transfers between devices: 28.4 us -> 32.5 us
  local copies, waits for them, and re-layouts: 4.84 us -> 1.49 us
  starting transfers between devices: 73.5 us -> 71.4 us
    pallas_call x2 -> x1, Pallas kernels: 20.3 us -> 13.9 us  [layer(): pl.pallas_call(layer_body, in_specs=[SMEM] + [ANY] * INPUTS, out_specs=[A...]
    unnamed x21 -> x15, local copies, waits for them, and re-layouts: 3.4 us -> 0.04 us
    ppermute x3, starting transfers between devices: 14.5 us -> 11.6 us  [shards(): lax.ppermute(local_sums, 'feat', [(f, f ^ distance) for f in range(F)])]
    ppermute x3, waiting for transfers between devices: 10.4 us -> 12.7 us  [shards(): lax.ppermute(local_sums, 'feat', [(f, f ^ distance) for f in range(F)])]
    all_to_all x3, waiting for transfers between devices: 3.19 us -> 4.67 us  [exchange(): return lax.all_to_all(values, axis, split_axis=0, concat_axis=0, tiled=True)]
  transfers between devices with their start and end apart: 16 -> 16, of which waited for: 10 -> 11; matrix products, arithmetic and copies ran while one was open for 2% -> 2% of each run, Pallas kernels for 4% -> 2%
where the time goes in v3:
time: 130 us; the launch traced here: 129 us
  starting transfers between devices  71.4 us (55%)
  waiting for transfers between devices  32.5 us (25%)
  Pallas kernels  18.9 us (15%)
  other arithmetic  4.14 us (3%)
  local copies, waits for them, and re-layouts  1.49 us (1%)
    ppermute x9, starting transfers between devices, shift(): lax.ppermute(values, axis, [(i, (i + step) % size) for i in range(size)])  34.8 us
    all_to_all x3, starting transfers between devices, exchange(): return lax.all_to_all(values, axis, split_axis=0, concat_axis=0, tiled=True)  22.8 us
    pallas_call x1, Pallas kernels, layer(): pl.pallas_call(layer_body, in_specs=[SMEM] + [ANY] * INPUTS, out_specs=[A...  13.9 us
    ppermute x9, waiting for transfers between devices, shift(): lax.ppermute(values, axis, [(i, (i + step) % size) for i in range(size)])  13.2 us
    ppermute x3, waiting for transfers between devices, shards(): lax.ppermute(local_sums, 'feat', [(f, f ^ distance) for f in range(F)])  12.7 us
    ppermute x3, starting transfers between devices, shards(): lax.ppermute(local_sums, 'feat', [(f, f ^ distance) for f in range(F)])  11.6 us
    all_to_all x3, waiting for transfers between devices, exchange(): return lax.all_to_all(values, axis, split_axis=0, concat_axis=0, tiled=True)  4.67 us
    pallas_call x1, Pallas kernels, index(): pl.pallas_call(index_body, in_specs=[SMEM] + [VMEM] * 14, out_specs=[VMEM...  2.6 us
  transfers between devices with their start and end apart: 16, of which 11 were waited for; matrix products, arithmetic and copies ran while one was open for 2% of the time, Pallas kernels for 2%

profile of v3, /device:TPU:6, one launch (start us, length us, event | category | flops | bytes accessed | tf_op | source)
XLA Modules:
  0.0 129.4 jit_solution(7069946883844970782)
XLA Ops:
  0.6 2.4 %pack.1 = bf16[8,224,512]{2,1,0:T(8,128)(2,1)} custom-call(s32[1]{0:T(128)} %bitcast.2.core, bf16[192,512]{1,0:T(8,128)(2,1)} %first.1, bf16[64,512]{1,0:T(8,128)(2,1)} %second.1, bf16[128,512]{1,0:T(8,128)(2,1)} %third.1, bf16[64,512]{1,0:T(8,128)(2,1)} %fourth.1), custom_call_target="tpu_custom_call" | custom-call | bytes 2000000 | tf_op jit(solution)/shard_map/pack/pallas_call | solution.py:351
  3.0 0.0 copy-start.3
  3.0 7.1 %all-to-all-start = ((bf16[8,224,512]{2,1,0:T(8,128)(2,1)}), bf16[8,224,512]{2,1,0:T(8,128)(2,1)}, u32[]{:S(2)}, u32[]{:S(2)}) async-start(bf16[8,224,512]{2,1,0:T(8,128)(2,1)} %pack.1), calls=%async_computation | async-start | bytes 3670016 | tf_op jit(solution)/shard_map/all_to_all | solution.py:368
  10.2 0.0 copy-done.3
  10.2 0.7 slice.19
  10.9 4.3 %collective-permute-start.1 = (bf16[24,512]{1,0:T(8,128)(2,1)S(1)}, bf16[24,512]{1,0:T(8,128)(2,1)S(1)}, u32[]{:S(2)}, u32[]{:S(2)}) collective-permute-start(bf16[24,512]{1,0:T(8,128)(2,1)S(1)} %get-tuple-element.33), channel_id=1, source_target_pairs={{0,64},{64,128},{128,192},{192,256},{256,320},{320,384},{384,448},... | collective-permute-start | bytes 73736 | tf_op jit(solution)/shard_map/ppermute | solution.py:364
  15.2 8.6 %collective-permute-start = (bf16[24,512]{1,0:T(8,128)(2,1)S(1)}, bf16[24,512]{1,0:T(8,128)(2,1)S(1)}, u32[]{:S(2)}, u32[]{:S(2)}) collective-permute-start(bf16[24,512]{1,0:T(8,128)(2,1)S(1)} %get-tuple-element.33), channel_id=1, source_target_pairs={{0,448},{64,0},{128,64},{192,128},{256,192},{320,256},{384,320},{4... | collective-permute-start | bytes 73736 | tf_op jit(solution)/shard_map/ppermute | solution.py:364
  23.8 0.0 collective-permute-done.1
  23.8 3.9 %collective-permute-start.3 = (bf16[2,24,512]{2,1,0:T(8,128)(2,1)S(1)}, bf16[2,24,512]{2,1,0:T(8,128)(2,1)S(1)}, u32[]{:S(2)}, u32[]{:S(2)}) collective-permute-start(bf16[2,24,512]{2,1,0:T(8,128)(2,1)S(1)} %pad_maximum_fusion.2), channel_id=1, source_target_pairs={{0,320},{64,384},{128,448},{192,0},{256,64},{320,128},{384,192},{4... | collective-permute-start | bytes 147464 | tf_op jit(solution)/shard_map/ppermute | solution.py:364
  27.7 0.0 collective-permute-done
  27.8 4.2 %collective-permute-start.2 = (bf16[3,24,512]{2,1,0:T(8,128)(2,1)S(1)}, bf16[3,24,512]{2,1,0:T(8,128)(2,1)S(1)}, u32[]{:S(2)}, u32[]{:S(2)}) collective-permute-start(bf16[3,24,512]{2,1,0:T(8,128)(2,1)S(1)} %pad_maximum_fusion.1), channel_id=1, source_target_pairs={{0,192},{64,256},{128,320},{192,384},{256,448},{320,0},{384,64},{4... | collective-permute-start | bytes 221192 | tf_op jit(solution)/shard_map/ppermute | solution.py:364
  32.0 6.7 %collective-permute-done.2 = bf16[3,24,512]{2,1,0:T(8,128)(2,1)S(1)} collective-permute-done((bf16[3,24,512]{2,1,0:T(8,128)(2,1)S(1)}, bf16[3,24,512]{2,1,0:T(8,128)(2,1)S(1)}, u32[]{:S(2)}, u32[]{:S(2)}) %collective-permute-start.2) | collective-permute-done | bytes 73760 | tf_op jit(solution)/shard_map/ppermute | solution.py:364
  38.7 0.0 collective-permute-done.3
  38.8 2.7 %collective-permute-start.6 = (bf16[8,24,512]{2,1,0:T(8,128)(2,1)S(1)}, bf16[8,24,512]{2,1,0:T(8,128)(2,1)S(1)}, u32[]{:S(2)}, u32[]{:S(2)}) collective-permute-start(bf16[8,24,512]{2,1,0:T(8,128)(2,1)S(1)} %constant_dynamic-update-slice_fusion), channel_id=1, source_target_pairs={{0,48},{16,0},{32,16},{48,32},{1,49},{17,1},{33,17},{49,33},{2,50}... | collective-permute-start | bytes 589832 | tf_op jit(solution)/shard_map/ppermute | solution.py:364
  41.5 3.0 %collective-permute-start.5 = (bf16[8,24,512]{2,1,0:T(8,128)(2,1)S(1)}, bf16[8,24,512]{2,1,0:T(8,128)(2,1)S(1)}, u32[]{:S(2)}, u32[]{:S(2)}) collective-permute-start(bf16[8,24,512]{2,1,0:T(8,128)(2,1)S(1)} %constant_dynamic-update-slice_fusion), channel_id=1, source_target_pairs={{0,32},{16,48},{32,0},{48,16},{1,33},{17,49},{33,1},{49,17},{2,34}... | collective-permute-start | bytes 589832 | tf_op jit(solution)/shard_map/ppermute | solution.py:364
  44.5 4.0 %collective-permute-start.4 = (bf16[8,24,512]{2,1,0:T(8,128)(2,1)S(1)}, bf16[8,24,512]{2,1,0:T(8,128)(2,1)S(1)}, u32[]{:S(2)}, u32[]{:S(2)}) collective-permute-start(bf16[8,24,512]{2,1,0:T(8,128)(2,1)S(1)} %constant_dynamic-update-slice_fusion), channel_id=1, source_target_pairs={{0,16},{16,32},{32,48},{48,0},{1,17},{17,33},{33,49},{49,1},{2,18}... | collective-permute-start | bytes 589832 | tf_op jit(solution)/shard_map/ppermute | solution.py:364
  48.5 2.4 %collective-permute-done.6 = bf16[8,24,512]{2,1,0:T(8,128)(2,1)S(1)} collective-permute-done((bf16[8,24,512]{2,1,0:T(8,128)(2,1)S(1)}, bf16[8,24,512]{2,1,0:T(8,128)(2,1)S(1)}, u32[]{:S(2)}, u32[]{:S(2)}) %collective-permute-start.6) | collective-permute-done | bytes 196640 | tf_op jit(solution)/shard_map/ppermute | solution.py:364
  50.9 0.0 collective-permute-done.5
  50.9 1.5 %collective-permute-done.4 = bf16[8,24,512]{2,1,0:T(8,128)(2,1)S(1)} collective-permute-done((bf16[8,24,512]{2,1,0:T(8,128)(2,1)S(1)}, bf16[8,24,512]{2,1,0:T(8,128)(2,1)S(1)}, u32[]{:S(2)}, u32[]{:S(2)}) %collective-permute-start.4) | collective-permute-done | bytes 196640 | tf_op jit(solution)/shard_map/ppermute | solution.py:364
  52.4 0.1 pad_maximum_fusion.refs_2_
  52.5 0.0 copy-start
  52.5 0.0 copy-start.5
  52.5 2.1 %collective-permute-start.7 = (bf16[4,8,24,512]{3,2,1,0:T(8,128)(2,1)S(1)}, bf16[4,8,24,512]{3,2,1,0:T(8,128)(2,1)}, u32[]{:S(2)}, u32[]{:S(2)}) collective-permute-start(bf16[4,8,24,512]{3,2,1,0:T(8,128)(2,1)S(1)} %pad_maximum_fusion.refs_2_), channel_id=1, source_target_pairs={{0,8},{8,0},{1,9},{9,1},{2,10},{10,2},{3,11},{11,3},{4,12},{12,4},... | collective-permute-start | bytes 2359304 | tf_op jit(solution)/shard_map/ppermute | solution.py:364
  54.6 2.4 %collective-permute-done.7.other.refs_3_ = bf16[4,8,24,512]{3,2,1,0:T(8,128)(2,1)} collective-permute-done((bf16[4,8,24,512]{3,2,1,0:T(8,128)(2,1)S(1)}, bf16[4,8,24,512]{3,2,1,0:T(8,128)(2,1)}, u32[]{:S(2)}, u32[]{:S(2)}) %collective-permute-start.7) | collective-permute-done | bytes 786464 | tf_op jit(solution)/shard_map/ppermute | solution.py:364
  57.0 0.0 all-to-all-done.values
  57.0 0.0 copy-done
  57.0 2.0 %collective-permute-start.8 = (bf16[8,224,512]{2,1,0:T(8,128)(2,1)}, bf16[8,224,512]{2,1,0:T(8,128)(2,1)}, u32[]{:S(2)}, u32[]{:S(2)}) collective-permute-start(bf16[8,224,512]{2,1,0:T(8,128)(2,1)} %after.1.refs_0_), channel_id=1, source_target_pairs={{0,8},{8,0},{1,9},{9,1},{2,10},{10,2},{3,11},{11,3},{4,12},{12,4},... | collective-permute-start | bytes 5505032 | tf_op jit(solution)/shard_map/ppermute | solution.py:364
  59.0 0.0 copy-done.5
  59.0 0.5 fusion.5.moved
  59.6 2.6 %index.1 = (bf16[128,512]{1,0:T(8,128)(2,1)}, bf16[1152,256]{1,0:T(8,128)(2,1)}, bf16[80,1152]{1,0:T(8,128)(2,1)}, bf16[640,128]{1,0:T(8,128)(2,1)}, bf16[80,512]{1,0:T(8,128)(2,1)}, /*index=5*/f32[8,512]{1,0:T(8,128)}) custom-call(s32[1]{0:T(128)} %bitcast.10.feat, bf16[640,512]{1,0:T(8,128)(2,1)} %nodes.1, s32[1,128]{1,0:T(1,128)} %bitcast.46, ...), custom_call_target="tpu_custom_call" | custom-call | flops 200000000 | bytes 3000000 | tf_op jit(solution)/shard_map/index/pallas_call | solution.py:263
  62.2 0.6 pad_add_fusion.where
  62.7 0.3 collective-permute-done.8.refs_1_
  63.0 13.9 %layer.1 = (bf16[80,512]{1,0:T(8,128)(2,1)}, bf16[128,512]{1,0:T(8,128)(2,1)}, bf16[1024,512]{1,0:T(8,128)(2,1)}, f32[80,512]{1,0:T(8,128)}, bf16[512,512]{1,0:T...) custom-call(s32[3]{0:T(128)} %pad_add_fusion.where, ...), custom_call_target="tpu_custom_call" | custom-call | flops 4000000000 | bytes 12000000 | tf_op jit(solution)/shard_map/layer/pallas_call | solution.py:277
  76.9 0.0 copy-start.4
  77.0 0.0 copy-start.1
  77.0 2.2 %collective-permute-start.12 = (bf16[512,512]{1,0:T(8,128)(2,1)}, bf16[512,512]{1,0:T(8,128)(2,1)S(1)}, u32[]{:S(2)}, u32[]{:S(2)}) collective-permute-start(bf16[512,512]{1,0:T(8,128)(2,1)} %get-tuple-element.29), channel_id=1, source_target_pairs={{0,8},{8,0},{1,9},{9,1},{2,10},{10,2},{3,11},{11,3},{4,12},{12,4},... | collective-permute-start | bytes 1572872 | tf_op jit(solution)/shard_map/ppermute | solution.py:400
  79.2 2.0 %collective-permute-done.12 = bf16[512,512]{1,0:T(8,128)(2,1)S(1)} collective-permute-done((bf16[512,512]{1,0:T(8,128)(2,1)}, bf16[512,512]{1,0:T(8,128)(2,1)S(1)}, u32[]{:S(2)}, u32[]{:S(2)}) %collective-permute-start.12) | collective-permute-done | bytes 524320 | tf_op jit(solution)/shard_map/ppermute | solution.py:400
  81.1 2.0 %add_convert_fusion = bf16[512,512]{1,0:T(8,128)(2,1)} fusion(bf16[512,512]{1,0:T(8,128)(2,1)S(1)} %collective-permute-done.12, bf16[512,512]{1,0:T(8,128)(2,1)} %get-tuple-element.28), kind=kLoop, calls=%fused_computation | loop fusion | flops 1048576 | bytes 1572864 | tf_op jit(solution)/shard_map/convert_element_type | solution.py:407
  83.1 12.3 %all-to-all-start.1 = ((bf16[32,16,512]{2,1,0:T(8,128)(2,1)}), bf16[32,16,512]{2,1,0:T(8,128)(2,1)S(1)}, u32[]{:S(2)}, u32[]{:S(2)}) async-start(bf16[32,16,512]{2,1,0:T(8,128)(2,1)} %bitcast.24), calls=%async_computation.1 | async-start | bytes 1048576 | tf_op jit(solution)/shard_map/all_to_all | solution.py:368
  95.4 0.0 copy-done.4
  95.4 2.5 %collective-permute-start.9 = (bf16[320,512]{1,0:T(8,128)(2,1)S(1)}, bf16[320,512]{1,0:T(8,128)(2,1)S(1)}, u32[]{:S(2)}, u32[]{:S(2)}) collective-permute-start(bf16[320,512]{1,0:T(8,128)(2,1)S(1)} %copy-done.4), channel_id=1, source_target_pairs={{0,1},{1,0},{2,3},{3,2},{4,5},{5,4},{6,7},{7,6},{8,9},{9,8},{10,11... | collective-permute-start | bytes 983048 | tf_op jit(solution)/shard_map/ppermute | solution.py:405
  97.9 8.6 %collective-permute-done.9 = bf16[320,512]{1,0:T(8,128)(2,1)S(1)} collective-permute-done((bf16[320,512]{1,0:T(8,128)(2,1)S(1)}, bf16[320,512]{1,0:T(8,128)(2,1)S(1)}, u32[]{:S(2)}, u32[]{:S(2)}) %collective-permute-start.9) | collective-permute-done | bytes 327712 | tf_op jit(solution)/shard_map/ppermute | solution.py:405
  106.5 0.0 copy-done.1
  106.5 0.0 copy-start.2
  106.5 0.1 convert_add_fusion
  106.6 2.4 %collective-permute-start.10 = (bf16[160,512]{1,0:T(8,128)(2,1)S(1)}, bf16[160,512]{1,0:T(8,128)(2,1)S(1)}, u32[]{:S(2)}, u32[]{:S(2)}) collective-permute-start(bf16[160,512]{1,0:T(8,128)(2,1)S(1)} %slice.36), channel_id=1, source_target_pairs={{0,2},{1,3},{2,0},{3,1},{4,6},{5,7},{6,4},{7,5},{8,10},{9,11},{10,... | collective-permute-start | bytes 491528 | tf_op jit(solution)/shard_map/ppermute | solution.py:405
  109.0 3.5 %all-to-all-done.1 = bf16[32,16,512]{2,1,0:T(8,128)(2,1)S(1)} async-done(((bf16[32,16,512]{2,1,0:T(8,128)(2,1)}), bf16[32,16,512]{2,1,0:T(8,128)(2,1)S(1)}, u32[]{:S(2)}, u32[]{:S(2)}) %all-to-all-start.1) | async-done | bytes 524320 | tf_op jit(solution)/shard_map/all_to_all | solution.py:368
  112.5 0.1 reduce_sum.21
  112.6 0.7 broadcast_in_dim.54
  113.3 3.4 %all-to-all-start.2 = ((bf16[8,16,512]{2,1,0:T(8,128)(2,1)}), bf16[8,16,512]{2,1,0:T(8,128)(2,1)S(1)}, u32[]{:S(2)}, u32[]{:S(2)}) async-start(bf16[8,16,512]{2,1,0:T(8,128)(2,1)} %broadcast_in_dim.54), calls=%async_computation.2 | async-start | bytes 262144 | tf_op jit(solution)/shard_map/all_to_all | solution.py:368
  116.6 1.0 collective-permute-done.10
  117.7 6.7 %collective-permute-start.11 = (bf16[80,512]{1,0:T(8,128)(2,1)S(1)}, bf16[80,512]{1,0:T(8,128)(2,1)S(1)}, u32[]{:S(2)}, u32[]{:S(2)}) collective-permute-start(bf16[80,512]{1,0:T(8,128)(2,1)S(1)} %slice.37), channel_id=1, source_target_pairs={{0,4},{1,5},{2,6},{3,7},{4,0},{5,1},{6,2},{7,3},{8,12},{9,13},{10,... | collective-permute-start | bytes 245768 | tf_op jit(solution)/shard_map/ppermute | solution.py:405
  124.5 1.1 all-to-all-done.2
  125.7 3.1 %collective-permute-done.11 = bf16[80,512]{1,0:T(8,128)(2,1)S(1)} collective-permute-done((bf16[80,512]{1,0:T(8,128)(2,1)S(1)}, bf16[80,512]{1,0:T(8,128)(2,1)S(1)}, u32[]{:S(2)}, u32[]{:S(2)}) %collective-permute-start.11) | collective-permute-done | bytes 81952 | tf_op jit(solution)/shard_map/ppermute | solution.py:405
  128.7 0.0 copy-done.2
  128.7 0.7 fusion.1
  (16 shorter events, 0.2 us)
Async XLA Ops:
  3.0 7.1 %copy-start.3 = (s32[1,1,1024]{2,1,0:T(1,128)S(1)}, s32[1,1,1024]{2,1,0:T(1,128)}, u32[]{:S(2)}) copy-start(s32[1,1,1024]{2,1,0:T(1,128)} %param.39) | copy-start | bytes 12292
  3.0 53.9 %all-to-all-start = ((bf16[8,224,512]{2,1,0:T(8,128)(2,1)}), bf16[8,224,512]{2,1,0:T(8,128)(2,1)}, u32[]{:S(2)}, u32[]{:S(2)}) async-start(bf16[8,224,512]{2,1,0:T(8,128)(2,1)} %pack.1), calls=%async_computation | async-start | bytes 3670016 | tf_op jit(solution)/shard_map/all_to_all | solution.py:368
  10.9 12.9 %collective-permute-start.1 = (bf16[24,512]{1,0:T(8,128)(2,1)S(1)}, bf16[24,512]{1,0:T(8,128)(2,1)S(1)}, u32[]{:S(2)}, u32[]{:S(2)}) collective-permute-start(bf16[24,512]{1,0:T(8,128)(2,1)S(1)} %get-tuple-element.33), channel_id=1, source_target_pairs={{0,64},{64,128},{128,192},{192,256},{256,320},{320,384},{384,448},... | collective-permute-start | bytes 73736 | tf_op jit(solution)/shard_map/ppermute | solution.py:364
  15.2 12.5 %collective-permute-start = (bf16[24,512]{1,0:T(8,128)(2,1)S(1)}, bf16[24,512]{1,0:T(8,128)(2,1)S(1)}, u32[]{:S(2)}, u32[]{:S(2)}) collective-permute-start(bf16[24,512]{1,0:T(8,128)(2,1)S(1)} %get-tuple-element.33), channel_id=1, source_target_pairs={{0,448},{64,0},{128,64},{192,128},{256,192},{320,256},{384,320},{4... | collective-permute-start | bytes 73736 | tf_op jit(solution)/shard_map/ppermute | solution.py:364
  23.8 14.9 %collective-permute-start.3 = (bf16[2,24,512]{2,1,0:T(8,128)(2,1)S(1)}, bf16[2,24,512]{2,1,0:T(8,128)(2,1)S(1)}, u32[]{:S(2)}, u32[]{:S(2)}) collective-permute-start(bf16[2,24,512]{2,1,0:T(8,128)(2,1)S(1)} %pad_maximum_fusion.2), channel_id=1, source_target_pairs={{0,320},{64,384},{128,448},{192,0},{256,64},{320,128},{384,192},{4... | collective-permute-start | bytes 147464 | tf_op jit(solution)/shard_map/ppermute | solution.py:364
  27.8 11.0 %collective-permute-start.2 = (bf16[3,24,512]{2,1,0:T(8,128)(2,1)S(1)}, bf16[3,24,512]{2,1,0:T(8,128)(2,1)S(1)}, u32[]{:S(2)}, u32[]{:S(2)}) collective-permute-start(bf16[3,24,512]{2,1,0:T(8,128)(2,1)S(1)} %pad_maximum_fusion.1), channel_id=1, source_target_pairs={{0,192},{64,256},{128,320},{192,384},{256,448},{320,0},{384,64},{4... | collective-permute-start | bytes 221192 | tf_op jit(solution)/shard_map/ppermute | solution.py:364
  38.8 12.2 %collective-permute-start.6 = (bf16[8,24,512]{2,1,0:T(8,128)(2,1)S(1)}, bf16[8,24,512]{2,1,0:T(8,128)(2,1)S(1)}, u32[]{:S(2)}, u32[]{:S(2)}) collective-permute-start(bf16[8,24,512]{2,1,0:T(8,128)(2,1)S(1)} %constant_dynamic-update-slice_fusion), channel_id=1, source_target_pairs={{0,48},{16,0},{32,16},{48,32},{1,49},{17,1},{33,17},{49,33},{2,50}... | collective-permute-start | bytes 589832 | tf_op jit(solution)/shard_map/ppermute | solution.py:364
  41.5 9.4 %collective-permute-start.5 = (bf16[8,24,512]{2,1,0:T(8,128)(2,1)S(1)}, bf16[8,24,512]{2,1,0:T(8,128)(2,1)S(1)}, u32[]{:S(2)}, u32[]{:S(2)}) collective-permute-start(bf16[8,24,512]{2,1,0:T(8,128)(2,1)S(1)} %constant_dynamic-update-slice_fusion), channel_id=1, source_target_pairs={{0,32},{16,48},{32,0},{48,16},{1,33},{17,49},{33,1},{49,17},{2,34}... | collective-permute-start | bytes 589832 | tf_op jit(solution)/shard_map/ppermute | solution.py:364
  44.5 7.9 %collective-permute-start.4 = (bf16[8,24,512]{2,1,0:T(8,128)(2,1)S(1)}, bf16[8,24,512]{2,1,0:T(8,128)(2,1)S(1)}, u32[]{:S(2)}, u32[]{:S(2)}) collective-permute-start(bf16[8,24,512]{2,1,0:T(8,128)(2,1)S(1)} %constant_dynamic-update-slice_fusion), channel_id=1, source_target_pairs={{0,16},{16,32},{32,48},{48,0},{1,17},{17,33},{33,49},{49,1},{2,18}... | collective-permute-start | bytes 589832 | tf_op jit(solution)/shard_map/ppermute | solution.py:364
  52.5 4.5 %copy-start = (bf16[4,8,24,512]{3,2,1,0:T(8,128)(2,1)}, bf16[4,8,24,512]{3,2,1,0:T(8,128)(2,1)S(1)}, u32[]{:S(2)}) copy-start(bf16[4,8,24,512]{3,2,1,0:T(8,128)(2,1)S(1)} %pad_maximum_fusion.refs_2_) | copy-start | bytes 2359300
  52.5 6.5 %copy-start.5 = (s32[128]{0:T(128)S(1)}, s32[128]{0:T(128)}, u32[]{:S(2)}) copy-start(s32[128]{0:T(128)} %param.37) | copy-start | bytes 1540
  52.5 4.4 %collective-permute-start.7 = (bf16[4,8,24,512]{3,2,1,0:T(8,128)(2,1)S(1)}, bf16[4,8,24,512]{3,2,1,0:T(8,128)(2,1)}, u32[]{:S(2)}, u32[]{:S(2)}) collective-permute-start(bf16[4,8,24,512]{3,2,1,0:T(8,128)(2,1)S(1)} %pad_maximum_fusion.refs_2_), channel_id=1, source_target_pairs={{0,8},{8,0},{1,9},{9,1},{2,10},{10,2},{3,11},{11,3},{4,12},{12,4},... | collective-permute-start | bytes 2359304 | tf_op jit(solution)/shard_map/ppermute | solution.py:364
  57.0 6.0 %collective-permute-start.8 = (bf16[8,224,512]{2,1,0:T(8,128)(2,1)}, bf16[8,224,512]{2,1,0:T(8,128)(2,1)}, u32[]{:S(2)}, u32[]{:S(2)}) collective-permute-start(bf16[8,224,512]{2,1,0:T(8,128)(2,1)} %after.1.refs_0_), channel_id=1, source_target_pairs={{0,8},{8,0},{1,9},{9,1},{2,10},{10,2},{3,11},{11,3},{4,12},{12,4},... | collective-permute-start | bytes 5505032 | tf_op jit(solution)/shard_map/ppermute | solution.py:364
  76.9 18.4 %copy-start.4 = (bf16[320,512]{1,0:T(8,128)(2,1)S(1)}, bf16[320,512]{1,0:T(8,128)(2,1)}, u32[]{:S(2)}) copy-start(bf16[320,512]{1,0:T(8,128)(2,1)} %get-tuple-element.27) | copy-start | bytes 983044
  77.0 29.5 %copy-start.1 = (f32[320,512]{1,0:T(8,128)S(1)}, f32[320,512]{1,0:T(8,128)}, u32[]{:S(2)}) copy-start(f32[320,512]{1,0:T(8,128)} %get-tuple-element.26) | copy-start | bytes 1966084
  77.0 4.1 %collective-permute-start.12 = (bf16[512,512]{1,0:T(8,128)(2,1)}, bf16[512,512]{1,0:T(8,128)(2,1)S(1)}, u32[]{:S(2)}, u32[]{:S(2)}) collective-permute-start(bf16[512,512]{1,0:T(8,128)(2,1)} %get-tuple-element.29), channel_id=1, source_target_pairs={{0,8},{8,0},{1,9},{9,1},{2,10},{10,2},{3,11},{11,3},{4,12},{12,4},... | collective-permute-start | bytes 1572872 | tf_op jit(solution)/shard_map/ppermute | solution.py:400
  83.1 29.4 %all-to-all-start.1 = ((bf16[32,16,512]{2,1,0:T(8,128)(2,1)}), bf16[32,16,512]{2,1,0:T(8,128)(2,1)S(1)}, u32[]{:S(2)}, u32[]{:S(2)}) async-start(bf16[32,16,512]{2,1,0:T(8,128)(2,1)} %bitcast.24), calls=%async_computation.1 | async-start | bytes 1048576 | tf_op jit(solution)/shard_map/all_to_all | solution.py:368
  95.4 11.1 %collective-permute-start.9 = (bf16[320,512]{1,0:T(8,128)(2,1)S(1)}, bf16[320,512]{1,0:T(8,128)(2,1)S(1)}, u32[]{:S(2)}, u32[]{:S(2)}) collective-permute-start(bf16[320,512]{1,0:T(8,128)(2,1)S(1)} %copy-done.4), channel_id=1, source_target_pairs={{0,1},{1,0},{2,3},{3,2},{4,5},{5,4},{6,7},{7,6},{8,9},{9,8},{10,11... | collective-permute-start | bytes 983048 | tf_op jit(solution)/shard_map/ppermute | solution.py:405
  106.5 22.3 %copy-start.2 = (f32[80,512]{1,0:T(8,128)S(1)}, f32[80,512]{1,0:T(8,128)}, u32[]{:S(2)}) copy-start(f32[80,512]{1,0:T(8,128)} %get-tuple-element.25) | copy-start | bytes 491524
  106.6 11.1 %collective-permute-start.10 = (bf16[160,512]{1,0:T(8,128)(2,1)S(1)}, bf16[160,512]{1,0:T(8,128)(2,1)S(1)}, u32[]{:S(2)}, u32[]{:S(2)}) collective-permute-start(bf16[160,512]{1,0:T(8,128)(2,1)S(1)} %slice.36), channel_id=1, source_target_pairs={{0,2},{1,3},{2,0},{3,1},{4,6},{5,7},{6,4},{7,5},{8,10},{9,11},{10,... | collective-permute-start | bytes 491528 | tf_op jit(solution)/shard_map/ppermute | solution.py:405
  113.3 12.4 %all-to-all-start.2 = ((bf16[8,16,512]{2,1,0:T(8,128)(2,1)}), bf16[8,16,512]{2,1,0:T(8,128)(2,1)S(1)}, u32[]{:S(2)}, u32[]{:S(2)}) async-start(bf16[8,16,512]{2,1,0:T(8,128)(2,1)} %broadcast_in_dim.54), calls=%async_computation.2 | async-start | bytes 262144 | tf_op jit(solution)/shard_map/all_to_all | solution.py:368
  117.7 11.0 %collective-permute-start.11 = (bf16[80,512]{1,0:T(8,128)(2,1)S(1)}, bf16[80,512]{1,0:T(8,128)(2,1)S(1)}, u32[]{:S(2)}, u32[]{:S(2)}) collective-permute-start(bf16[80,512]{1,0:T(8,128)(2,1)S(1)} %slice.37), channel_id=1, source_target_pairs={{0,4},{1,5},{2,6},{3,7},{4,0},{5,1},{6,2},{7,3},{8,12},{9,13},{10,... | collective-permute-start | bytes 245768 | tf_op jit(solution)/shard_map/ppermute | solution.py:405

commit v4 on v3

--- a/solution.py
+++ b/solution.py
@@ -84,8 +84,7 @@
         match = jnp.where(to == iota((128, count), 0), 1.0, 0.0)
         spread[:, start : start + count] = match[0:OWN, :].astype(BF16)
         turned = match.T.astype(BF16)
-        expand[start : start + count, 0:128] = turned
-        expand[start : start + count, 128:256] = turned
+        expand[start : start + count, :] = turned
 
 
 def pick_senders(where, near, far, senders, pick_t, selected):
@@ -153,7 +152,7 @@
         ]
         for i, (ref, (start, size)) in enumerate(zip((w1, w2, n1, n2), WEIGHTS))
     ]
-    for copy in (*copies[:2], *weight_copies[0], *copies[2:], *weight_copies[1], *weight_copies[2], *weight_copies[3]):
+    for copy in (*copies[:2], *weight_copies[0], *copies[2:7], *copies[8:10], *weight_copies[1]):
         copy.start()
     leaving = []
 
@@ -170,11 +169,14 @@
     pick_senders(where, near, far, senders, pick_t, selected)
     eb1, eb2, eg, es, nb1, nb2, ng, ns = [vectors.at[pl.ds(i, 1), :] for i in range(8)]
     forward = ((0, LOC + CUT // 2), (LOC + CUT // 2, CUT // 2))
-    chunks = ((0, LOC), (LOC, CUT))
+    chunks = ((LOC, CUT // 2), (LOC + CUT // 2, CUT // 2), (0, LOC))
     zeros = jnp.zeros((128 - OWN, D), BF16)
 
-    for copy in (*copies[2:], *weight_copies[0]):
-        copy.wait()
+    late = (*weight_copies[2], *weight_copies[3], copies[7], copies[10])
+    for copy in (*copies[2:7], *copies[8:10], *weight_copies[0]):
+        copy.wait()
+    for copy in late:
+        copy.start()
     first = whole(w1)
     first_edge, first_send, first_recv = first[0:D], first[D : 2 * D], first[2 * D : 3 * D]
     received = dot(own[...], first_recv) + eb1[...]
@@ -187,7 +189,7 @@
     for row, count in forward:
         at = slice(row, row + count)
         edge = edges[at, :]
-        pre = dot(edge, first_edge) + dot(senders[at, :], first_send) + dot(expand[at, :], table)
+        pre = dot(edge, first_edge) + dot(senders[at, :], first_send) + dot(jnp.concatenate([expand[at, :]] * 2, axis=1), table)
         act, slope[at, :] = silu_and_slope(pre)
         unit, inv_std = normalize(dot(act, second) + eb2[...])
         normed[at, :] = unit
@@ -195,7 +197,7 @@
         message = edge.astype(F32) + unit * eg[...] + es[...]
         aggregate += dot(spread[:, at], message.astype(BF16))
 
-    for copy in (*weight_copies[2], *weight_copies[3]):
+    for copy in late:
         copy.wait()
     node_first, node_second = whole(n1), whole(n2)
     pre = dot(own[...], node_first[0:D]) + dot(aggregate.astype(BF16), node_first[D : 2 * D]) + nb1[...]
@@ -212,15 +214,15 @@
 
     received = jnp.zeros((OWN, D), F32)
     is_first = c == 0
-    for index, (row, count) in enumerate(chunks):
+    for row, count in chunks:
         at = slice(row, row + count)
-        grad = dot(expand[at, :], table)
+        grad = dot(jnp.concatenate([expand[at, :]] * 2, axis=1), table)
         back = norm_back(grad * eg[...], normed[at, :], inv[at, :]).astype(BF16)
         back = (dot_t(back, second) * slope[at, :]).astype(BF16)
         edges[at, :] = (grad + dot_t(back, first_edge)).astype(BF16)
         send_grad = dot_t(back, first_send).astype(BF16)
         received += dot(spread[:, at], back)
-        if index == 0:
+        if row == 0:
             leave(edges.at[pl.ds(0, LOC), :], local_grad)
             by_owner = dot(send_t[...], send_grad)
             local_keep_v[...] = by_owner[0 : PART // 2, :]
@@ -265,7 +267,7 @@
         in_specs=[SMEM] + [VMEM] * 14,
         out_specs=[VMEM] * 6,
         out_shape=[
-            shape(LOC, D), shape(ALL, 256), shape(OWN, ALL), shape(PART, LOC), shape(OWN, D), shape(8, D, kind=F32),
+            shape(LOC, D), shape(ALL, 128), shape(OWN, ALL), shape(PART, LOC), shape(OWN, D), shape(8, D, kind=F32),
         ],
         compiler_params=pltpu.CompilerParams(vmem_limit_bytes=LIMIT),
         cost_estimate=pl.CostEstimate(flops=200_000_000, bytes_accessed=3_000_000, transcendentals=0),
@@ -288,7 +290,7 @@
             pltpu.VMEM((X, Z, PACK, D), BF16),
             pltpu.VMEM((ALL, D), BF16),
             pltpu.VMEM((ALL, D), BF16),
-            pltpu.VMEM((ALL, 256), BF16),
+            pltpu.VMEM((ALL, 128), BF16),
             pltpu.VMEM((OWN, ALL), BF16),
             pltpu.VMEM((PART, LOC), BF16),
             pltpu.VMEM((OWN, D), BF16),

time: 130 us -> 130 us (level)
  no operation moved by 1% of the time
where the time goes in v4:
time: 130 us; the launch traced here: 129 us
  starting transfers between devices  71.4 us (55%)
  waiting for transfers between devices  32.5 us (25%)
  Pallas kernels  18.2 us (14%)
  other arithmetic  4.2 us (3%)
  local copies, waits for them, and re-layouts  1.49 us (1%)
    ppermute x9, starting transfers between devices, shift(): lax.ppermute(values, axis, [(i, (i + step) % size) for i in range(size)])  34.8 us
    all_to_all x3, starting transfers between devices, exchange(): return lax.all_to_all(values, axis, split_axis=0, concat_axis=0, tiled=True)  22.8 us
    pallas_call x1, Pallas kernels, layer(): pl.pallas_call(layer_body, in_specs=[SMEM] + [ANY] * INPUTS, out_specs=[A...  13.3 us
    ppermute x9, waiting for transfers between devices, shift(): lax.ppermute(values, axis, [(i, (i + step) % size) for i in range(size)])  13.3 us
    ppermute x3, waiting for transfers between devices, shards(): lax.ppermute(local_sums, 'feat', [(f, f ^ distance) for f in range(F)])  12.7 us
    ppermute x3, starting transfers between devices, shards(): lax.ppermute(local_sums, 'feat', [(f, f ^ distance) for f in range(F)])  11.6 us
    all_to_all x3, waiting for transfers between devices, exchange(): return lax.all_to_all(values, axis, split_axis=0, concat_axis=0, tiled=True)  4.65 us
  transfers between devices with their start and end apart: 16, of which 11 were waited for; matrix products, arithmetic and copies ran while one was open for 2% of the time, Pallas kernels for 2%

profile of v4, /device:TPU:6, one launch (start us, length us, event | category | flops | bytes accessed | tf_op | source)
XLA Modules:
  0.0 128.8 jit_solution(4465936959677410967)
XLA Ops:
  0.6 2.4 %pack.1 = bf16[8,224,512]{2,1,0:T(8,128)(2,1)} custom-call(s32[1]{0:T(128)} %bitcast.2.core, bf16[192,512]{1,0:T(8,128)(2,1)} %first.1, bf16[64,512]{1,0:T(8,128)(2,1)} %second.1, bf16[128,512]{1,0:T(8,128)(2,1)} %third.1, bf16[64,512]{1,0:T(8,128)(2,1)} %fourth.1), custom_call_target="tpu_custom_call" | custom-call | bytes 2000000 | tf_op jit(solution)/shard_map/pack/pallas_call | solution.py:353
  3.0 0.0 copy-start.3
  3.0 7.1 %all-to-all-start = ((bf16[8,224,512]{2,1,0:T(8,128)(2,1)}), bf16[8,224,512]{2,1,0:T(8,128)(2,1)}, u32[]{:S(2)}, u32[]{:S(2)}) async-start(bf16[8,224,512]{2,1,0:T(8,128)(2,1)} %pack.1), calls=%async_computation | async-start | bytes 3670016 | tf_op jit(solution)/shard_map/all_to_all | solution.py:370
  10.2 0.0 copy-done.3
  10.2 0.7 slice.19
  10.9 4.3 %collective-permute-start.1 = (bf16[24,512]{1,0:T(8,128)(2,1)S(1)}, bf16[24,512]{1,0:T(8,128)(2,1)S(1)}, u32[]{:S(2)}, u32[]{:S(2)}) collective-permute-start(bf16[24,512]{1,0:T(8,128)(2,1)S(1)} %get-tuple-element.33), channel_id=1, source_target_pairs={{0,64},{64,128},{128,192},{192,256},{256,320},{320,384},{384,448},... | collective-permute-start | bytes 73736 | tf_op jit(solution)/shard_map/ppermute | solution.py:366
  15.2 8.6 %collective-permute-start = (bf16[24,512]{1,0:T(8,128)(2,1)S(1)}, bf16[24,512]{1,0:T(8,128)(2,1)S(1)}, u32[]{:S(2)}, u32[]{:S(2)}) collective-permute-start(bf16[24,512]{1,0:T(8,128)(2,1)S(1)} %get-tuple-element.33), channel_id=1, source_target_pairs={{0,448},{64,0},{128,64},{192,128},{256,192},{320,256},{384,320},{4... | collective-permute-start | bytes 73736 | tf_op jit(solution)/shard_map/ppermute | solution.py:366
  23.8 0.0 collective-permute-done.1
  23.8 3.9 %collective-permute-start.3 = (bf16[2,24,512]{2,1,0:T(8,128)(2,1)S(1)}, bf16[2,24,512]{2,1,0:T(8,128)(2,1)S(1)}, u32[]{:S(2)}, u32[]{:S(2)}) collective-permute-start(bf16[2,24,512]{2,1,0:T(8,128)(2,1)S(1)} %pad_maximum_fusion.2), channel_id=1, source_target_pairs={{0,320},{64,384},{128,448},{192,0},{256,64},{320,128},{384,192},{4... | collective-permute-start | bytes 147464 | tf_op jit(solution)/shard_map/ppermute | solution.py:366
  27.7 0.0 collective-permute-done
  27.8 4.2 %collective-permute-start.2 = (bf16[3,24,512]{2,1,0:T(8,128)(2,1)S(1)}, bf16[3,24,512]{2,1,0:T(8,128)(2,1)S(1)}, u32[]{:S(2)}, u32[]{:S(2)}) collective-permute-start(bf16[3,24,512]{2,1,0:T(8,128)(2,1)S(1)} %pad_maximum_fusion.1), channel_id=1, source_target_pairs={{0,192},{64,256},{128,320},{192,384},{256,448},{320,0},{384,64},{4... | collective-permute-start | bytes 221192 | tf_op jit(solution)/shard_map/ppermute | solution.py:366
  32.0 6.7 %collective-permute-done.2 = bf16[3,24,512]{2,1,0:T(8,128)(2,1)S(1)} collective-permute-done((bf16[3,24,512]{2,1,0:T(8,128)(2,1)S(1)}, bf16[3,24,512]{2,1,0:T(8,128)(2,1)S(1)}, u32[]{:S(2)}, u32[]{:S(2)}) %collective-permute-start.2) | collective-permute-done | bytes 73760 | tf_op jit(solution)/shard_map/ppermute | solution.py:366
  38.7 0.0 collective-permute-done.3
  38.8 2.7 %collective-permute-start.6 = (bf16[8,24,512]{2,1,0:T(8,128)(2,1)S(1)}, bf16[8,24,512]{2,1,0:T(8,128)(2,1)S(1)}, u32[]{:S(2)}, u32[]{:S(2)}) collective-permute-start(bf16[8,24,512]{2,1,0:T(8,128)(2,1)S(1)} %constant_dynamic-update-slice_fusion), channel_id=1, source_target_pairs={{0,48},{16,0},{32,16},{48,32},{1,49},{17,1},{33,17},{49,33},{2,50}... | collective-permute-start | bytes 589832 | tf_op jit(solution)/shard_map/ppermute | solution.py:366
  41.5 3.0 %collective-permute-start.5 = (bf16[8,24,512]{2,1,0:T(8,128)(2,1)S(1)}, bf16[8,24,512]{2,1,0:T(8,128)(2,1)S(1)}, u32[]{:S(2)}, u32[]{:S(2)}) collective-permute-start(bf16[8,24,512]{2,1,0:T(8,128)(2,1)S(1)} %constant_dynamic-update-slice_fusion), channel_id=1, source_target_pairs={{0,32},{16,48},{32,0},{48,16},{1,33},{17,49},{33,1},{49,17},{2,34}... | collective-permute-start | bytes 589832 | tf_op jit(solution)/shard_map/ppermute | solution.py:366
  44.5 4.0 %collective-permute-start.4 = (bf16[8,24,512]{2,1,0:T(8,128)(2,1)S(1)}, bf16[8,24,512]{2,1,0:T(8,128)(2,1)S(1)}, u32[]{:S(2)}, u32[]{:S(2)}) collective-permute-start(bf16[8,24,512]{2,1,0:T(8,128)(2,1)S(1)} %constant_dynamic-update-slice_fusion), channel_id=1, source_target_pairs={{0,16},{16,32},{32,48},{48,0},{1,17},{17,33},{33,49},{49,1},{2,18}... | collective-permute-start | bytes 589832 | tf_op jit(solution)/shard_map/ppermute | solution.py:366
  48.5 2.4 %collective-permute-done.6 = bf16[8,24,512]{2,1,0:T(8,128)(2,1)S(1)} collective-permute-done((bf16[8,24,512]{2,1,0:T(8,128)(2,1)S(1)}, bf16[8,24,512]{2,1,0:T(8,128)(2,1)S(1)}, u32[]{:S(2)}, u32[]{:S(2)}) %collective-permute-start.6) | collective-permute-done | bytes 196640 | tf_op jit(solution)/shard_map/ppermute | solution.py:366
  50.9 0.0 collective-permute-done.5
  50.9 1.5 %collective-permute-done.4 = bf16[8,24,512]{2,1,0:T(8,128)(2,1)S(1)} collective-permute-done((bf16[8,24,512]{2,1,0:T(8,128)(2,1)S(1)}, bf16[8,24,512]{2,1,0:T(8,128)(2,1)S(1)}, u32[]{:S(2)}, u32[]{:S(2)}) %collective-permute-start.4) | collective-permute-done | bytes 196640 | tf_op jit(solution)/shard_map/ppermute | solution.py:366
  52.4 0.1 pad_maximum_fusion.refs_2_
  52.5 0.0 copy-start
  52.5 0.0 copy-start.5
  52.5 2.1 %collective-permute-start.7 = (bf16[4,8,24,512]{3,2,1,0:T(8,128)(2,1)S(1)}, bf16[4,8,24,512]{3,2,1,0:T(8,128)(2,1)}, u32[]{:S(2)}, u32[]{:S(2)}) collective-permute-start(bf16[4,8,24,512]{3,2,1,0:T(8,128)(2,1)S(1)} %pad_maximum_fusion.refs_2_), channel_id=1, source_target_pairs={{0,8},{8,0},{1,9},{9,1},{2,10},{10,2},{3,11},{11,3},{4,12},{12,4},... | collective-permute-start | bytes 2359304 | tf_op jit(solution)/shard_map/ppermute | solution.py:366
  54.6 2.4 %collective-permute-done.7.other.refs_3_ = bf16[4,8,24,512]{3,2,1,0:T(8,128)(2,1)} collective-permute-done((bf16[4,8,24,512]{3,2,1,0:T(8,128)(2,1)S(1)}, bf16[4,8,24,512]{3,2,1,0:T(8,128)(2,1)}, u32[]{:S(2)}, u32[]{:S(2)}) %collective-permute-start.7) | collective-permute-done | bytes 786464 | tf_op jit(solution)/shard_map/ppermute | solution.py:366
  57.0 0.0 all-to-all-done.values
  57.0 0.0 copy-done
  57.0 2.0 %collective-permute-start.8 = (bf16[8,224,512]{2,1,0:T(8,128)(2,1)}, bf16[8,224,512]{2,1,0:T(8,128)(2,1)}, u32[]{:S(2)}, u32[]{:S(2)}) collective-permute-start(bf16[8,224,512]{2,1,0:T(8,128)(2,1)} %after.1.refs_0_), channel_id=1, source_target_pairs={{0,8},{8,0},{1,9},{9,1},{2,10},{10,2},{3,11},{11,3},{4,12},{12,4},... | collective-permute-start | bytes 5505032 | tf_op jit(solution)/shard_map/ppermute | solution.py:366
  59.0 0.0 copy-done.5
  59.0 0.5 fusion.5.moved
  59.6 2.5 %index.1 = (bf16[128,512]{1,0:T(8,128)(2,1)}, bf16[1152,128]{1,0:T(8,128)(2,1)}, bf16[80,1152]{1,0:T(8,128)(2,1)}, bf16[640,128]{1,0:T(8,128)(2,1)}, bf16[80,512]{1,0:T(8,128)(2,1)}, /*index=5*/f32[8,512]{1,0:T(8,128)}) custom-call(s32[1]{0:T(128)} %bitcast.10.feat, bf16[640,512]{1,0:T(8,128)(2,1)} %nodes.1, s32[1,128]{1,0:T(1,128)} %bitcast.46, ...), custom_call_target="tpu_custom_call" | custom-call | flops 200000000 | bytes 3000000 | tf_op jit(solution)/shard_map/index/pallas_call | solution.py:265
  62.1 0.6 pad_add_fusion.where
  62.7 0.3 collective-permute-done.8.refs_1_
  63.0 13.3 %layer.1 = (bf16[80,512]{1,0:T(8,128)(2,1)}, bf16[128,512]{1,0:T(8,128)(2,1)}, bf16[1024,512]{1,0:T(8,128)(2,1)}, f32[80,512]{1,0:T(8,128)}, bf16[512,512]{1,0:T...) custom-call(s32[3]{0:T(128)} %pad_add_fusion.where, ...), custom_call_target="tpu_custom_call" | custom-call | flops 4000000000 | bytes 12000000 | tf_op jit(solution)/shard_map/layer/pallas_call | solution.py:279
  76.3 0.0 copy-start.4
  76.3 0.0 copy-start.1
  76.3 2.2 %collective-permute-start.12 = (bf16[512,512]{1,0:T(8,128)(2,1)}, bf16[512,512]{1,0:T(8,128)(2,1)S(1)}, u32[]{:S(2)}, u32[]{:S(2)}) collective-permute-start(bf16[512,512]{1,0:T(8,128)(2,1)} %get-tuple-element.29), channel_id=1, source_target_pairs={{0,8},{8,0},{1,9},{9,1},{2,10},{10,2},{3,11},{11,3},{4,12},{12,4},... | collective-permute-start | bytes 1572872 | tf_op jit(solution)/shard_map/ppermute | solution.py:402
  78.5 1.9 %collective-permute-done.12 = bf16[512,512]{1,0:T(8,128)(2,1)S(1)} collective-permute-done((bf16[512,512]{1,0:T(8,128)(2,1)}, bf16[512,512]{1,0:T(8,128)(2,1)S(1)}, u32[]{:S(2)}, u32[]{:S(2)}) %collective-permute-start.12) | collective-permute-done | bytes 524320 | tf_op jit(solution)/shard_map/ppermute | solution.py:402
  80.5 2.0 %add_convert_fusion = bf16[512,512]{1,0:T(8,128)(2,1)} fusion(bf16[512,512]{1,0:T(8,128)(2,1)S(1)} %collective-permute-done.12, bf16[512,512]{1,0:T(8,128)(2,1)} %get-tuple-element.28), kind=kLoop, calls=%fused_computation | loop fusion | flops 1048576 | bytes 1572864 | tf_op jit(solution)/shard_map/convert_element_type | solution.py:409
  82.4 12.3 %all-to-all-start.1 = ((bf16[32,16,512]{2,1,0:T(8,128)(2,1)}), bf16[32,16,512]{2,1,0:T(8,128)(2,1)S(1)}, u32[]{:S(2)}, u32[]{:S(2)}) async-start(bf16[32,16,512]{2,1,0:T(8,128)(2,1)} %bitcast.24), calls=%async_computation.1 | async-start | bytes 1048576 | tf_op jit(solution)/shard_map/all_to_all | solution.py:370
  94.7 0.0 copy-done.4
  94.7 2.5 %collective-permute-start.9 = (bf16[320,512]{1,0:T(8,128)(2,1)S(1)}, bf16[320,512]{1,0:T(8,128)(2,1)S(1)}, u32[]{:S(2)}, u32[]{:S(2)}) collective-permute-start(bf16[320,512]{1,0:T(8,128)(2,1)S(1)} %copy-done.4), channel_id=1, source_target_pairs={{0,1},{1,0},{2,3},{3,2},{4,5},{5,4},{6,7},{7,6},{8,9},{9,8},{10,11... | collective-permute-start | bytes 983048 | tf_op jit(solution)/shard_map/ppermute | solution.py:407
  97.2 8.6 %collective-permute-done.9 = bf16[320,512]{1,0:T(8,128)(2,1)S(1)} collective-permute-done((bf16[320,512]{1,0:T(8,128)(2,1)S(1)}, bf16[320,512]{1,0:T(8,128)(2,1)S(1)}, u32[]{:S(2)}, u32[]{:S(2)}) %collective-permute-start.9) | collective-permute-done | bytes 327712 | tf_op jit(solution)/shard_map/ppermute | solution.py:407
  105.8 0.0 copy-done.1
  105.8 0.0 copy-start.2
  105.8 0.1 convert_add_fusion
  105.9 2.4 %collective-permute-start.10 = (bf16[160,512]{1,0:T(8,128)(2,1)S(1)}, bf16[160,512]{1,0:T(8,128)(2,1)S(1)}, u32[]{:S(2)}, u32[]{:S(2)}) collective-permute-start(bf16[160,512]{1,0:T(8,128)(2,1)S(1)} %slice.36), channel_id=1, source_target_pairs={{0,2},{1,3},{2,0},{3,1},{4,6},{5,7},{6,4},{7,5},{8,10},{9,11},{10,... | collective-permute-start | bytes 491528 | tf_op jit(solution)/shard_map/ppermute | solution.py:407
  108.3 3.5 %all-to-all-done.1 = bf16[32,16,512]{2,1,0:T(8,128)(2,1)S(1)} async-done(((bf16[32,16,512]{2,1,0:T(8,128)(2,1)}), bf16[32,16,512]{2,1,0:T(8,128)(2,1)S(1)}, u32[]{:S(2)}, u32[]{:S(2)}) %all-to-all-start.1) | async-done | bytes 524320 | tf_op jit(solution)/shard_map/all_to_all | solution.py:370
  111.8 0.1 reduce_sum.21
  111.9 0.7 broadcast_in_dim.54
  112.6 3.4 %all-to-all-start.2 = ((bf16[8,16,512]{2,1,0:T(8,128)(2,1)}), bf16[8,16,512]{2,1,0:T(8,128)(2,1)S(1)}, u32[]{:S(2)}, u32[]{:S(2)}) async-start(bf16[8,16,512]{2,1,0:T(8,128)(2,1)} %broadcast_in_dim.54), calls=%async_computation.2 | async-start | bytes 262144 | tf_op jit(solution)/shard_map/all_to_all | solution.py:370
  116.0 1.0 collective-permute-done.10
  117.1 6.7 %collective-permute-start.11 = (bf16[80,512]{1,0:T(8,128)(2,1)S(1)}, bf16[80,512]{1,0:T(8,128)(2,1)S(1)}, u32[]{:S(2)}, u32[]{:S(2)}) collective-permute-start(bf16[80,512]{1,0:T(8,128)(2,1)S(1)} %slice.37), channel_id=1, source_target_pairs={{0,4},{1,5},{2,6},{3,7},{4,0},{5,1},{6,2},{7,3},{8,12},{9,13},{10,... | collective-permute-start | bytes 245768 | tf_op jit(solution)/shard_map/ppermute | solution.py:407
  123.8 1.1 all-to-all-done.2
  125.0 3.1 %collective-permute-done.11 = bf16[80,512]{1,0:T(8,128)(2,1)S(1)} collective-permute-done((bf16[80,512]{1,0:T(8,128)(2,1)S(1)}, bf16[80,512]{1,0:T(8,128)(2,1)S(1)}, u32[]{:S(2)}, u32[]{:S(2)}) %collective-permute-start.11) | collective-permute-done | bytes 81952 | tf_op jit(solution)/shard_map/ppermute | solution.py:407
  128.1 0.0 copy-done.2
  128.1 0.7 fusion.1
  (16 shorter events, 0.2 us)
Async XLA Ops:
  3.0 7.1 %copy-start.3 = (s32[1,1,1024]{2,1,0:T(1,128)S(1)}, s32[1,1,1024]{2,1,0:T(1,128)}, u32[]{:S(2)}) copy-start(s32[1,1,1024]{2,1,0:T(1,128)} %param.39) | copy-start | bytes 12292
  3.0 53.9 %all-to-all-start = ((bf16[8,224,512]{2,1,0:T(8,128)(2,1)}), bf16[8,224,512]{2,1,0:T(8,128)(2,1)}, u32[]{:S(2)}, u32[]{:S(2)}) async-start(bf16[8,224,512]{2,1,0:T(8,128)(2,1)} %pack.1), calls=%async_computation | async-start | bytes 3670016 | tf_op jit(solution)/shard_map/all_to_all | solution.py:370
  10.9 12.9 %collective-permute-start.1 = (bf16[24,512]{1,0:T(8,128)(2,1)S(1)}, bf16[24,512]{1,0:T(8,128)(2,1)S(1)}, u32[]{:S(2)}, u32[]{:S(2)}) collective-permute-start(bf16[24,512]{1,0:T(8,128)(2,1)S(1)} %get-tuple-element.33), channel_id=1, source_target_pairs={{0,64},{64,128},{128,192},{192,256},{256,320},{320,384},{384,448},... | collective-permute-start | bytes 73736 | tf_op jit(solution)/shard_map/ppermute | solution.py:366
  15.2 12.5 %collective-permute-start = (bf16[24,512]{1,0:T(8,128)(2,1)S(1)}, bf16[24,512]{1,0:T(8,128)(2,1)S(1)}, u32[]{:S(2)}, u32[]{:S(2)}) collective-permute-start(bf16[24,512]{1,0:T(8,128)(2,1)S(1)} %get-tuple-element.33), channel_id=1, source_target_pairs={{0,448},{64,0},{128,64},{192,128},{256,192},{320,256},{384,320},{4... | collective-permute-start | bytes 73736 | tf_op jit(solution)/shard_map/ppermute | solution.py:366
  23.8 14.9 %collective-permute-start.3 = (bf16[2,24,512]{2,1,0:T(8,128)(2,1)S(1)}, bf16[2,24,512]{2,1,0:T(8,128)(2,1)S(1)}, u32[]{:S(2)}, u32[]{:S(2)}) collective-permute-start(bf16[2,24,512]{2,1,0:T(8,128)(2,1)S(1)} %pad_maximum_fusion.2), channel_id=1, source_target_pairs={{0,320},{64,384},{128,448},{192,0},{256,64},{320,128},{384,192},{4... | collective-permute-start | bytes 147464 | tf_op jit(solution)/shard_map/ppermute | solution.py:366
  27.8 11.0 %collective-permute-start.2 = (bf16[3,24,512]{2,1,0:T(8,128)(2,1)S(1)}, bf16[3,24,512]{2,1,0:T(8,128)(2,1)S(1)}, u32[]{:S(2)}, u32[]{:S(2)}) collective-permute-start(bf16[3,24,512]{2,1,0:T(8,128)(2,1)S(1)} %pad_maximum_fusion.1), channel_id=1, source_target_pairs={{0,192},{64,256},{128,320},{192,384},{256,448},{320,0},{384,64},{4... | collective-permute-start | bytes 221192 | tf_op jit(solution)/shard_map/ppermute | solution.py:366
  38.8 12.2 %collective-permute-start.6 = (bf16[8,24,512]{2,1,0:T(8,128)(2,1)S(1)}, bf16[8,24,512]{2,1,0:T(8,128)(2,1)S(1)}, u32[]{:S(2)}, u32[]{:S(2)}) collective-permute-start(bf16[8,24,512]{2,1,0:T(8,128)(2,1)S(1)} %constant_dynamic-update-slice_fusion), channel_id=1, source_target_pairs={{0,48},{16,0},{32,16},{48,32},{1,49},{17,1},{33,17},{49,33},{2,50}... | collective-permute-start | bytes 589832 | tf_op jit(solution)/shard_map/ppermute | solution.py:366
  41.5 9.4 %collective-permute-start.5 = (bf16[8,24,512]{2,1,0:T(8,128)(2,1)S(1)}, bf16[8,24,512]{2,1,0:T(8,128)(2,1)S(1)}, u32[]{:S(2)}, u32[]{:S(2)}) collective-permute-start(bf16[8,24,512]{2,1,0:T(8,128)(2,1)S(1)} %constant_dynamic-update-slice_fusion), channel_id=1, source_target_pairs={{0,32},{16,48},{32,0},{48,16},{1,33},{17,49},{33,1},{49,17},{2,34}... | collective-permute-start | bytes 589832 | tf_op jit(solution)/shard_map/ppermute | solution.py:366
  44.5 7.9 %collective-permute-start.4 = (bf16[8,24,512]{2,1,0:T(8,128)(2,1)S(1)}, bf16[8,24,512]{2,1,0:T(8,128)(2,1)S(1)}, u32[]{:S(2)}, u32[]{:S(2)}) collective-permute-start(bf16[8,24,512]{2,1,0:T(8,128)(2,1)S(1)} %constant_dynamic-update-slice_fusion), channel_id=1, source_target_pairs={{0,16},{16,32},{32,48},{48,0},{1,17},{17,33},{33,49},{49,1},{2,18}... | collective-permute-start | bytes 589832 | tf_op jit(solution)/shard_map/ppermute | solution.py:366
  52.5 4.5 %copy-start = (bf16[4,8,24,512]{3,2,1,0:T(8,128)(2,1)}, bf16[4,8,24,512]{3,2,1,0:T(8,128)(2,1)S(1)}, u32[]{:S(2)}) copy-start(bf16[4,8,24,512]{3,2,1,0:T(8,128)(2,1)S(1)} %pad_maximum_fusion.refs_2_) | copy-start | bytes 2359300
  52.5 6.5 %copy-start.5 = (s32[128]{0:T(128)S(1)}, s32[128]{0:T(128)}, u32[]{:S(2)}) copy-start(s32[128]{0:T(128)} %param.37) | copy-start | bytes 1540
  52.5 4.4 %collective-permute-start.7 = (bf16[4,8,24,512]{3,2,1,0:T(8,128)(2,1)S(1)}, bf16[4,8,24,512]{3,2,1,0:T(8,128)(2,1)}, u32[]{:S(2)}, u32[]{:S(2)}) collective-permute-start(bf16[4,8,24,512]{3,2,1,0:T(8,128)(2,1)S(1)} %pad_maximum_fusion.refs_2_), channel_id=1, source_target_pairs={{0,8},{8,0},{1,9},{9,1},{2,10},{10,2},{3,11},{11,3},{4,12},{12,4},... | collective-permute-start | bytes 2359304 | tf_op jit(solution)/shard_map/ppermute | solution.py:366
  57.0 6.0 %collective-permute-start.8 = (bf16[8,224,512]{2,1,0:T(8,128)(2,1)}, bf16[8,224,512]{2,1,0:T(8,128)(2,1)}, u32[]{:S(2)}, u32[]{:S(2)}) collective-permute-start(bf16[8,224,512]{2,1,0:T(8,128)(2,1)} %after.1.refs_0_), channel_id=1, source_target_pairs={{0,8},{8,0},{1,9},{9,1},{2,10},{10,2},{3,11},{11,3},{4,12},{12,4},... | collective-permute-start | bytes 5505032 | tf_op jit(solution)/shard_map/ppermute | solution.py:366
  76.3 18.4 %copy-start.4 = (bf16[320,512]{1,0:T(8,128)(2,1)S(1)}, bf16[320,512]{1,0:T(8,128)(2,1)}, u32[]{:S(2)}) copy-start(bf16[320,512]{1,0:T(8,128)(2,1)} %get-tuple-element.27) | copy-start | bytes 983044
  76.3 29.5 %copy-start.1 = (f32[320,512]{1,0:T(8,128)S(1)}, f32[320,512]{1,0:T(8,128)}, u32[]{:S(2)}) copy-start(f32[320,512]{1,0:T(8,128)} %get-tuple-element.26) | copy-start | bytes 1966084
  76.3 4.1 %collective-permute-start.12 = (bf16[512,512]{1,0:T(8,128)(2,1)}, bf16[512,512]{1,0:T(8,128)(2,1)S(1)}, u32[]{:S(2)}, u32[]{:S(2)}) collective-permute-start(bf16[512,512]{1,0:T(8,128)(2,1)} %get-tuple-element.29), channel_id=1, source_target_pairs={{0,8},{8,0},{1,9},{9,1},{2,10},{10,2},{3,11},{11,3},{4,12},{12,4},... | collective-permute-start | bytes 1572872 | tf_op jit(solution)/shard_map/ppermute | solution.py:402
  82.4 29.4 %all-to-all-start.1 = ((bf16[32,16,512]{2,1,0:T(8,128)(2,1)}), bf16[32,16,512]{2,1,0:T(8,128)(2,1)S(1)}, u32[]{:S(2)}, u32[]{:S(2)}) async-start(bf16[32,16,512]{2,1,0:T(8,128)(2,1)} %bitcast.24), calls=%async_computation.1 | async-start | bytes 1048576 | tf_op jit(solution)/shard_map/all_to_all | solution.py:370
  94.7 11.1 %collective-permute-start.9 = (bf16[320,512]{1,0:T(8,128)(2,1)S(1)}, bf16[320,512]{1,0:T(8,128)(2,1)S(1)}, u32[]{:S(2)}, u32[]{:S(2)}) collective-permute-start(bf16[320,512]{1,0:T(8,128)(2,1)S(1)} %copy-done.4), channel_id=1, source_target_pairs={{0,1},{1,0},{2,3},{3,2},{4,5},{5,4},{6,7},{7,6},{8,9},{9,8},{10,11... | collective-permute-start | bytes 983048 | tf_op jit(solution)/shard_map/ppermute | solution.py:407
  105.8 22.3 %copy-start.2 = (f32[80,512]{1,0:T(8,128)S(1)}, f32[80,512]{1,0:T(8,128)}, u32[]{:S(2)}) copy-start(f32[80,512]{1,0:T(8,128)} %get-tuple-element.25) | copy-start | bytes 491524
  105.9 11.1 %collective-permute-start.10 = (bf16[160,512]{1,0:T(8,128)(2,1)S(1)}, bf16[160,512]{1,0:T(8,128)(2,1)S(1)}, u32[]{:S(2)}, u32[]{:S(2)}) collective-permute-start(bf16[160,512]{1,0:T(8,128)(2,1)S(1)} %slice.36), channel_id=1, source_target_pairs={{0,2},{1,3},{2,0},{3,1},{4,6},{5,7},{6,4},{7,5},{8,10},{9,11},{10,... | collective-permute-start | bytes 491528 | tf_op jit(solution)/shard_map/ppermute | solution.py:407
  112.6 12.4 %all-to-all-start.2 = ((bf16[8,16,512]{2,1,0:T(8,128)(2,1)}), bf16[8,16,512]{2,1,0:T(8,128)(2,1)S(1)}, u32[]{:S(2)}, u32[]{:S(2)}) async-start(bf16[8,16,512]{2,1,0:T(8,128)(2,1)} %broadcast_in_dim.54), calls=%async_computation.2 | async-start | bytes 262144 | tf_op jit(solution)/shard_map/all_to_all | solution.py:370
  117.1 11.0 %collective-permute-start.11 = (bf16[80,512]{1,0:T(8,128)(2,1)S(1)}, bf16[80,512]{1,0:T(8,128)(2,1)S(1)}, u32[]{:S(2)}, u32[]{:S(2)}) collective-permute-start(bf16[80,512]{1,0:T(8,128)(2,1)S(1)} %slice.37), channel_id=1, source_target_pairs={{0,4},{1,5},{2,6},{3,7},{4,0},{5,1},{6,2},{7,3},{8,12},{9,13},{10,... | collective-permute-start | bytes 245768 | tf_op jit(solution)/shard_map/ppermute | solution.py:407

commit v5 on v4

--- a/solution.py
+++ b/solution.py
@@ -366,6 +366,25 @@
     return lax.ppermute(values, axis, [(i, (i + step) % size) for i in range(size)])
 
 
+def stage_body(values, out, sem):
+    copy = pltpu.make_async_copy(values, out, sem)
+    copy.start()
+    copy.wait()
+
+
+def stage(values):
+    return pl.pallas_call(
+        stage_body,
+        in_specs=[ANY],
+        out_specs=VMEM,
+        out_shape=jax.ShapeDtypeStruct(values.shape, values.dtype),
+        scratch_shapes=[pltpu.SemaphoreType.DMA],
+        compiler_params=pltpu.CompilerParams(vmem_limit_bytes=8 * 1024 * 1024),
+        cost_estimate=pl.CostEstimate(flops=0, bytes_accessed=1_000_000, transcendentals=0),
+        name="stage",
+    )(values)
+
+
 def exchange(values, axis):
     return lax.all_to_all(values, axis, split_axis=0, concat_axis=0, tiled=True)
 
@@ -399,7 +418,7 @@
     node_out, local_grad, cut_grad, own_grad, keep, send, local_keep, local_sums = layer(
         place, weights, other_weights, near, far, local_edges, cut_edges, *indices, node_cot
     )
-    summed = keep.astype(F32) + lax.ppermute(send, "core", [(0, 1), (1, 0)]).astype(F32)
+    summed = stage(keep).astype(F32) + lax.ppermute(send, "core", [(0, 1), (1, 0)]).astype(F32)
     for distance in (1, 2, 4):
         if distance > 1:
             half = local_keep.shape[0] // 2

time: 130 us -> 128 us (0.985)
  no operation moved by 1% of the time
where the time goes in v5:
time: 128 us
  starting transfers between devices  71.2 us (56%)
  waiting for transfers between devices  31.4 us (25%)
  Pallas kernels  18.2 us (14%)
  other arithmetic  3.22 us (3%)
  local copies, waits for them, and re-layouts  2.52 us (2%)
    ppermute x9, starting transfers between devices, shift(): lax.ppermute(values, axis, [(i, (i + step) % size) for i in range(size)])  34.8 us
    all_to_all x3, starting transfers between devices, exchange(): return lax.all_to_all(values, axis, split_axis=0, concat_axis=0, tiled=True)  22.8 us
    pallas_call x1, Pallas kernels, layer(): pl.pallas_call(layer_body, in_specs=[SMEM] + [ANY] * INPUTS, out_specs=[A...  13.3 us
    ppermute x9, waiting for transfers between devices, shift(): lax.ppermute(values, axis, [(i, (i + step) % size) for i in range(size)])  13.2 us
    ppermute x3, waiting for transfers between devices, shards(): lax.ppermute(local_sums, 'feat', [(f, f ^ distance) for f in range(F)])  12.7 us
    ppermute x3, starting transfers between devices, shards(): lax.ppermute(local_sums, 'feat', [(f, f ^ distance) for f in range(F)])  11.6 us
    all_to_all x3, waiting for transfers between devices, exchange(): return lax.all_to_all(values, axis, split_axis=0, concat_axis=0, tiled=True)  4.69 us
  transfers between devices with their start and end apart: 16, of which 11 were waited for; matrix products, arithmetic and copies ran while one was open for 2% of the time, Pallas kernels for 2%

profile of v5, /device:TPU:6, one launch (start us, length us, event | category | flops | bytes accessed | tf_op | source)
XLA Modules:
  0.0 127.6 jit_solution(9219395926935182007)
XLA Ops:
  0.6 2.4 %pack.1 = bf16[8,224,512]{2,1,0:T(8,128)(2,1)} custom-call(s32[1]{0:T(128)} %bitcast.2.core, bf16[192,512]{1,0:T(8,128)(2,1)} %first.1, bf16[64,512]{1,0:T(8,128)(2,1)} %second.1, bf16[128,512]{1,0:T(8,128)(2,1)} %third.1, bf16[64,512]{1,0:T(8,128)(2,1)} %fourth.1), custom_call_target="tpu_custom_call" | custom-call | bytes 2000000 | tf_op jit(solution)/shard_map/pack/pallas_call | solution.py:353
  3.0 0.0 copy-start.4
  3.0 7.1 %all-to-all-start = ((bf16[8,224,512]{2,1,0:T(8,128)(2,1)}), bf16[8,224,512]{2,1,0:T(8,128)(2,1)}, u32[]{:S(2)}, u32[]{:S(2)}) async-start(bf16[8,224,512]{2,1,0:T(8,128)(2,1)} %pack.1), calls=%async_computation | async-start | bytes 3670016 | tf_op jit(solution)/shard_map/all_to_all | solution.py:389
  10.1 0.0 copy-done.4
  10.2 0.7 slice.19
  10.9 4.3 %collective-permute-start.1 = (bf16[24,512]{1,0:T(8,128)(2,1)S(1)}, bf16[24,512]{1,0:T(8,128)(2,1)S(1)}, u32[]{:S(2)}, u32[]{:S(2)}) collective-permute-start(bf16[24,512]{1,0:T(8,128)(2,1)S(1)} %get-tuple-element.33), channel_id=1, source_target_pairs={{0,64},{64,128},{128,192},{192,256},{256,320},{320,384},{384,448},... | collective-permute-start | bytes 73736 | tf_op jit(solution)/shard_map/ppermute | solution.py:366
  15.2 8.6 %collective-permute-start = (bf16[24,512]{1,0:T(8,128)(2,1)S(1)}, bf16[24,512]{1,0:T(8,128)(2,1)S(1)}, u32[]{:S(2)}, u32[]{:S(2)}) collective-permute-start(bf16[24,512]{1,0:T(8,128)(2,1)S(1)} %get-tuple-element.33), channel_id=1, source_target_pairs={{0,448},{64,0},{128,64},{192,128},{256,192},{320,256},{384,320},{4... | collective-permute-start | bytes 73736 | tf_op jit(solution)/shard_map/ppermute | solution.py:366
  23.8 0.0 collective-permute-done.1
  23.8 3.9 %collective-permute-start.3 = (bf16[2,24,512]{2,1,0:T(8,128)(2,1)S(1)}, bf16[2,24,512]{2,1,0:T(8,128)(2,1)S(1)}, u32[]{:S(2)}, u32[]{:S(2)}) collective-permute-start(bf16[2,24,512]{2,1,0:T(8,128)(2,1)S(1)} %pad_maximum_fusion.2), channel_id=1, source_target_pairs={{0,320},{64,384},{128,448},{192,0},{256,64},{320,128},{384,192},{4... | collective-permute-start | bytes 147464 | tf_op jit(solution)/shard_map/ppermute | solution.py:366
  27.7 0.0 collective-permute-done
  27.8 4.2 %collective-permute-start.2 = (bf16[3,24,512]{2,1,0:T(8,128)(2,1)S(1)}, bf16[3,24,512]{2,1,0:T(8,128)(2,1)S(1)}, u32[]{:S(2)}, u32[]{:S(2)}) collective-permute-start(bf16[3,24,512]{2,1,0:T(8,128)(2,1)S(1)} %pad_maximum_fusion.1), channel_id=1, source_target_pairs={{0,192},{64,256},{128,320},{192,384},{256,448},{320,0},{384,64},{4... | collective-permute-start | bytes 221192 | tf_op jit(solution)/shard_map/ppermute | solution.py:366
  32.0 6.7 %collective-permute-done.2 = bf16[3,24,512]{2,1,0:T(8,128)(2,1)S(1)} collective-permute-done((bf16[3,24,512]{2,1,0:T(8,128)(2,1)S(1)}, bf16[3,24,512]{2,1,0:T(8,128)(2,1)S(1)}, u32[]{:S(2)}, u32[]{:S(2)}) %collective-permute-start.2) | collective-permute-done | bytes 73760 | tf_op jit(solution)/shard_map/ppermute | solution.py:366
  38.7 0.0 collective-permute-done.3
  38.7 2.7 %collective-permute-start.6 = (bf16[8,24,512]{2,1,0:T(8,128)(2,1)S(1)}, bf16[8,24,512]{2,1,0:T(8,128)(2,1)S(1)}, u32[]{:S(2)}, u32[]{:S(2)}) collective-permute-start(bf16[8,24,512]{2,1,0:T(8,128)(2,1)S(1)} %constant_dynamic-update-slice_fusion), channel_id=1, source_target_pairs={{0,48},{16,0},{32,16},{48,32},{1,49},{17,1},{33,17},{49,33},{2,50}... | collective-permute-start | bytes 589832 | tf_op jit(solution)/shard_map/ppermute | solution.py:366
  41.5 3.0 %collective-permute-start.5 = (bf16[8,24,512]{2,1,0:T(8,128)(2,1)S(1)}, bf16[8,24,512]{2,1,0:T(8,128)(2,1)S(1)}, u32[]{:S(2)}, u32[]{:S(2)}) collective-permute-start(bf16[8,24,512]{2,1,0:T(8,128)(2,1)S(1)} %constant_dynamic-update-slice_fusion), channel_id=1, source_target_pairs={{0,32},{16,48},{32,0},{48,16},{1,33},{17,49},{33,1},{49,17},{2,34}... | collective-permute-start | bytes 589832 | tf_op jit(solution)/shard_map/ppermute | solution.py:366
  44.5 4.0 %collective-permute-start.4 = (bf16[8,24,512]{2,1,0:T(8,128)(2,1)S(1)}, bf16[8,24,512]{2,1,0:T(8,128)(2,1)S(1)}, u32[]{:S(2)}, u32[]{:S(2)}) collective-permute-start(bf16[8,24,512]{2,1,0:T(8,128)(2,1)S(1)} %constant_dynamic-update-slice_fusion), channel_id=1, source_target_pairs={{0,16},{16,32},{32,48},{48,0},{1,17},{17,33},{33,49},{49,1},{2,18}... | collective-permute-start | bytes 589832 | tf_op jit(solution)/shard_map/ppermute | solution.py:366
  48.5 2.4 %collective-permute-done.6 = bf16[8,24,512]{2,1,0:T(8,128)(2,1)S(1)} collective-permute-done((bf16[8,24,512]{2,1,0:T(8,128)(2,1)S(1)}, bf16[8,24,512]{2,1,0:T(8,128)(2,1)S(1)}, u32[]{:S(2)}, u32[]{:S(2)}) %collective-permute-start.6) | collective-permute-done | bytes 196640 | tf_op jit(solution)/shard_map/ppermute | solution.py:366
  50.9 0.0 collective-permute-done.5
  50.9 1.5 %collective-permute-done.4 = bf16[8,24,512]{2,1,0:T(8,128)(2,1)S(1)} collective-permute-done((bf16[8,24,512]{2,1,0:T(8,128)(2,1)S(1)}, bf16[8,24,512]{2,1,0:T(8,128)(2,1)S(1)}, u32[]{:S(2)}, u32[]{:S(2)}) %collective-permute-start.4) | collective-permute-done | bytes 196640 | tf_op jit(solution)/shard_map/ppermute | solution.py:366
  52.4 0.1 pad_maximum_fusion.refs_2_
  52.5 0.0 copy-start.1
  52.5 0.0 copy-start.6
  52.5 2.1 %collective-permute-start.7 = (bf16[4,8,24,512]{3,2,1,0:T(8,128)(2,1)S(1)}, bf16[4,8,24,512]{3,2,1,0:T(8,128)(2,1)}, u32[]{:S(2)}, u32[]{:S(2)}) collective-permute-start(bf16[4,8,24,512]{3,2,1,0:T(8,128)(2,1)S(1)} %pad_maximum_fusion.refs_2_), channel_id=1, source_target_pairs={{0,8},{8,0},{1,9},{9,1},{2,10},{10,2},{3,11},{11,3},{4,12},{12,4},... | collective-permute-start | bytes 2359304 | tf_op jit(solution)/shard_map/ppermute | solution.py:366
  54.6 2.4 %collective-permute-done.7.other.refs_3_ = bf16[4,8,24,512]{3,2,1,0:T(8,128)(2,1)} collective-permute-done((bf16[4,8,24,512]{3,2,1,0:T(8,128)(2,1)S(1)}, bf16[4,8,24,512]{3,2,1,0:T(8,128)(2,1)}, u32[]{:S(2)}, u32[]{:S(2)}) %collective-permute-start.7) | collective-permute-done | bytes 786464 | tf_op jit(solution)/shard_map/ppermute | solution.py:366
  57.0 0.0 all-to-all-done.values
  57.0 0.0 copy-done.1
  57.0 2.0 %collective-permute-start.8 = (bf16[8,224,512]{2,1,0:T(8,128)(2,1)}, bf16[8,224,512]{2,1,0:T(8,128)(2,1)}, u32[]{:S(2)}, u32[]{:S(2)}) collective-permute-start(bf16[8,224,512]{2,1,0:T(8,128)(2,1)} %after.1.refs_0_), channel_id=1, source_target_pairs={{0,8},{8,0},{1,9},{9,1},{2,10},{10,2},{3,11},{11,3},{4,12},{12,4},... | collective-permute-start | bytes 5505032 | tf_op jit(solution)/shard_map/ppermute | solution.py:366
  59.0 0.0 copy-done.6
  59.0 0.6 fusion.5.moved
  59.6 2.5 %index.1 = (bf16[128,512]{1,0:T(8,128)(2,1)}, bf16[1152,128]{1,0:T(8,128)(2,1)}, bf16[80,1152]{1,0:T(8,128)(2,1)}, bf16[640,128]{1,0:T(8,128)(2,1)}, bf16[80,512]{1,0:T(8,128)(2,1)}, /*index=5*/f32[8,512]{1,0:T(8,128)}) custom-call(s32[1]{0:T(128)} %bitcast.10.feat, bf16[640,512]{1,0:T(8,128)(2,1)} %nodes.1, s32[1,128]{1,0:T(1,128)} %bitcast.46, ...), custom_call_target="tpu_custom_call" | custom-call | flops 200000000 | bytes 3000000 | tf_op jit(solution)/shard_map/index/pallas_call | solution.py:265
  62.1 0.7 pad_add_fusion.where
  62.8 0.2 collective-permute-done.8.refs_1_
  63.0 13.3 %layer.1 = (bf16[80,512]{1,0:T(8,128)(2,1)}, bf16[128,512]{1,0:T(8,128)(2,1)}, bf16[1024,512]{1,0:T(8,128)(2,1)}, f32[80,512]{1,0:T(8,128)}, bf16[512,512]{1,0:T...) custom-call(s32[3]{0:T(128)} %pad_add_fusion.where, ...), custom_call_target="tpu_custom_call" | custom-call | flops 4000000000 | bytes 12000000 | tf_op jit(solution)/shard_map/layer/pallas_call | solution.py:279
  76.3 2.1 %collective-permute-start.12 = (bf16[512,512]{1,0:T(8,128)(2,1)}, bf16[512,512]{1,0:T(8,128)(2,1)S(1)}, u32[]{:S(2)}, u32[]{:S(2)}) collective-permute-start(bf16[512,512]{1,0:T(8,128)(2,1)} %get-tuple-element.29), channel_id=1, source_target_pairs={{0,8},{8,0},{1,9},{9,1},{2,10},{10,2},{3,11},{11,3},{4,12},{12,4},... | collective-permute-start | bytes 1572872 | tf_op jit(solution)/shard_map/ppermute | solution.py:421
  78.4 0.0 copy-start
  78.4 1.0 copy-done
  79.4 0.0 copy-start.5
  79.4 0.0 copy-start.2
  79.5 0.8 collective-permute-done.12
  80.3 0.9 add_convert_fusion
  81.2 12.3 %all-to-all-start.1 = ((bf16[32,16,512]{2,1,0:T(8,128)(2,1)}), bf16[32,16,512]{2,1,0:T(8,128)(2,1)S(1)}, u32[]{:S(2)}, u32[]{:S(2)}) async-start(bf16[32,16,512]{2,1,0:T(8,128)(2,1)} %bitcast.24), calls=%async_computation.1 | async-start | bytes 1048576 | tf_op jit(solution)/shard_map/all_to_all | solution.py:389
  93.5 0.0 copy-done.5
  93.5 2.5 %collective-permute-start.9 = (bf16[320,512]{1,0:T(8,128)(2,1)S(1)}, bf16[320,512]{1,0:T(8,128)(2,1)S(1)}, u32[]{:S(2)}, u32[]{:S(2)}) collective-permute-start(bf16[320,512]{1,0:T(8,128)(2,1)S(1)} %copy-done.5), channel_id=1, source_target_pairs={{0,1},{1,0},{2,3},{3,2},{4,5},{5,4},{6,7},{7,6},{8,9},{9,8},{10,11... | collective-permute-start | bytes 983048 | tf_op jit(solution)/shard_map/ppermute | solution.py:426
  96.0 8.6 %collective-permute-done.9 = bf16[320,512]{1,0:T(8,128)(2,1)S(1)} collective-permute-done((bf16[320,512]{1,0:T(8,128)(2,1)S(1)}, bf16[320,512]{1,0:T(8,128)(2,1)S(1)}, u32[]{:S(2)}, u32[]{:S(2)}) %collective-permute-start.9) | collective-permute-done | bytes 327712 | tf_op jit(solution)/shard_map/ppermute | solution.py:426
  104.6 0.0 copy-done.2
  104.6 0.0 copy-start.3
  104.6 0.1 convert_add_fusion
  104.8 2.4 %collective-permute-start.10 = (bf16[160,512]{1,0:T(8,128)(2,1)S(1)}, bf16[160,512]{1,0:T(8,128)(2,1)S(1)}, u32[]{:S(2)}, u32[]{:S(2)}) collective-permute-start(bf16[160,512]{1,0:T(8,128)(2,1)S(1)} %slice.36), channel_id=1, source_target_pairs={{0,2},{1,3},{2,0},{3,1},{4,6},{5,7},{6,4},{7,5},{8,10},{9,11},{10,... | collective-permute-start | bytes 491528 | tf_op jit(solution)/shard_map/ppermute | solution.py:426
  107.1 3.5 %all-to-all-done.1 = bf16[32,16,512]{2,1,0:T(8,128)(2,1)S(1)} async-done(((bf16[32,16,512]{2,1,0:T(8,128)(2,1)}), bf16[32,16,512]{2,1,0:T(8,128)(2,1)S(1)}, u32[]{:S(2)}, u32[]{:S(2)}) %all-to-all-start.1) | async-done | bytes 524320 | tf_op jit(solution)/shard_map/all_to_all | solution.py:389
  110.7 0.1 reduce_sum.21
  110.8 0.7 broadcast_in_dim.54
  111.4 3.4 %all-to-all-start.2 = ((bf16[8,16,512]{2,1,0:T(8,128)(2,1)}), bf16[8,16,512]{2,1,0:T(8,128)(2,1)S(1)}, u32[]{:S(2)}, u32[]{:S(2)}) async-start(bf16[8,16,512]{2,1,0:T(8,128)(2,1)} %broadcast_in_dim.54), calls=%async_computation.2 | async-start | bytes 262144 | tf_op jit(solution)/shard_map/all_to_all | solution.py:389
  114.8 1.0 collective-permute-done.10
  115.9 6.8 %collective-permute-start.11 = (bf16[80,512]{1,0:T(8,128)(2,1)S(1)}, bf16[80,512]{1,0:T(8,128)(2,1)S(1)}, u32[]{:S(2)}, u32[]{:S(2)}) collective-permute-start(bf16[80,512]{1,0:T(8,128)(2,1)S(1)} %slice.37), channel_id=1, source_target_pairs={{0,4},{1,5},{2,6},{3,7},{4,0},{5,1},{6,2},{7,3},{8,12},{9,13},{10,... | collective-permute-start | bytes 245768 | tf_op jit(solution)/shard_map/ppermute | solution.py:426
  122.6 1.1 all-to-all-done.2
  123.8 3.1 %collective-permute-done.11 = bf16[80,512]{1,0:T(8,128)(2,1)S(1)} collective-permute-done((bf16[80,512]{1,0:T(8,128)(2,1)S(1)}, bf16[80,512]{1,0:T(8,128)(2,1)S(1)}, u32[]{:S(2)}, u32[]{:S(2)}) %collective-permute-start.11) | collective-permute-done | bytes 81952 | tf_op jit(solution)/shard_map/ppermute | solution.py:426
  126.9 0.0 copy-done.3
  126.9 0.7 fusion.1
  (17 shorter events, 0.2 us)
Async XLA Ops:
  3.0 7.1 %copy-start.4 = (s32[1,1,1024]{2,1,0:T(1,128)S(1)}, s32[1,1,1024]{2,1,0:T(1,128)}, u32[]{:S(2)}) copy-start(s32[1,1,1024]{2,1,0:T(1,128)} %param.39) | copy-start | bytes 12292
  3.0 53.9 %all-to-all-start = ((bf16[8,224,512]{2,1,0:T(8,128)(2,1)}), bf16[8,224,512]{2,1,0:T(8,128)(2,1)}, u32[]{:S(2)}, u32[]{:S(2)}) async-start(bf16[8,224,512]{2,1,0:T(8,128)(2,1)} %pack.1), calls=%async_computation | async-start | bytes 3670016 | tf_op jit(solution)/shard_map/all_to_all | solution.py:389
  10.9 12.9 %collective-permute-start.1 = (bf16[24,512]{1,0:T(8,128)(2,1)S(1)}, bf16[24,512]{1,0:T(8,128)(2,1)S(1)}, u32[]{:S(2)}, u32[]{:S(2)}) collective-permute-start(bf16[24,512]{1,0:T(8,128)(2,1)S(1)} %get-tuple-element.33), channel_id=1, source_target_pairs={{0,64},{64,128},{128,192},{192,256},{256,320},{320,384},{384,448},... | collective-permute-start | bytes 73736 | tf_op jit(solution)/shard_map/ppermute | solution.py:366
  15.2 12.5 %collective-permute-start = (bf16[24,512]{1,0:T(8,128)(2,1)S(1)}, bf16[24,512]{1,0:T(8,128)(2,1)S(1)}, u32[]{:S(2)}, u32[]{:S(2)}) collective-permute-start(bf16[24,512]{1,0:T(8,128)(2,1)S(1)} %get-tuple-element.33), channel_id=1, source_target_pairs={{0,448},{64,0},{128,64},{192,128},{256,192},{320,256},{384,320},{4... | collective-permute-start | bytes 73736 | tf_op jit(solution)/shard_map/ppermute | solution.py:366
  23.8 14.9 %collective-permute-start.3 = (bf16[2,24,512]{2,1,0:T(8,128)(2,1)S(1)}, bf16[2,24,512]{2,1,0:T(8,128)(2,1)S(1)}, u32[]{:S(2)}, u32[]{:S(2)}) collective-permute-start(bf16[2,24,512]{2,1,0:T(8,128)(2,1)S(1)} %pad_maximum_fusion.2), channel_id=1, source_target_pairs={{0,320},{64,384},{128,448},{192,0},{256,64},{320,128},{384,192},{4... | collective-permute-start | bytes 147464 | tf_op jit(solution)/shard_map/ppermute | solution.py:366
  27.8 11.0 %collective-permute-start.2 = (bf16[3,24,512]{2,1,0:T(8,128)(2,1)S(1)}, bf16[3,24,512]{2,1,0:T(8,128)(2,1)S(1)}, u32[]{:S(2)}, u32[]{:S(2)}) collective-permute-start(bf16[3,24,512]{2,1,0:T(8,128)(2,1)S(1)} %pad_maximum_fusion.1), channel_id=1, source_target_pairs={{0,192},{64,256},{128,320},{192,384},{256,448},{320,0},{384,64},{4... | collective-permute-start | bytes 221192 | tf_op jit(solution)/shard_map/ppermute | solution.py:366
  38.7 12.2 %collective-permute-start.6 = (bf16[8,24,512]{2,1,0:T(8,128)(2,1)S(1)}, bf16[8,24,512]{2,1,0:T(8,128)(2,1)S(1)}, u32[]{:S(2)}, u32[]{:S(2)}) collective-permute-start(bf16[8,24,512]{2,1,0:T(8,128)(2,1)S(1)} %constant_dynamic-update-slice_fusion), channel_id=1, source_target_pairs={{0,48},{16,0},{32,16},{48,32},{1,49},{17,1},{33,17},{49,33},{2,50}... | collective-permute-start | bytes 589832 | tf_op jit(solution)/shard_map/ppermute | solution.py:366
  41.5 9.4 %collective-permute-start.5 = (bf16[8,24,512]{2,1,0:T(8,128)(2,1)S(1)}, bf16[8,24,512]{2,1,0:T(8,128)(2,1)S(1)}, u32[]{:S(2)}, u32[]{:S(2)}) collective-permute-start(bf16[8,24,512]{2,1,0:T(8,128)(2,1)S(1)} %constant_dynamic-update-slice_fusion), channel_id=1, source_target_pairs={{0,32},{16,48},{32,0},{48,16},{1,33},{17,49},{33,1},{49,17},{2,34}... | collective-permute-start | bytes 589832 | tf_op jit(solution)/shard_map/ppermute | solution.py:366
  44.5 7.9 %collective-permute-start.4 = (bf16[8,24,512]{2,1,0:T(8,128)(2,1)S(1)}, bf16[8,24,512]{2,1,0:T(8,128)(2,1)S(1)}, u32[]{:S(2)}, u32[]{:S(2)}) collective-permute-start(bf16[8,24,512]{2,1,0:T(8,128)(2,1)S(1)} %constant_dynamic-update-slice_fusion), channel_id=1, source_target_pairs={{0,16},{16,32},{32,48},{48,0},{1,17},{17,33},{33,49},{49,1},{2,18}... | collective-permute-start | bytes 589832 | tf_op jit(solution)/shard_map/ppermute | solution.py:366
  52.5 4.5 %copy-start.1 = (bf16[4,8,24,512]{3,2,1,0:T(8,128)(2,1)}, bf16[4,8,24,512]{3,2,1,0:T(8,128)(2,1)S(1)}, u32[]{:S(2)}) copy-start(bf16[4,8,24,512]{3,2,1,0:T(8,128)(2,1)S(1)} %pad_maximum_fusion.refs_2_) | copy-start | bytes 2359300
  52.5 6.5 %copy-start.6 = (s32[128]{0:T(128)S(1)}, s32[128]{0:T(128)}, u32[]{:S(2)}) copy-start(s32[128]{0:T(128)} %param.37) | copy-start | bytes 1540
  52.5 4.4 %collective-permute-start.7 = (bf16[4,8,24,512]{3,2,1,0:T(8,128)(2,1)S(1)}, bf16[4,8,24,512]{3,2,1,0:T(8,128)(2,1)}, u32[]{:S(2)}, u32[]{:S(2)}) collective-permute-start(bf16[4,8,24,512]{3,2,1,0:T(8,128)(2,1)S(1)} %pad_maximum_fusion.refs_2_), channel_id=1, source_target_pairs={{0,8},{8,0},{1,9},{9,1},{2,10},{10,2},{3,11},{11,3},{4,12},{12,4},... | collective-permute-start | bytes 2359304 | tf_op jit(solution)/shard_map/ppermute | solution.py:366
  57.0 6.0 %collective-permute-start.8 = (bf16[8,224,512]{2,1,0:T(8,128)(2,1)}, bf16[8,224,512]{2,1,0:T(8,128)(2,1)}, u32[]{:S(2)}, u32[]{:S(2)}) collective-permute-start(bf16[8,224,512]{2,1,0:T(8,128)(2,1)} %after.1.refs_0_), channel_id=1, source_target_pairs={{0,8},{8,0},{1,9},{9,1},{2,10},{10,2},{3,11},{11,3},{4,12},{12,4},... | collective-permute-start | bytes 5505032 | tf_op jit(solution)/shard_map/ppermute | solution.py:366
  76.3 4.0 %collective-permute-start.12 = (bf16[512,512]{1,0:T(8,128)(2,1)}, bf16[512,512]{1,0:T(8,128)(2,1)S(1)}, u32[]{:S(2)}, u32[]{:S(2)}) collective-permute-start(bf16[512,512]{1,0:T(8,128)(2,1)} %get-tuple-element.29), channel_id=1, source_target_pairs={{0,8},{8,0},{1,9},{9,1},{2,10},{10,2},{3,11},{11,3},{4,12},{12,4},... | collective-permute-start | bytes 1572872 | tf_op jit(solution)/shard_map/ppermute | solution.py:421
  78.4 1.0 copy-start
  79.4 14.1 %copy-start.5 = (bf16[320,512]{1,0:T(8,128)(2,1)S(1)}, bf16[320,512]{1,0:T(8,128)(2,1)}, u32[]{:S(2)}) copy-start(bf16[320,512]{1,0:T(8,128)(2,1)} %get-tuple-element.27) | copy-start | bytes 983044
  79.4 25.2 %copy-start.2 = (f32[320,512]{1,0:T(8,128)S(1)}, f32[320,512]{1,0:T(8,128)}, u32[]{:S(2)}) copy-start(f32[320,512]{1,0:T(8,128)} %get-tuple-element.26) | copy-start | bytes 1966084
  81.2 29.4 %all-to-all-start.1 = ((bf16[32,16,512]{2,1,0:T(8,128)(2,1)}), bf16[32,16,512]{2,1,0:T(8,128)(2,1)S(1)}, u32[]{:S(2)}, u32[]{:S(2)}) async-start(bf16[32,16,512]{2,1,0:T(8,128)(2,1)} %bitcast.24), calls=%async_computation.1 | async-start | bytes 1048576 | tf_op jit(solution)/shard_map/all_to_all | solution.py:389
  93.5 11.1 %collective-permute-start.9 = (bf16[320,512]{1,0:T(8,128)(2,1)S(1)}, bf16[320,512]{1,0:T(8,128)(2,1)S(1)}, u32[]{:S(2)}, u32[]{:S(2)}) collective-permute-start(bf16[320,512]{1,0:T(8,128)(2,1)S(1)} %copy-done.5), channel_id=1, source_target_pairs={{0,1},{1,0},{2,3},{3,2},{4,5},{5,4},{6,7},{7,6},{8,9},{9,8},{10,11... | collective-permute-start | bytes 983048 | tf_op jit(solution)/shard_map/ppermute | solution.py:426
  104.6 22.3 %copy-start.3 = (f32[80,512]{1,0:T(8,128)S(1)}, f32[80,512]{1,0:T(8,128)}, u32[]{:S(2)}) copy-start(f32[80,512]{1,0:T(8,128)} %get-tuple-element.25) | copy-start | bytes 491524
  104.8 11.1 %collective-permute-start.10 = (bf16[160,512]{1,0:T(8,128)(2,1)S(1)}, bf16[160,512]{1,0:T(8,128)(2,1)S(1)}, u32[]{:S(2)}, u32[]{:S(2)}) collective-permute-start(bf16[160,512]{1,0:T(8,128)(2,1)S(1)} %slice.36), channel_id=1, source_target_pairs={{0,2},{1,3},{2,0},{3,1},{4,6},{5,7},{6,4},{7,5},{8,10},{9,11},{10,... | collective-permute-start | bytes 491528 | tf_op jit(solution)/shard_map/ppermute | solution.py:426
  111.4 12.4 %all-to-all-start.2 = ((bf16[8,16,512]{2,1,0:T(8,128)(2,1)}), bf16[8,16,512]{2,1,0:T(8,128)(2,1)S(1)}, u32[]{:S(2)}, u32[]{:S(2)}) async-start(bf16[8,16,512]{2,1,0:T(8,128)(2,1)} %broadcast_in_dim.54), calls=%async_computation.2 | async-start | bytes 262144 | tf_op jit(solution)/shard_map/all_to_all | solution.py:389
  115.9 11.0 %collective-permute-start.11 = (bf16[80,512]{1,0:T(8,128)(2,1)S(1)}, bf16[80,512]{1,0:T(8,128)(2,1)S(1)}, u32[]{:S(2)}, u32[]{:S(2)}) collective-permute-start(bf16[80,512]{1,0:T(8,128)(2,1)S(1)} %slice.37), channel_id=1, source_target_pairs={{0,4},{1,5},{2,6},{3,7},{4,0},{5,1},{6,2},{7,3},{8,12},{9,13},{10,... | collective-permute-start | bytes 245768 | tf_op jit(solution)/shard_map/ppermute | solution.py:426
